TPU v7x, 32 devices: a whole 2x2x4 slice. The times are simulated.
32 devices in a mesh: uly: 2 (over y), blk: 16 (over z, x, core).
Axes of the slice: x: 2, y: 2, z: 4, core: 2. Of those that a mesh axis runs over, the one named last changes fastest.
Arguments:
- query: bfloat16 [8192, 1024], P(('uly', 'blk')), as said below
- key: bfloat16 [8192, 1024], P(('uly', 'blk')), as said below
- value: bfloat16 [8192, 1024], P(('uly', 'blk')), may hold values from -5 to 5
- live: int32 [8, 4, 16, 27], P('uly', None, 'blk'), may hold values from 0 to 1, as said below
Outputs:
- attended: bfloat16 [8192, 1024], P(('uly', 'blk'))
Inputs may be any that keep to these rules, and one draw needn't show every extreme that they name: `query`: entries lie within -5 to 5. `key`: entries lie within -5 to 5. live[h, f, s, 13] = 1 always; live is 0 for every neighbour that lies outside the grid of 4 x 2 x 8 tiles.
All inputs are finite; a program needn't handle non-finite values.
Results may differ from a plain program's by a relative error of at most 0.0046.
Values may be sent and summed in bfloat16 or wider, within the bound.
No kernel may reach another device: no remote copies, remote signals or barrier semaphores. Data moves between devices by JAX's collectives and lax.ppermute only.
A program may use at most 128 MiB of HBM per device.

v0:
```python
import jax
import jax.numpy as jnp
from jax import lax
from jax.sharding import PartitionSpec as P

HD = 128
HEADS = 8
TILE = 128
TW = 8


def shifted(block, axis, distance):
    devices = range(lax.axis_size(axis))
    route = [(i - distance, i) for i in devices if i - distance in devices]
    return lax.ppermute(block, axis, route)


def local(query, key, value, live):
    uly_count = lax.axis_size("uly")
    tok_rows = query.shape[0]
    local_heads = HEADS // uly_count
    frames = uly_count * tok_rows // TILE
    scale = HD ** (-0.5)
    query_in, key_in, value_in = (
        lax.all_to_all(
            query.reshape(tok_rows, HEADS, HD), "uly", split_axis=1, concat_axis=0, tiled=True
        ),
        lax.all_to_all(
            key.reshape(tok_rows, HEADS, HD), "uly", split_axis=1, concat_axis=0, tiled=True
        ),
        lax.all_to_all(
            value.reshape(tok_rows, HEADS, HD), "uly", split_axis=1, concat_axis=0, tiled=True
        ),
    )
    query_tiles = query_in.reshape(frames, TILE, local_heads, HD)
    paired = jnp.stack(
        [
            key_in.reshape(frames, TILE, local_heads, HD),
            value_in.reshape(frames, TILE, local_heads, HD),
        ],
        axis=1,
    )
    pieces = []
    for row_step in (-1, 0, 1):
        for col_step in (-1, 0, 1):
            if row_step == 0 and col_step == 0:
                pieces.append(paired)
            else:
                pieces.append(shifted(paired, "blk", -(row_step * TW + col_step)))
    near = jnp.stack(pieces, axis=1).reshape((frames, 3, 3) + paired.shape[1:])
    padded = jnp.pad(near, ((1, 1),) + ((0, 0),) * (near.ndim - 1))
    allowed_all = live.reshape(local_heads, frames, 27)

    def one_frame(frame):
        block = lax.dynamic_slice_in_dim(padded, frame, 3, 0)
        keys_block = block[:, :, :, 0].reshape(27 * TILE, local_heads, HD)
        values_block = block[:, :, :, 1].reshape(27 * TILE, local_heads, HD)
        query_tile = lax.dynamic_index_in_dim(query_tiles, frame, 0, keepdims=False)
        scores = (
            jnp.einsum("qhd,khd->hqk", query_tile, keys_block, preferred_element_type=jnp.float32)
            * scale
        )
        allowed = lax.dynamic_index_in_dim(allowed_all, frame, 1, keepdims=False)
        allowed = jnp.repeat(allowed > 0, TILE, axis=1)[:, None, :]
        masked = jnp.where(allowed, scores, -1e30)
        top = jnp.max(masked, axis=2, keepdims=True)
        weights = jnp.where(allowed, jnp.exp(masked - top), 0.0)
        total = jnp.sum(weights, axis=2)
        mixed = jnp.einsum(
            "hqk,khd->qhd",
            weights.astype(jnp.bfloat16),
            values_block,
            preferred_element_type=jnp.float32,
        )
        return (mixed / jnp.transpose(total)[:, :, None]).astype(jnp.bfloat16)

    outputs = lax.map(one_frame, jnp.arange(frames))
    returned = lax.all_to_all(
        outputs.reshape(uly_count * tok_rows, local_heads, HD),
        "uly",
        split_axis=0,
        concat_axis=1,
        tiled=True,
    )
    return returned.reshape(tok_rows, HEADS * HD)


def solution(mesh):
    return jax.shard_map(
        local,
        mesh=mesh,
        in_specs=(
            P(("uly", "blk"), None),
            P(("uly", "blk"), None),
            P(("uly", "blk"), None),
            P("uly", None, "blk", None),
        ),
        out_specs=P(("uly", "blk"), None),
        check_vma=False,
    )
```

profile of v0, /device:TPU:2, one launch (start us, length us, event | category | flops | bytes accessed | tf_op | source)
XLA Modules:
  0.0 337.9 jit_solution(2974738752062058999)
XLA Ops:
  0.0 1.3 copy.103
  1.3 1.0 copy.104
  2.3 3.5 %all-to-all-start = ((bf16[256,8,128]{2,0,1:T(8,128)(2,1)}), bf16[256,8,128]{2,0,1:T(8,128)(2,1)S(1)}, u32[]{:S(2)}, u32[]{:S(2)}) async-start(bf16[256,8,128]{2,0,1:T(8,128)(2,1)} %copy.104), calls=%async_computation | async-start | bytes 1048576 | tf_op jit(solution)/shard_map/all_to_all | solution.py:28
  5.8 1.2 copy.106
  7.1 1.0 copy.107
  8.1 6.0 %all-to-all-done = bf16[256,8,128]{2,0,1:T(8,128)(2,1)S(1)} async-done(((bf16[256,8,128]{2,0,1:T(8,128)(2,1)}), bf16[256,8,128]{2,0,1:T(8,128)(2,1)S(1)}, u32[]{:S(2)}, u32[]{:S(2)}) %all-to-all-start) | async-done | bytes 524320 | tf_op jit(solution)/shard_map/all_to_all | solution.py:28
  14.0 3.5 %all-to-all-start.1 = ((bf16[256,8,128]{2,0,1:T(8,128)(2,1)}), bf16[256,8,128]{2,0,1:T(8,128)(2,1)S(1)}, u32[]{:S(2)}, u32[]{:S(2)}) async-start(bf16[256,8,128]{2,0,1:T(8,128)(2,1)} %copy.107), calls=%async_computation.1 | async-start | bytes 1048576 | tf_op jit(solution)/shard_map/all_to_all | solution.py:31
  17.6 7.3 %all-to-all-done.1 = bf16[256,8,128]{2,0,1:T(8,128)(2,1)S(1)} async-done(((bf16[256,8,128]{2,0,1:T(8,128)(2,1)}), bf16[256,8,128]{2,0,1:T(8,128)(2,1)S(1)}, u32[]{:S(2)}, u32[]{:S(2)}) %all-to-all-start.1) | async-done | bytes 524320 | tf_op jit(solution)/shard_map/all_to_all | solution.py:31
  25.0 3.1 collective-permute-start
  28.2 3.7 %collective-permute-start.1 = (bf16[4,2,128,4,128]{4,2,0,3,1:T(8,128)(2,1)S(1)}, bf16[4,2,128,4,128]{4,2,0,3,1:T(8,128)(2,1)}, u32[]{:S(2)}, u32[]{:S(2)}) collective-permute-start(bf16[4,2,128,4,128]{4,2,0,3,1:T(8,128)(2,1)S(1)} %pad_maximum_fusion), channel_id=1, source_target_pairs={{0,8},{1,9},{2,10},{3,11},{4,12},{5,13},{6,14},{7,15},{16,24},{17,... | collective-permute-start | bytes 3145736 | tf_op jit(solution)/shard_map/ppermute | solution.py:15
  31.9 2.3 collective-permute-start.2
  34.2 1.0 copy.111
  35.2 3.5 %all-to-all-start.2 = ((bf16[256,8,128]{0,2,1:T(8,128)(2,1)}), bf16[256,8,128]{0,2,1:T(8,128)(2,1)S(1)}, u32[]{:S(2)}, u32[]{:S(2)}) async-start(bf16[256,8,128]{0,2,1:T(8,128)(2,1)} %bitcast.27), calls=%async_computation.2 | async-start | bytes 1048576 | tf_op jit(solution)/shard_map/all_to_all | solution.py:25
  38.7 4.0 %collective-permute-start.3 = (bf16[4,2,128,4,128]{4,2,0,3,1:T(8,128)(2,1)S(1)}, bf16[4,2,128,4,128]{4,2,0,3,1:T(8,128)(2,1)}, u32[]{:S(2)}, u32[]{:S(2)}) collective-permute-start(bf16[4,2,128,4,128]{4,2,0,3,1:T(8,128)(2,1)S(1)} %pad_maximum_fusion), channel_id=1, source_target_pairs={{0,1},{1,2},{2,3},{3,4},{4,5},{5,6},{6,7},{7,8},{8,9},{9,10},{10,1... | collective-permute-start | bytes 3145736 | tf_op jit(solution)/shard_map/ppermute | solution.py:15
  42.7 2.0 collective-permute-start.4
  44.7 2.3 all-to-all-done.2
  47.0 1.0 copy.113
  48.0 1.3 collective-permute-start.5
  49.3 2.3 bitcast_dynamic-update-slice_fusion.8
  51.6 18.9 %collective-permute-done.1 = bf16[4,2,128,4,128]{4,2,0,3,1:T(8,128)(2,1)} collective-permute-done((bf16[4,2,128,4,128]{4,2,0,3,1:T(8,128)(2,1)S(1)}, bf16[4,2,128,4,128]{4,2,0,3,1:T(8,128)(2,1)}, u32[]{:S(2)}, u32[]{:S(2)}) %collective-permute-start.1) | collective-permute-done | bytes 1048608 | tf_op jit(solution)/shard_map/ppermute | solution.py:15
  70.5 1.3 collective-permute-start.6
  71.7 2.3 bitcast_dynamic-update-slice_fusion.7
  74.1 18.9 %collective-permute-done.2 = bf16[4,2,128,4,128]{4,2,0,3,1:T(8,128)(2,1)} collective-permute-done((bf16[4,2,128,4,128]{4,2,0,3,1:T(8,128)(2,1)S(1)}, bf16[4,2,128,4,128]{4,2,0,3,1:T(8,128)(2,1)}, u32[]{:S(2)}, u32[]{:S(2)}) %collective-permute-start.2) | collective-permute-done | bytes 1048608 | tf_op jit(solution)/shard_map/ppermute | solution.py:15
  92.9 1.5 collective-permute-start.7
  94.4 2.3 bitcast_dynamic-update-slice_fusion.6
  96.7 2.3 bitcast_dynamic-update-slice_fusion.5
  99.0 1.0 bitcast_dynamic-update-slice_fusion.4
  100.1 2.3 bitcast_dynamic-update-slice_fusion.3
  102.4 1.1 bitcast_dynamic-update-slice_fusion.2
  103.5 1.1 bitcast_dynamic-update-slice_fusion.1
  104.6 98.6 %collective-permute-done.7 = bf16[4,2,128,4,128]{4,2,0,3,1:T(8,128)(2,1)S(1)} collective-permute-done((bf16[4,2,128,4,128]{4,2,0,3,1:T(8,128)(2,1)S(1)}, bf16[4,2,128,4,128]{4,2,0,3,1:T(8,128)(2,1)S(1)}, u32[]{:S(2)}, u32[]{:S(2)}) %collective-permute-start.7) | collective-permute-done | bytes 1048608 | tf_op jit(solution)/shard_map/ppermute | solution.py:15
  203.2 1.1 bitcast_dynamic-update-slice_fusion
  204.3 11.6 %copy.109 = bf16[4,3,3,2,128,4,128]{6,4,2,1,0,5,3:T(8,128)(2,1)} copy(bf16[4,3,3,2,128,4,128]{6,4,0,5,3,2,1:T(8,128)(2,1)} %bitcast.25) | data formatting | bytes 18874368 | tf_op jit(solution)/shard_map/reshape | solution.py:50
  215.9 11.0 %pad.4 = bf16[6,3,3,2,128,4,128]{6,4,2,1,0,5,3:T(8,128)(2,1)} pad(bf16[4,3,3,2,128,4,128]{6,4,2,1,0,5,3:T(8,128)(2,1)} %copy.109, bf16[]{:T(256)} %constant.32.clone.1), padding=1_1x0_0x0_0x0_0x0_0x0_0x0_0 | pad | bytes 23592962 | tf_op jit(solution)/shard_map/jit(_pad)/pad | solution.py:51
  226.9 0.6 iota.3
  227.5 98.7 %while.10 = (s32[]{:T(128)}, bf16[4,128,4,128]{3,1,0,2:T(8,128)(2,1)}, s32[4]{0:T(128)}, bf16[6,3,3,2,128,4,128]{6,4,2,1,0,5,3:T(8,128)(2,1)}, s32[4,4,27]{2,0,1...) while((s32[]{:T(128)}, ...), condition=%wide.region_3.4_spmd, body=%wide.region_0.3_spmd.sunk | while | flops 916721152 | bytes 29186448 | solution.py:77
  227.5 1.3 dynamic_slice.34
  230.6 7.2 %constant_dynamic-slice_fusion.3 = (bf16[3,3,3,1,128,4,128]{6,4,2,1,0,5,3:T(8,128)(2,1)}, bf16[3,3,3,1,128,4,128]{6,4,2,1,0,5,3:T(8,128)(2,1)S(1)}) fusion(bf16[6,3,3,2,128,4,128]{6,4,2,1,0,5,3:T(8,128)(2,1)} %get-tuple-element.162, s32[]{:T(128)S(6)} %select_n.28, s32[]{:T(128)S(6)} %add.21), kind=kLoop, calls=%fused_computation.23.clone.1 | loop fusion | bytes 14155784 | tf_op jit(solution)/shard_map/while/body/eval_jaxpr/slice | solution.py:56
  239.2 7.2 %fusion.49 = (f32[4,128]{1,0:T(4,128)}, bf16[4,128,3456]{2,1,0:T(8,128)(2,1)}) fusion(bf16[3456,4,128]{2,0,1:T(8,128)(2,1)} %bitcast.105, pred[4,3456]{1,0:T(4,128)(4,1)S(1)} %bitcast.119, bf16[4,128,4,128]{3,1,0,2:T(8,128)(2,1)} %get-tuple-element.164, s32[]{:T(128)S(6)} %select_n.29), kind=kOutput, calls=%fused_computation.37.clone.1 | convolution fusion | flops 463605120 | bytes 7238660 | tf_op jit(solution)/shard_map/while/body/eval_jaxpr/sub | solution.py:67
  246.4 4.0 %fusion.50 = bf16[1,128,4,128]{1,3,2,0:T(8,128)(2,1)} fusion(bf16[3456,4,128]{2,0,1:T(8,128)(2,1)S(1)} %bitcast.104, bf16[4,128,3456]{2,1,0:T(8,128)(2,1)} %get-tuple-element.135, f32[128,4]{0,1:T(4,128)} %bitcast.120), kind=kOutput, calls=%fused_computation.9.clone.1 | convolution fusion | flops 453115904 | bytes 7211008 | tf_op jit(solution)/shard_map/while/body/eval_jaxpr/hqk,khd->qhd/dot_general | solution.py:69
  250.4 1.0 copy.134
  251.4 0.7 constant_dynamic-update-slice_fusion.2
  252.1 1.3 dynamic_slice.34
  255.3 7.2 %constant_dynamic-slice_fusion.3 = (bf16[3,3,3,1,128,4,128]{6,4,2,1,0,5,3:T(8,128)(2,1)}, bf16[3,3,3,1,128,4,128]{6,4,2,1,0,5,3:T(8,128)(2,1)S(1)}) fusion(bf16[6,3,3,2,128,4,128]{6,4,2,1,0,5,3:T(8,128)(2,1)} %get-tuple-element.162, s32[]{:T(128)S(6)} %select_n.28, s32[]{:T(128)S(6)} %add.21), kind=kLoop, calls=%fused_computation.23.clone.1 | loop fusion | bytes 14155784 | tf_op jit(solution)/shard_map/while/body/eval_jaxpr/slice | solution.py:56
  263.9 7.2 %fusion.49 = (f32[4,128]{1,0:T(4,128)}, bf16[4,128,3456]{2,1,0:T(8,128)(2,1)}) fusion(bf16[3456,4,128]{2,0,1:T(8,128)(2,1)} %bitcast.105, pred[4,3456]{1,0:T(4,128)(4,1)S(1)} %bitcast.119, bf16[4,128,4,128]{3,1,0,2:T(8,128)(2,1)} %get-tuple-element.164, s32[]{:T(128)S(6)} %select_n.29), kind=kOutput, calls=%fused_computation.37.clone.1 | convolution fusion | flops 463605120 | bytes 7238660 | tf_op jit(solution)/shard_map/while/body/eval_jaxpr/sub | solution.py:67
  271.1 4.0 %fusion.50 = bf16[1,128,4,128]{1,3,2,0:T(8,128)(2,1)} fusion(bf16[3456,4,128]{2,0,1:T(8,128)(2,1)S(1)} %bitcast.104, bf16[4,128,3456]{2,1,0:T(8,128)(2,1)} %get-tuple-element.135, f32[128,4]{0,1:T(4,128)} %bitcast.120), kind=kOutput, calls=%fused_computation.9.clone.1 | convolution fusion | flops 453115904 | bytes 7211008 | tf_op jit(solution)/shard_map/while/body/eval_jaxpr/hqk,khd->qhd/dot_general | solution.py:69
  275.1 1.0 copy.134
  276.1 0.7 constant_dynamic-update-slice_fusion.2
  276.8 1.3 dynamic_slice.34
  280.0 7.2 %constant_dynamic-slice_fusion.3 = (bf16[3,3,3,1,128,4,128]{6,4,2,1,0,5,3:T(8,128)(2,1)}, bf16[3,3,3,1,128,4,128]{6,4,2,1,0,5,3:T(8,128)(2,1)S(1)}) fusion(bf16[6,3,3,2,128,4,128]{6,4,2,1,0,5,3:T(8,128)(2,1)} %get-tuple-element.162, s32[]{:T(128)S(6)} %select_n.28, s32[]{:T(128)S(6)} %add.21), kind=kLoop, calls=%fused_computation.23.clone.1 | loop fusion | bytes 14155784 | tf_op jit(solution)/shard_map/while/body/eval_jaxpr/slice | solution.py:56
  288.5 7.2 %fusion.49 = (f32[4,128]{1,0:T(4,128)}, bf16[4,128,3456]{2,1,0:T(8,128)(2,1)}) fusion(bf16[3456,4,128]{2,0,1:T(8,128)(2,1)} %bitcast.105, pred[4,3456]{1,0:T(4,128)(4,1)S(1)} %bitcast.119, bf16[4,128,4,128]{3,1,0,2:T(8,128)(2,1)} %get-tuple-element.164, s32[]{:T(128)S(6)} %select_n.29), kind=kOutput, calls=%fused_computation.37.clone.1 | convolution fusion | flops 463605120 | bytes 7238660 | tf_op jit(solution)/shard_map/while/body/eval_jaxpr/sub | solution.py:67
  295.7 4.0 %fusion.50 = bf16[1,128,4,128]{1,3,2,0:T(8,128)(2,1)} fusion(bf16[3456,4,128]{2,0,1:T(8,128)(2,1)S(1)} %bitcast.104, bf16[4,128,3456]{2,1,0:T(8,128)(2,1)} %get-tuple-element.135, f32[128,4]{0,1:T(4,128)} %bitcast.120), kind=kOutput, calls=%fused_computation.9.clone.1 | convolution fusion | flops 453115904 | bytes 7211008 | tf_op jit(solution)/shard_map/while/body/eval_jaxpr/hqk,khd->qhd/dot_general | solution.py:69
  299.7 1.0 copy.134
  300.8 0.7 constant_dynamic-update-slice_fusion.2
  301.5 1.3 dynamic_slice.34
  304.6 7.2 %constant_dynamic-slice_fusion.3 = (bf16[3,3,3,1,128,4,128]{6,4,2,1,0,5,3:T(8,128)(2,1)}, bf16[3,3,3,1,128,4,128]{6,4,2,1,0,5,3:T(8,128)(2,1)S(1)}) fusion(bf16[6,3,3,2,128,4,128]{6,4,2,1,0,5,3:T(8,128)(2,1)} %get-tuple-element.162, s32[]{:T(128)S(6)} %select_n.28, s32[]{:T(128)S(6)} %add.21), kind=kLoop, calls=%fused_computation.23.clone.1 | loop fusion | bytes 14155784 | tf_op jit(solution)/shard_map/while/body/eval_jaxpr/slice | solution.py:56
  313.2 7.2 %fusion.49 = (f32[4,128]{1,0:T(4,128)}, bf16[4,128,3456]{2,1,0:T(8,128)(2,1)}) fusion(bf16[3456,4,128]{2,0,1:T(8,128)(2,1)} %bitcast.105, pred[4,3456]{1,0:T(4,128)(4,1)S(1)} %bitcast.119, bf16[4,128,4,128]{3,1,0,2:T(8,128)(2,1)} %get-tuple-element.164, s32[]{:T(128)S(6)} %select_n.29), kind=kOutput, calls=%fused_computation.37.clone.1 | convolution fusion | flops 463605120 | bytes 7238660 | tf_op jit(solution)/shard_map/while/body/eval_jaxpr/sub | solution.py:67
  320.4 4.0 %fusion.50 = bf16[1,128,4,128]{1,3,2,0:T(8,128)(2,1)} fusion(bf16[3456,4,128]{2,0,1:T(8,128)(2,1)S(1)} %bitcast.104, bf16[4,128,3456]{2,1,0:T(8,128)(2,1)} %get-tuple-element.135, f32[128,4]{0,1:T(4,128)} %bitcast.120), kind=kOutput, calls=%fused_computation.9.clone.1 | convolution fusion | flops 453115904 | bytes 7211008 | tf_op jit(solution)/shard_map/while/body/eval_jaxpr/hqk,khd->qhd/dot_general | solution.py:69
  324.4 1.0 copy.134
  325.4 0.7 constant_dynamic-update-slice_fusion.2
  326.1 1.4 copy.116
  327.6 9.0 %all_to_all.60 = bf16[512,4,128]{2,1,0:T(4,128)(2,1)S(1)} all-to-all(bf16[512,4,128]{2,1,0:T(4,128)(2,1)S(1)} %copy.116), channel_id=1, replica_groups=mesh['uly'=2,'blk'=16] {'uly'}, dimensions={0} | all-to-all | bytes 1048576 | tf_op jit(solution)/shard_map/all_to_all | solution.py:78
  336.6 0.2 copy.118
  336.9 1.0 copy.119
  (43 shorter events, 0.8 us)
Async XLA Ops:
  0.0 34.2 %copy-start = (bf16[256,1024]{1,0:T(8,128)(2,1)S(1)}, bf16[256,1024]{1,0:T(8,128)(2,1)}, u32[]{:S(2)}) copy-start(bf16[256,1024]{1,0:T(8,128)(2,1)} %param.6) | copy-start | bytes 1572868
  0.0 42.7 %copy-start.3 = (s32[4,4,1,27]{3,2,1,0:T(1,128)S(1)}, s32[4,4,1,27]{3,2,1,0:T(1,128)}, u32[]{:S(2)}) copy-start(s32[4,4,1,27]{3,2,1,0:T(1,128)} %param.9) | copy-start | bytes 5188
  2.3 11.7 %all-to-all-start = ((bf16[256,8,128]{2,0,1:T(8,128)(2,1)}), bf16[256,8,128]{2,0,1:T(8,128)(2,1)S(1)}, u32[]{:S(2)}, u32[]{:S(2)}) async-start(bf16[256,8,128]{2,0,1:T(8,128)(2,1)} %copy.104), calls=%async_computation | async-start | bytes 1048576 | tf_op jit(solution)/shard_map/all_to_all | solution.py:28
  14.0 10.9 %all-to-all-start.1 = ((bf16[256,8,128]{2,0,1:T(8,128)(2,1)}), bf16[256,8,128]{2,0,1:T(8,128)(2,1)S(1)}, u32[]{:S(2)}, u32[]{:S(2)}) async-start(bf16[256,8,128]{2,0,1:T(8,128)(2,1)} %copy.107), calls=%async_computation.1 | async-start | bytes 1048576 | tf_op jit(solution)/shard_map/all_to_all | solution.py:31
  25.0 22.9 %collective-permute-start = (bf16[4,2,128,4,128]{4,2,0,3,1:T(8,128)(2,1)S(1)}, bf16[4,2,128,4,128]{4,2,0,3,1:T(8,128)(2,1)}, u32[]{:S(2)}, u32[]{:S(2)}) collective-permute-start(bf16[4,2,128,4,128]{4,2,0,3,1:T(8,128)(2,1)S(1)} %pad_maximum_fusion), channel_id=1, source_target_pairs={{0,9},{1,10},{2,11},{3,12},{4,13},{5,14},{6,15},{16,25},{17,26},{1... | collective-permute-start | bytes 3145736 | tf_op jit(solution)/shard_map/ppermute | solution.py:15
  28.2 42.3 %collective-permute-start.1 = (bf16[4,2,128,4,128]{4,2,0,3,1:T(8,128)(2,1)S(1)}, bf16[4,2,128,4,128]{4,2,0,3,1:T(8,128)(2,1)}, u32[]{:S(2)}, u32[]{:S(2)}) collective-permute-start(bf16[4,2,128,4,128]{4,2,0,3,1:T(8,128)(2,1)S(1)} %pad_maximum_fusion), channel_id=1, source_target_pairs={{0,8},{1,9},{2,10},{3,11},{4,12},{5,13},{6,14},{7,15},{16,24},{17,... | collective-permute-start | bytes 3145736 | tf_op jit(solution)/shard_map/ppermute | solution.py:15
  31.9 61.0 %collective-permute-start.2 = (bf16[4,2,128,4,128]{4,2,0,3,1:T(8,128)(2,1)S(1)}, bf16[4,2,128,4,128]{4,2,0,3,1:T(8,128)(2,1)}, u32[]{:S(2)}, u32[]{:S(2)}) collective-permute-start(bf16[4,2,128,4,128]{4,2,0,3,1:T(8,128)(2,1)S(1)} %pad_maximum_fusion), channel_id=1, source_target_pairs={{0,7},{1,8},{2,9},{3,10},{4,11},{5,12},{6,13},{7,14},{8,15},{16,23... | collective-permute-start | bytes 3145736 | tf_op jit(solution)/shard_map/ppermute | solution.py:15
  35.2 11.8 %all-to-all-start.2 = ((bf16[256,8,128]{0,2,1:T(8,128)(2,1)}), bf16[256,8,128]{0,2,1:T(8,128)(2,1)S(1)}, u32[]{:S(2)}, u32[]{:S(2)}) async-start(bf16[256,8,128]{0,2,1:T(8,128)(2,1)} %bitcast.27), calls=%async_computation.2 | async-start | bytes 1048576 | tf_op jit(solution)/shard_map/all_to_all | solution.py:25
  38.7 58.0 %collective-permute-start.3 = (bf16[4,2,128,4,128]{4,2,0,3,1:T(8,128)(2,1)S(1)}, bf16[4,2,128,4,128]{4,2,0,3,1:T(8,128)(2,1)}, u32[]{:S(2)}, u32[]{:S(2)}) collective-permute-start(bf16[4,2,128,4,128]{4,2,0,3,1:T(8,128)(2,1)S(1)} %pad_maximum_fusion), channel_id=1, source_target_pairs={{0,1},{1,2},{2,3},{3,4},{4,5},{5,6},{6,7},{7,8},{8,9},{9,10},{10,1... | collective-permute-start | bytes 3145736 | tf_op jit(solution)/shard_map/ppermute | solution.py:15
  42.7 57.4 %collective-permute-start.4 = (bf16[4,2,128,4,128]{4,2,0,3,1:T(8,128)(2,1)S(1)}, bf16[4,2,128,4,128]{4,2,0,3,1:T(8,128)(2,1)}, u32[]{:S(2)}, u32[]{:S(2)}) collective-permute-start(bf16[4,2,128,4,128]{4,2,0,3,1:T(8,128)(2,1)S(1)} %pad_maximum_fusion), channel_id=1, source_target_pairs={{1,0},{2,1},{3,2},{4,3},{5,4},{6,5},{7,6},{8,7},{9,8},{10,9},{11,1... | collective-permute-start | bytes 3145736 | tf_op jit(solution)/shard_map/ppermute | solution.py:15
  48.0 54.5 %collective-permute-start.5 = (bf16[4,2,128,4,128]{4,2,0,3,1:T(8,128)(2,1)S(1)}, bf16[4,2,128,4,128]{4,2,0,3,1:T(8,128)(2,1)S(1)}, u32[]{:S(2)}, u32[]{:S(2)}) collective-permute-start(bf16[4,2,128,4,128]{4,2,0,3,1:T(8,128)(2,1)S(1)} %pad_maximum_fusion), channel_id=1, source_target_pairs={{7,0},{8,1},{9,2},{10,3},{11,4},{12,5},{13,6},{14,7},{15,8},{23,16... | collective-permute-start | bytes 3145736 | tf_op jit(solution)/shard_map/ppermute | solution.py:15
  70.5 33.1 %collective-permute-start.6 = (bf16[4,2,128,4,128]{4,2,0,3,1:T(8,128)(2,1)S(1)}, bf16[4,2,128,4,128]{4,2,0,3,1:T(8,128)(2,1)S(1)}, u32[]{:S(2)}, u32[]{:S(2)}) collective-permute-start(bf16[4,2,128,4,128]{4,2,0,3,1:T(8,128)(2,1)S(1)} %pad_maximum_fusion), channel_id=1, source_target_pairs={{8,0},{9,1},{10,2},{11,3},{12,4},{13,5},{14,6},{15,7},{24,16},{25,... | collective-permute-start | bytes 3145736 | tf_op jit(solution)/shard_map/ppermute | solution.py:15
  92.9 110.3 %collective-permute-start.7 = (bf16[4,2,128,4,128]{4,2,0,3,1:T(8,128)(2,1)S(1)}, bf16[4,2,128,4,128]{4,2,0,3,1:T(8,128)(2,1)S(1)}, u32[]{:S(2)}, u32[]{:S(2)}) collective-permute-start(bf16[4,2,128,4,128]{4,2,0,3,1:T(8,128)(2,1)S(1)} %pad_maximum_fusion), channel_id=1, source_target_pairs={{9,0},{10,1},{11,2},{12,3},{13,4},{14,5},{15,6},{25,16},{26,17},{2... | collective-permute-start | bytes 3145736 | tf_op jit(solution)/shard_map/ppermute | solution.py:15
  227.5 11.6 %copy-start.1 = (s32[4,4,27]{2,0,1:T(4,128)}, s32[4,4,27]{2,0,1:T(4,128)S(1)}, u32[]{:S(2)}) copy-start(s32[4,4,27]{2,0,1:T(4,128)S(1)} %get-tuple-element.163) | copy-start | bytes 5188 | tf_op jit(solution)/shard_map/while
  246.4 5.7 %copy-start.2 = (s32[4,4,27]{2,0,1:T(4,128)S(1)}, s32[4,4,27]{2,0,1:T(4,128)}, u32[]{:S(2)}) copy-start(s32[4,4,27]{2,0,1:T(4,128)} %copy-done.1) | copy-start | bytes 5188 | tf_op jit(solution)/shard_map/while
  252.1 11.6 %copy-start.1 = (s32[4,4,27]{2,0,1:T(4,128)}, s32[4,4,27]{2,0,1:T(4,128)S(1)}, u32[]{:S(2)}) copy-start(s32[4,4,27]{2,0,1:T(4,128)S(1)} %get-tuple-element.163) | copy-start | bytes 5188 | tf_op jit(solution)/shard_map/while
  271.1 5.7 %copy-start.2 = (s32[4,4,27]{2,0,1:T(4,128)S(1)}, s32[4,4,27]{2,0,1:T(4,128)}, u32[]{:S(2)}) copy-start(s32[4,4,27]{2,0,1:T(4,128)} %copy-done.1) | copy-start | bytes 5188 | tf_op jit(solution)/shard_map/while
  276.8 11.6 %copy-start.1 = (s32[4,4,27]{2,0,1:T(4,128)}, s32[4,4,27]{2,0,1:T(4,128)S(1)}, u32[]{:S(2)}) copy-start(s32[4,4,27]{2,0,1:T(4,128)S(1)} %get-tuple-element.163) | copy-start | bytes 5188 | tf_op jit(solution)/shard_map/while
  295.7 5.7 %copy-start.2 = (s32[4,4,27]{2,0,1:T(4,128)S(1)}, s32[4,4,27]{2,0,1:T(4,128)}, u32[]{:S(2)}) copy-start(s32[4,4,27]{2,0,1:T(4,128)} %copy-done.1) | copy-start | bytes 5188 | tf_op jit(solution)/shard_map/while
  301.5 11.6 %copy-start.1 = (s32[4,4,27]{2,0,1:T(4,128)}, s32[4,4,27]{2,0,1:T(4,128)S(1)}, u32[]{:S(2)}) copy-start(s32[4,4,27]{2,0,1:T(4,128)S(1)} %get-tuple-element.163) | copy-start | bytes 5188 | tf_op jit(solution)/shard_map/while
  320.4 5.7 %copy-start.2 = (s32[4,4,27]{2,0,1:T(4,128)S(1)}, s32[4,4,27]{2,0,1:T(4,128)}, u32[]{:S(2)}) copy-start(s32[4,4,27]{2,0,1:T(4,128)} %copy-done.1) | copy-start | bytes 5188 | tf_op jit(solution)/shard_map/while
where the time goes:
time: 339 us; the launch traced here: 338 us
  waiting for transfers between devices  152 us (45%)
  local copies, waits for them, and re-layouts  88.5 us (26%)
  matrix products  44.8 us (13%)
  starting transfers between devices  29.6 us (9%)
  loops' own time  12.7 us (4%)
  blocking collectives  8.99 us (3%)
    ppermute x8, waiting for transfers between devices, shifted(): return lax.ppermute(block, axis, route)  136 us
    sub x4, matrix products, one_frame(): weights = jnp.where(allowed, jnp.exp(masked - top), 0.0)  28.8 us
    slice x4, local copies, waits for them, and re-layouts, one_frame(): keys_block = block[:, :, :, 0].reshape(27 * TILE, local_heads, HD)  28.6 us
    ppermute x8, starting transfers between devices, shifted(): return lax.ppermute(block, axis, route)  19.1 us
    unnamed x15, local copies, waits for them, and re-layouts  17.4 us
    dot_general x4, matrix products, one_frame(): jnp.einsum('hqk,khd->qhd', weights.astype(jnp.bfloat16), values_block, pr...  16 us
    another operation x1, loops' own time, local(): outputs = lax.map(one_frame, jnp.arange(frames))  12.7 us
    reshape x1, local copies, waits for them, and re-layouts, local(): near = jnp.stack(pieces, axis=1).reshape((frames, 3, 3) + paired.shape[1:])  11.6 us
  transfers between devices with their start and end apart: 11, of which 6 were waited for; matrix products, arithmetic and copies ran while one was open for 6% of the time, Pallas kernels for 0%

commit v1 on v0

v1 whole, which is shorter than its diff:
```python
import functools

import jax
import jax.numpy as jnp
from jax import lax
from jax.experimental import pallas as pl
from jax.experimental.pallas import tpu as pltpu
from jax.sharding import PartitionSpec as P

HD = 128
HEADS = 8
TILE = 128
TW = 8
NEAR = 27
STEP = 4
COL = STEP * HD
C2 = HD ** (-0.5) * 1.4426950408889634
NONE = -1e30
VMEM = 63 * 2**20

ANYWHERE = pl.BlockSpec(memory_space=pl.ANY)
IN_SMEM = pl.BlockSpec(memory_space=pltpu.SMEM)
IN_VMEM = pl.BlockSpec(memory_space=pltpu.VMEM)


def frame_of(at):
    if lax.axis_size("uly") == 2:
        g = lax.axis_index("uly")
        return 1 - g if at == 0 else g
    return at


def slots_of(at):
    if lax.axis_size("uly") == 2:
        outward = 1 - 2 * lax.axis_index("uly")
        return ((0, 0), (1, -outward), (2, outward)) if at == 0 else ((0, outward), (1, 0))
    return ((0, 0), (1, 1), (2, -1)) if at == 0 else ((0, -1), (1, 0), (3, 1))


def rows_of(at):
    return pl.ds(pl.multiple_of(frame_of(at) * TILE, TILE), TILE)


def pack_kernel(key, value, first, second, sems):
    copies = []
    for at, out in enumerate((first, second)):
        for part, source in enumerate((key, value)):
            copies.append(
                pltpu.make_async_copy(
                    source.at[rows_of(at)], out.at[pl.ds(part * TILE, TILE)], sems.at[at, part]
                )
            )
    for copy in copies:
        copy.start()
    for copy in copies:
        copy.wait()


def pack(key, value):
    shape = jax.ShapeDtypeStruct((2 * TILE, HEADS * HD), key.dtype)
    return pl.pallas_call(
        pack_kernel,
        out_shape=(shape, shape),
        in_specs=[ANYWHERE, ANYWHERE],
        out_specs=(IN_VMEM, IN_VMEM),
        scratch_shapes=[pltpu.SemaphoreType.DMA((2, 2))],
        compiler_params=pltpu.CompilerParams(vmem_limit_bytes=VMEM),
        cost_estimate=pl.CostEstimate(flops=0, bytes_accessed=2**21, transcendentals=0),
        name="pack_kv",
    )(key, value)


def attend_kernel(at, height_step, n_slots, normalise, live, query, *refs):
    tiles = refs[: 3 * n_slots]
    out, stats_out = refs[-2:]
    step = pl.program_id(0)
    n_uly = lax.axis_size("uly")
    g, s = lax.axis_index("uly"), lax.axis_index("blk")
    height = 2 * (s // TW) - 1 if height_step is None else height_step
    width = 1 - 2 * (s % 2)
    offsets = [
        9 * (frame_step + 1) + 3 * (height + 1) + width_step + 1
        for _, frame_step in slots_of(at)
        for width_step in (0, width, -width)
    ]
    n = len(offsets)
    rows = rows_of(at)

    def live_row(h):
        head = step * STEP + h
        if n_uly == 2:
            held = HEADS // n_uly
            half = lax.rem(lax.div(head, held) + g, 2)
            return (half * held + lax.rem(head, held)) * 4 * NEAR + (2 * g + frame_of(at)) * NEAR
        return head * 2 * NEAR + frame_of(at) * NEAR

    heads = range(STEP)
    cols = [slice(h * HD, (h + 1) * HD) for h in heads]
    scores, highest = {}, {}
    for h in heads:
        row = live_row(h)
        q = query[rows, cols[h]]
        for t in range(n):
            score = lax.dot_general(
                q,
                tiles[t][:TILE, cols[h]],
                (((1,), (1,)), ((), ())),
                preferred_element_type=jnp.float32,
            )
            score = score + jnp.where(live[row + offsets[t]] > 0, 0.0, NONE)
            scores[h, t] = score
            highest[h] = score if t == 0 else jnp.maximum(highest[h], score)
    top = {h: jnp.max(highest[h], axis=1, keepdims=True) for h in heads}
    shift = {h: top[h] * C2 for h in heads}
    mixed, sums = {}, {}
    for h in heads:
        for t in range(n):
            w = jnp.exp2(scores[h, t] * C2 - shift[h])
            sums[h] = w if t == 0 else sums[h] + w
            o = jnp.dot(
                w.astype(jnp.bfloat16),
                tiles[t][TILE:, cols[h]],
                preferred_element_type=jnp.float32,
            )
            mixed[h] = o if t == 0 else mixed[h] + o
    total = {h: jnp.sum(sums[h], axis=1, keepdims=True) for h in heads}
    lane = lax.broadcasted_iota(jnp.int32, (TILE, HD), 1)
    stats = jnp.zeros((TILE, HD), jnp.float32)
    for h in heads:
        if normalise:
            any_live = top[h] > 0.5 * NONE
            total[h] = jnp.where(any_live, total[h], 0.0)
            mixed[h] = mixed[h] * jnp.where(any_live, 1.0 / total[h], 0.0)
        out[:, cols[h]] = mixed[h].astype(out.dtype)
        stats = jnp.where(lane == h, top[h], stats)
        stats = jnp.where(lane == STEP + h, total[h], stats)
    stats_out[...] = jnp.transpose(stats)[: 2 * STEP]


def attend(at, height_step, live, query, slots, normalise, name):
    tiles = [tile for slot, _ in slots_of(at) for tile in slots[slot]]
    pairs = len(tiles) * HEADS
    return pl.pallas_call(
        functools.partial(attend_kernel, at, height_step, len(tiles) // 3, normalise),
        out_shape=(
            jax.ShapeDtypeStruct((TILE, HEADS * HD), jnp.bfloat16 if normalise else jnp.float32),
            jax.ShapeDtypeStruct((2 * HEADS, HD), jnp.float32),
        ),
        grid=(HEADS // STEP,),
        in_specs=[IN_SMEM]
        + [pl.BlockSpec((2 * TILE, COL), lambda j: (0, j))] * (1 + len(tiles)),
        out_specs=(
            pl.BlockSpec((TILE, COL), lambda j: (0, j)),
            pl.BlockSpec((2 * STEP, HD), lambda j: (j, 0)),
        ),
        compiler_params=pltpu.CompilerParams(vmem_limit_bytes=VMEM),
        cost_estimate=pl.CostEstimate(
            flops=4 * pairs * TILE * TILE * HD,
            bytes_accessed=(len(tiles) + 2) * 2 * TILE * HEADS * HD * 2,
            transcendentals=pairs * TILE * TILE,
        ),
        name=name,
    )(live, query, *tiles)


def split_stats(stats):
    tops, totals = [], []
    for step in range(HEADS // STEP):
        start = step * 2 * STEP
        tops.append(stats[start : start + STEP])
        totals.append(stats[start + STEP : start + 2 * STEP])
    return jnp.concatenate(tops, axis=0), jnp.concatenate(totals, axis=0)


def combine_kernel(at, n_more, *refs):
    out, made, sem = refs[-3:]
    top, total = split_stats(refs[1][...])
    more = []
    best = top
    for m in range(n_more):
        top2, total2 = split_stats(refs[3 + 2 * m][...])
        top2 = jnp.where(total2 > 0.0, top2, NONE)
        more.append((top2, total2))
        best = jnp.maximum(best, top2)
    own = jnp.exp2((top - best) * C2)
    weights = [own]
    whole = total * own
    for top2, total2 in more:
        w = jnp.exp2((top2 - best) * C2) * total2
        weights.append(w)
        whole = whole + w
    inverse = 1.0 / whole
    weights = [w * inverse for w in weights]
    fill = TILE - HEADS * len(weights)
    columns = jnp.transpose(
        jnp.concatenate(weights + [jnp.zeros((fill, HD), jnp.float32)], axis=0)
    )
    for h in range(HEADS):
        cols = slice(h * HD, (h + 1) * HD)
        value = refs[0][:, cols] * columns[:, h : h + 1]
        for m in range(n_more):
            c = (m + 1) * HEADS + h
            value = value + refs[2 + 2 * m][:, cols].astype(jnp.float32) * columns[:, c : c + 1]
        made[:, cols] = value.astype(made.dtype)
    copy = pltpu.make_async_copy(made, out.at[rows_of(at)], sem)
    copy.start()
    copy.wait()


def combine(at, parts, n_more, into=None):
    specs = [IN_VMEM] * len(parts)
    extra, aliases = [], {}
    if into is not None:
        specs.append(ANYWHERE)
        extra, aliases = [into], {len(parts): 0}
    return pl.pallas_call(
        functools.partial(combine_kernel, at, n_more),
        out_shape=jax.ShapeDtypeStruct((2 * TILE, HEADS * HD), jnp.bfloat16),
        in_specs=specs,
        out_specs=ANYWHERE,
        scratch_shapes=[
            pltpu.VMEM((TILE, HEADS * HD), jnp.bfloat16),
            pltpu.SemaphoreType.DMA,
        ],
        input_output_aliases=aliases,
        compiler_params=pltpu.CompilerParams(vmem_limit_bytes=VMEM),
        name="combine",
    )(*parts, *extra)


def local(query, key, value, live):
    n_uly, n_blk = lax.axis_size("uly"), lax.axis_size("blk")
    high = n_blk // TW

    def blk_move(block, pairs):
        return lax.ppermute(block, "blk", pairs)

    def uly_shift(block, distance):
        pairs = [(i, i + distance) for i in range(n_uly) if 0 <= i + distance < n_uly]
        return lax.ppermute(block, "uly", pairs)

    def uly_swap(block):
        return lax.ppermute(block, "uly", [(0, 1), (1, 0)])

    def halo(first, second):
        if n_uly == 2:
            return [uly_swap(first)]
        return [uly_shift(second, 1), uly_shift(first, -1)]

    mate_pairs = [(i, i ^ 1) for i in range(n_blk)]
    outer_pairs = [(i, i - 1) for i in range(0, n_blk, 2) if i % TW > 0]
    outer_pairs += [(i, i + 1) for i in range(1, n_blk, 2) if i % TW < TW - 1]

    if high == 2:
        swap = [(i, (i + TW) % n_blk) for i in range(n_blk)]
        beside = [(swap, swap, None)]
    else:
        down = [(i, i + TW) for i in range(n_blk - TW)]
        up = [(i + TW, i) for i in range(n_blk - TW)]
        beside = [(down, up, 1), (up, down, -1)]

    far_queries = [blk_move(query, there) for there, _, _ in beside]
    first, second = pack(key, value)
    other_first = blk_move(first, outer_pairs)
    own_halo = halo(first, second)
    other_second = blk_move(second, outer_pairs)
    mate_first, mate_second = blk_move(first, mate_pairs), blk_move(second, mate_pairs)

    if n_uly == 2:
        other_live = uly_swap(live)
        other_first, other_live = lax.optimization_barrier((other_first, other_live))
        own_live = jnp.concatenate([live, other_live], axis=0).reshape(-1)
    else:
        own_live = lax.all_to_all(live, "uly", split_axis=1, concat_axis=0, tiled=True).reshape(-1)
    far_live = [blk_move(own_live, there) for there, _, _ in beside]
    other_halo = halo(other_first, other_second)

    def attend_beside(at, slots):
        return [
            list(attend(at, height_step, masks, queries, slots, True, "attend_beside"))
            for queries, masks, (_, _, height_step) in zip(far_queries, far_live, beside)
        ]

    slots = [(first, mate_first, other_first), (second, mate_second, other_second)]
    made = [None, None]
    if n_uly == 2:
        made[1] = attend_beside(1, slots)
        own_halo, other_halo, stats = lax.optimization_barrier(
            (own_halo, other_halo, [stats for _, stats in made[1]])
        )
        made[1] = [(part, late) for (part, _), late in zip(made[1], stats)]
    mate_halo = [blk_move(block, mate_pairs) for block in own_halo]
    slots += list(zip(own_halo, mate_halo, other_halo))
    for at in (1, 0):
        if made[at] is None:
            made[at] = attend_beside(at, slots)
    returned = [
        [blk_move(array, back) for pair, (_, back, _) in zip(made[at], beside) for array in pair]
        for at in range(2)
    ]
    own = [list(attend(at, 0, own_live, query, slots, False, "attend_own")) for at in range(2)]
    own, returned[1] = lax.optimization_barrier((own, returned[1]))
    out = None
    for at in (1, 0):
        out = combine(at, own[at] + returned[at], len(beside), out)
    return out


def solution(mesh):
    return jax.shard_map(
        local,
        mesh=mesh,
        in_specs=(
            P(("uly", "blk"), None),
            P(("uly", "blk"), None),
            P(("uly", "blk"), None),
            P("uly", None, "blk", None),
        ),
        out_specs=P(("uly", "blk"), None),
        check_vma=False,
    )
```

time: 339 us -> 77.6 us (0.23)
  the two profiles are of different devices: /device:TPU:2 before, /device:TPU:0 now
where the time goes in v1:
time: 77.6 us; the launch traced here: 77.4 us
  Pallas kernels  26.5 us (34%)
  waiting for transfers between devices  25.9 us (33%)
  starting transfers between devices  21.4 us (28%)
  local copies, waits for them, and re-layouts  3.39 us (4%)
    ppermute x11, waiting for transfers between devices, blk_move(): return lax.ppermute(block, 'blk', pairs)  23.8 us
    pallas_call x4, Pallas kernels, attend(): pl.pallas_call(functools.partial(attend_kernel, at, height_step, len(tile...  19.6 us
    ppermute x11, starting transfers between devices, blk_move(): return lax.ppermute(block, 'blk', pairs)  16.2 us
    ppermute x3, starting transfers between devices, uly_swap(): return lax.ppermute(block, 'uly', [(0, 1), (1, 0)])  5.21 us
    pallas_call x2, Pallas kernels, combine(): pl.pallas_call(functools.partial(combine_kernel, at, n_more), out_shape=j...  4.67 us
    unnamed x22, local copies, waits for them, and re-layouts  3.28 us
    pallas_call x1, Pallas kernels, pack(): pl.pallas_call(pack_kernel, out_shape=(shape, shape), in_specs=[ANYWHERE,...  2.22 us
    ppermute x3, waiting for transfers between devices, uly_swap(): return lax.ppermute(block, 'uly', [(0, 1), (1, 0)])  2.05 us
  transfers between devices with their start and end apart: 14, of which 5 were waited for; matrix products, arithmetic and copies ran while one was open for 0% of the time, Pallas kernels for 28%

profile of v1, /device:TPU:0, one launch (start us, length us, event | category | flops | bytes accessed | tf_op | source)
XLA Modules:
  0.0 77.4 jit_solution(7039752889101595259)
XLA Ops:
  0.0 0.0 copy-start.7
  0.0 2.2 %pack_kv.1 = (bf16[256,1024]{1,0:T(8,128)(2,1)}, bf16[256,1024]{1,0:T(8,128)(2,1)}) custom-call(bf16[256,1024]{1,0:T(8,128)(2,1)} %key.1, bf16[256,1024]{1,0:T(8,128)(2,1)} %value.1), custom_call_target="tpu_custom_call" | custom-call | bytes 2097152 | tf_op jit(solution)/shard_map/pack_kv/pallas_call | solution.py:61
  2.2 0.7 collective-permute-start
  2.9 4.1 %collective-permute-start.8 = (bf16[256,1024]{1,0:T(8,128)(2,1)}, bf16[256,1024]{1,0:T(8,128)(2,1)}, u32[]{:S(2)}, u32[]{:S(2)}) collective-permute-start(bf16[256,1024]{1,0:T(8,128)(2,1)} %query.3), channel_id=1, source_target_pairs={{0,8},{1,9},{2,10},{3,11},{4,12},{5,13},{6,14},{7,15},{8,0},{9,1},... | collective-permute-start | bytes 1572872 | tf_op jit(solution)/shard_map/ppermute | solution.py:236
  7.0 1.5 %collective-permute-start.4 = (bf16[256,1024]{1,0:T(8,128)(2,1)}, bf16[256,1024]{1,0:T(8,128)(2,1)}, u32[]{:S(2)}, u32[]{:S(2)}) collective-permute-start(bf16[256,1024]{1,0:T(8,128)(2,1)} %get-tuple-element.29.refs_3_), channel_id=1, source_target_pairs={{2,1},{4,3},{6,5},{10,9},{12,11},{14,13},{1,2},{3,4},{5,6},{9,10},... | collective-permute-start | bytes 1572872 | tf_op jit(solution)/shard_map/ppermute | solution.py:236
  8.5 0.0 copy-done.7
  8.5 1.5 %collective-permute-start.1 = (s32[4,4,1,27]{3,2,1,0:T(1,128)S(1)}, s32[4,4,1,27]{3,2,1,0:T(1,128)S(1)}, u32[]{:S(2)}, u32[]{:S(2)}) collective-permute-start(s32[4,4,1,27]{3,2,1,0:T(1,128)S(1)} %copy-done.7), channel_id=1, source_target_pairs={{0,16},{16,0},{1,17},{17,1},{2,18},{18,2},{3,19},{19,3},{4,20},{20... | collective-permute-start | bytes 5192 | tf_op jit(solution)/shard_map/ppermute | solution.py:243
  10.0 3.1 %collective-permute-start.3 = (bf16[256,1024]{1,0:T(8,128)(2,1)}, bf16[256,1024]{1,0:T(8,128)(2,1)}, u32[]{:S(2)}, u32[]{:S(2)}) collective-permute-start(bf16[256,1024]{1,0:T(8,128)(2,1)} %get-tuple-element.29.refs_3_), channel_id=1, source_target_pairs={{0,1},{1,0},{2,3},{3,2},{4,5},{5,4},{6,7},{7,6},{8,9},{9,8},{10,11... | collective-permute-start | bytes 1572872 | tf_op jit(solution)/shard_map/ppermute | solution.py:236
  13.1 0.0 collective-permute-done.1
  13.1 1.7 %collective-permute-start.2 = (bf16[256,1024]{1,0:T(8,128)(2,1)}, bf16[256,1024]{1,0:T(8,128)(2,1)}, u32[]{:S(2)}, u32[]{:S(2)}) collective-permute-start(bf16[256,1024]{1,0:T(8,128)(2,1)} %get-tuple-element.26.refs_0_), channel_id=1, source_target_pairs={{0,1},{1,0},{2,3},{3,2},{4,5},{5,4},{6,7},{7,6},{8,9},{9,8},{10,11... | collective-permute-start | bytes 1572872 | tf_op jit(solution)/shard_map/ppermute | solution.py:236
  14.7 0.0 collective-permute-done.refs_2_
  14.8 0.0 copy-start
  14.8 1.5 %collective-permute-start.5 = (bf16[256,1024]{1,0:T(8,128)(2,1)}, bf16[256,1024]{1,0:T(8,128)(2,1)}, u32[]{:S(2)}, u32[]{:S(2)}) collective-permute-start(bf16[256,1024]{1,0:T(8,128)(2,1)} %get-tuple-element.26.refs_0_), channel_id=1, source_target_pairs={{0,16},{16,0},{1,17},{17,1},{2,18},{18,2},{3,19},{19,3},{4,20},{20... | collective-permute-start | bytes 1572872 | tf_op jit(solution)/shard_map/ppermute | solution.py:243
  16.3 12.9 %collective-permute-done.8.query = bf16[256,1024]{1,0:T(8,128)(2,1)} collective-permute-done((bf16[256,1024]{1,0:T(8,128)(2,1)}, bf16[256,1024]{1,0:T(8,128)(2,1)}, u32[]{:S(2)}, u32[]{:S(2)}) %collective-permute-start.8) | collective-permute-done | bytes 524320 | tf_op jit(solution)/shard_map/ppermute | solution.py:236
  29.2 2.2 %collective-permute-start.6 = (bf16[256,1024]{1,0:T(8,128)(2,1)S(1)}, bf16[256,1024]{1,0:T(8,128)(2,1)}, u32[]{:S(2)}, u32[]{:S(2)}) collective-permute-start(bf16[256,1024]{1,0:T(8,128)(2,1)S(1)} %collective-permute-done.refs_2_), channel_id=1, source_target_pairs={{0,16},{16,0},{1,17},{17,1},{2,18},{18,2},{3,19},{19,3},{4,20},{20... | collective-permute-start | bytes 1572872 | tf_op jit(solution)/shard_map/ppermute | solution.py:243
  31.3 0.1 add_reduce_fusion
  31.4 0.1 reshape.3.live
  31.5 0.0 copy-start.4
  31.5 0.0 collective-permute-done.4.refs_5_
  31.5 0.1 collective-permute-start.7
  31.6 0.0 collective-permute-done.3.refs_4_
  31.6 0.0 collective-permute-done.2.refs_1_
  31.6 4.5 %collective-permute-done.7.live = s32[864]{0:T(1024)S(1)} collective-permute-done((s32[864]{0:T(1024)S(1)}, s32[864]{0:T(1024)S(1)}, u32[]{:S(2)}, u32[]{:S(2)}) %collective-permute-start.7) | collective-permute-done | bytes 3488 | tf_op jit(solution)/shard_map/ppermute | solution.py:236
  36.1 0.0 copy-done
  36.1 0.0 copy-start.5
  36.1 0.6 copy-done.5
  36.7 4.4 %attend_beside.2 = (bf16[128,1024]{1,0:T(8,128)(2,1)}, f32[16,128]{1,0:T(8,128)}) custom-call(s32[864]{0:T(1024)} %copy-done.5, bf16[256,1024]{1,0:T(8,128)(2,1)} %collective-permute-done.8.query, bf16[256,1024]{1,0:T(8,128)(2,1)} %get-tuple-element.26.refs_0_, bf16[256,1024]{1,0:T(8,128)(2,1)} %collective-permute-done.2.refs_1_, bf16[256,1024]{1,0:T(8,128)(2,1)} %copy-done, ...), custom_call_target="tpu_custom_call" | custom-call | flops 402653184 | bytes 4194304 | tf_op jit(solution)/shard_map/attend_beside/pallas_call | solution.py:143
  41.1 0.0 copy-done.4
  41.1 0.0 collective-permute-done.5.refs_6_
  41.1 2.0 %collective-permute-done.6.refs_8_ = bf16[256,1024]{1,0:T(8,128)(2,1)} collective-permute-done((bf16[256,1024]{1,0:T(8,128)(2,1)S(1)}, bf16[256,1024]{1,0:T(8,128)(2,1)}, u32[]{:S(2)}, u32[]{:S(2)}) %collective-permute-start.6) | collective-permute-done | bytes 524320 | tf_op jit(solution)/shard_map/ppermute | solution.py:243
  43.2 0.9 %collective-permute-start.9 = (bf16[256,1024]{1,0:T(8,128)(2,1)}, bf16[256,1024]{1,0:T(8,128)(2,1)S(1)}, u32[]{:S(2)}, u32[]{:S(2)}) collective-permute-start(bf16[256,1024]{1,0:T(8,128)(2,1)} %collective-permute-done.5.refs_6_), channel_id=1, source_target_pairs={{0,1},{1,0},{2,3},{3,2},{4,5},{5,4},{6,7},{7,6},{8,9},{9,8},{10,11... | collective-permute-start | bytes 1572872 | tf_op jit(solution)/shard_map/ppermute | solution.py:236
  44.0 0.0 collective-permute-start.10
  44.0 1.7 %collective-permute-done.9.refs_7_ = bf16[256,1024]{1,0:T(8,128)(2,1)S(1)} collective-permute-done((bf16[256,1024]{1,0:T(8,128)(2,1)}, bf16[256,1024]{1,0:T(8,128)(2,1)S(1)}, u32[]{:S(2)}, u32[]{:S(2)}) %collective-permute-start.9) | collective-permute-done | bytes 524320 | tf_op jit(solution)/shard_map/ppermute | solution.py:236
  45.8 0.0 copy-start.1
  45.8 0.8 %copy-done.1 = bf16[256,1024]{1,0:T(8,128)(2,1)} copy-done((bf16[256,1024]{1,0:T(8,128)(2,1)}, bf16[256,1024]{1,0:T(8,128)(2,1)S(1)}, u32[]{:S(2)}) %copy-start.1) | copy-done | bytes 524312
  46.6 5.4 %attend_beside.3 = (bf16[128,1024]{1,0:T(8,128)(2,1)}, f32[16,128]{1,0:T(8,128)}) custom-call(s32[864]{0:T(1024)} %copy-done.5, bf16[256,1024]{1,0:T(8,128)(2,1)} %collective-permute-done.8.query, bf16[256,1024]{1,0:T(8,128)(2,1)} %get-tuple-element.26.refs_0_, bf16[256,1024]{1,0:T(8,128)(2,1)} %collective-permute-done.2.refs_1_, bf16[256,1024]{1,0:T(8,128)(2,1)} %copy-done, ...), custom_call_target="tpu_custom_call" | custom-call | flops 603979776 | bytes 5767168 | tf_op jit(solution)/shard_map/attend_beside/pallas_call | solution.py:143
  52.0 0.0 copy-start.9
  52.0 0.0 copy-start.10
  52.0 1.2 %collective-permute-start.12 = (bf16[128,1024]{1,0:T(8,128)(2,1)}, bf16[128,1024]{1,0:T(8,128)(2,1)S(1)}, u32[]{:S(2)}, u32[]{:S(2)}) collective-permute-start(bf16[128,1024]{1,0:T(8,128)(2,1)} %get-tuple-element.41), channel_id=1, source_target_pairs={{0,8},{1,9},{2,10},{3,11},{4,12},{5,13},{6,14},{7,15},{8,0},{9,1},... | collective-permute-start | bytes 786440 | tf_op jit(solution)/shard_map/ppermute | solution.py:236
  53.3 4.5 %attend_own.3 = (f32[128,1024]{1,0:T(8,128)}, f32[16,128]{1,0:T(8,128)}) custom-call(s32[864]{0:T(1024)} %copy-done.4, bf16[256,1024]{1,0:T(8,128)(2,1)} %query.3, bf16[256,1024]{1,0:T(8,128)(2,1)} %get-tuple-element.26.refs_0_, bf16[256,1024]{1,0:T(8,128)(2,1)} %collective-permute-done.2.refs_1_, bf16[256,1024]{1,0:T(8,128)(2,1)} %copy-done, ...), custom_call_target="tpu_custom_call" | custom-call | flops 402653184 | bytes 4194304 | tf_op jit(solution)/shard_map/attend_own/pallas_call | solution.py:143
  57.7 0.0 copy-done.9
  57.7 1.8 %collective-permute-start.11 = (f32[16,128]{1,0:T(8,128)S(1)}, f32[16,128]{1,0:T(8,128)S(1)}, u32[]{:S(2)}, u32[]{:S(2)}) collective-permute-start(f32[16,128]{1,0:T(8,128)S(1)} %copy-done.9), channel_id=1, source_target_pairs={{0,8},{1,9},{2,10},{3,11},{4,12},{5,13},{6,14},{7,15},{8,0},{9,1},... | collective-permute-start | bytes 24584 | tf_op jit(solution)/shard_map/ppermute | solution.py:236
  59.6 0.0 copy-done.10
  59.6 1.2 %collective-permute-start.13 = (f32[16,128]{1,0:T(8,128)S(1)}, f32[16,128]{1,0:T(8,128)S(1)}, u32[]{:S(2)}, u32[]{:S(2)}) collective-permute-start(f32[16,128]{1,0:T(8,128)S(1)} %copy-done.10), channel_id=1, source_target_pairs={{0,8},{1,9},{2,10},{3,11},{4,12},{5,13},{6,14},{7,15},{8,0},{9,1},... | collective-permute-start | bytes 24584 | tf_op jit(solution)/shard_map/ppermute | solution.py:236
  60.7 5.4 %attend_own.2 = (f32[128,1024]{1,0:T(8,128)}, f32[16,128]{1,0:T(8,128)}) custom-call(s32[864]{0:T(1024)} %copy-done.4, bf16[256,1024]{1,0:T(8,128)(2,1)} %query.3, bf16[256,1024]{1,0:T(8,128)(2,1)} %get-tuple-element.26.refs_0_, bf16[256,1024]{1,0:T(8,128)(2,1)} %collective-permute-done.2.refs_1_, bf16[256,1024]{1,0:T(8,128)(2,1)} %copy-done, ...), custom_call_target="tpu_custom_call" | custom-call | flops 603979776 | bytes 5767168 | tf_op jit(solution)/shard_map/attend_own/pallas_call | solution.py:143
  66.1 0.0 collective-permute-done.10.refs_2_
  66.1 0.0 copy-start.3
  66.1 4.7 %collective-permute-done.11.refs_3_ = f32[16,128]{1,0:T(8,128)S(1)} collective-permute-done((f32[16,128]{1,0:T(8,128)S(1)}, f32[16,128]{1,0:T(8,128)S(1)}, u32[]{:S(2)}, u32[]{:S(2)}) %collective-permute-start.11) | collective-permute-done | bytes 8224 | tf_op jit(solution)/shard_map/ppermute | solution.py:236
  70.8 0.0 copy-start.8
  70.8 0.0 copy-done.3
  70.8 0.6 copy-done.8
  71.4 2.3 %combine.2.refs_4_ = bf16[256,1024]{1,0:T(8,128)(2,1)} custom-call(f32[128,1024]{1,0:T(8,128)} %get-tuple-element.43.refs_0_, f32[16,128]{1,0:T(8,128)} %get-tuple-element.44.refs_1_, bf16[128,1024]{1,0:T(8,128)(2,1)} %copy-done.3, f32[16,128]{1,0:T(8,128)} %copy-done.8), custom_call_target="tpu_custom_call" | custom-call | tf_op jit(solution)/shard_map/combine/pallas_call | solution.py:216
  73.8 0.0 collective-permute-done.13.refs_3_
  73.8 0.0 copy-start.6
  73.8 0.0 collective-permute-done.12.refs_2_
  73.8 0.6 copy-done.6
  74.4 0.0 copy-start.2
  74.4 0.7 copy-done.2
  75.1 2.3 %combine.3 = bf16[256,1024]{1,0:T(8,128)(2,1)} custom-call(f32[128,1024]{1,0:T(8,128)} %get-tuple-element.39.refs_0_, f32[16,128]{1,0:T(8,128)} %get-tuple-element.40.refs_1_, bf16[128,1024]{1,0:T(8,128)(2,1)} %copy-done.2, f32[16,128]{1,0:T(8,128)} %copy-done.6, bf16[256,1024]{1,0:T(8,128)(2,1)} %combine.2.refs_4_), custom_call_target="tpu_custom_call", output_to_operand_aliasing={{}: (4, {})} | custom-call | tf_op jit(solution)/shard_map/combine/pallas_call | solution.py:216
Async XLA Ops:
  0.0 8.5 %copy-start.7 = (s32[4,4,1,27]{3,2,1,0:T(1,128)S(1)}, s32[4,4,1,27]{3,2,1,0:T(1,128)}, u32[]{:S(2)}) copy-start(s32[4,4,1,27]{3,2,1,0:T(1,128)} %param.7) | copy-start | bytes 5188
  2.2 12.5 %collective-permute-start = (bf16[256,1024]{1,0:T(8,128)(2,1)}, bf16[256,1024]{1,0:T(8,128)(2,1)S(1)}, u32[]{:S(2)}, u32[]{:S(2)}) collective-permute-start(bf16[256,1024]{1,0:T(8,128)(2,1)} %get-tuple-element.26.refs_0_), channel_id=1, source_target_pairs={{2,1},{4,3},{6,5},{10,9},{12,11},{14,13},{1,2},{3,4},{5,6},{9,10},... | collective-permute-start | bytes 1572872 | tf_op jit(solution)/shard_map/ppermute | solution.py:236
  2.9 26.2 %collective-permute-start.8 = (bf16[256,1024]{1,0:T(8,128)(2,1)}, bf16[256,1024]{1,0:T(8,128)(2,1)}, u32[]{:S(2)}, u32[]{:S(2)}) collective-permute-start(bf16[256,1024]{1,0:T(8,128)(2,1)} %query.3), channel_id=1, source_target_pairs={{0,8},{1,9},{2,10},{3,11},{4,12},{5,13},{6,14},{7,15},{8,0},{9,1},... | collective-permute-start | bytes 1572872 | tf_op jit(solution)/shard_map/ppermute | solution.py:236
  7.0 24.5 %collective-permute-start.4 = (bf16[256,1024]{1,0:T(8,128)(2,1)}, bf16[256,1024]{1,0:T(8,128)(2,1)}, u32[]{:S(2)}, u32[]{:S(2)}) collective-permute-start(bf16[256,1024]{1,0:T(8,128)(2,1)} %get-tuple-element.29.refs_3_), channel_id=1, source_target_pairs={{2,1},{4,3},{6,5},{10,9},{12,11},{14,13},{1,2},{3,4},{5,6},{9,10},... | collective-permute-start | bytes 1572872 | tf_op jit(solution)/shard_map/ppermute | solution.py:236
  8.5 4.6 %collective-permute-start.1 = (s32[4,4,1,27]{3,2,1,0:T(1,128)S(1)}, s32[4,4,1,27]{3,2,1,0:T(1,128)S(1)}, u32[]{:S(2)}, u32[]{:S(2)}) collective-permute-start(s32[4,4,1,27]{3,2,1,0:T(1,128)S(1)} %copy-done.7), channel_id=1, source_target_pairs={{0,16},{16,0},{1,17},{17,1},{2,18},{18,2},{3,19},{19,3},{4,20},{20... | collective-permute-start | bytes 5192 | tf_op jit(solution)/shard_map/ppermute | solution.py:243
  10.0 21.6 %collective-permute-start.3 = (bf16[256,1024]{1,0:T(8,128)(2,1)}, bf16[256,1024]{1,0:T(8,128)(2,1)}, u32[]{:S(2)}, u32[]{:S(2)}) collective-permute-start(bf16[256,1024]{1,0:T(8,128)(2,1)} %get-tuple-element.29.refs_3_), channel_id=1, source_target_pairs={{0,1},{1,0},{2,3},{3,2},{4,5},{5,4},{6,7},{7,6},{8,9},{9,8},{10,11... | collective-permute-start | bytes 1572872 | tf_op jit(solution)/shard_map/ppermute | solution.py:236
  13.1 18.5 %collective-permute-start.2 = (bf16[256,1024]{1,0:T(8,128)(2,1)}, bf16[256,1024]{1,0:T(8,128)(2,1)}, u32[]{:S(2)}, u32[]{:S(2)}) collective-permute-start(bf16[256,1024]{1,0:T(8,128)(2,1)} %get-tuple-element.26.refs_0_), channel_id=1, source_target_pairs={{0,1},{1,0},{2,3},{3,2},{4,5},{5,4},{6,7},{7,6},{8,9},{9,8},{10,11... | collective-permute-start | bytes 1572872 | tf_op jit(solution)/shard_map/ppermute | solution.py:236
  14.8 21.3 %copy-start = (bf16[256,1024]{1,0:T(8,128)(2,1)}, bf16[256,1024]{1,0:T(8,128)(2,1)S(1)}, u32[]{:S(2)}) copy-start(bf16[256,1024]{1,0:T(8,128)(2,1)S(1)} %collective-permute-done.refs_2_) | copy-start | bytes 1572868
  14.8 26.4 %collective-permute-start.5 = (bf16[256,1024]{1,0:T(8,128)(2,1)}, bf16[256,1024]{1,0:T(8,128)(2,1)}, u32[]{:S(2)}, u32[]{:S(2)}) collective-permute-start(bf16[256,1024]{1,0:T(8,128)(2,1)} %get-tuple-element.26.refs_0_), channel_id=1, source_target_pairs={{0,16},{16,0},{1,17},{17,1},{2,18},{18,2},{3,19},{19,3},{4,20},{20... | collective-permute-start | bytes 1572872 | tf_op jit(solution)/shard_map/ppermute | solution.py:243
  29.2 14.0 %collective-permute-start.6 = (bf16[256,1024]{1,0:T(8,128)(2,1)S(1)}, bf16[256,1024]{1,0:T(8,128)(2,1)}, u32[]{:S(2)}, u32[]{:S(2)}) collective-permute-start(bf16[256,1024]{1,0:T(8,128)(2,1)S(1)} %collective-permute-done.refs_2_), channel_id=1, source_target_pairs={{0,16},{16,0},{1,17},{17,1},{2,18},{18,2},{3,19},{19,3},{4,20},{20... | collective-permute-start | bytes 1572872 | tf_op jit(solution)/shard_map/ppermute | solution.py:243
  31.5 9.6 %copy-start.4 = (s32[864]{0:T(1024)}, s32[864]{0:T(1024)S(1)}, u32[]{:S(2)}) copy-start(s32[864]{0:T(1024)S(1)} %reshape.3.live) | copy-start | bytes 10372
  31.5 4.6 %collective-permute-start.7 = (s32[864]{0:T(1024)S(1)}, s32[864]{0:T(1024)S(1)}, u32[]{:S(2)}, u32[]{:S(2)}) collective-permute-start(s32[864]{0:T(1024)S(1)} %reshape.3.live), channel_id=1, source_target_pairs={{0,8},{1,9},{2,10},{3,11},{4,12},{5,13},{6,14},{7,15},{8,0},{9,1},... | collective-permute-start | bytes 10376 | tf_op jit(solution)/shard_map/ppermute | solution.py:236
  36.1 0.6 copy-start.5
  43.2 2.6 %collective-permute-start.9 = (bf16[256,1024]{1,0:T(8,128)(2,1)}, bf16[256,1024]{1,0:T(8,128)(2,1)S(1)}, u32[]{:S(2)}, u32[]{:S(2)}) collective-permute-start(bf16[256,1024]{1,0:T(8,128)(2,1)} %collective-permute-done.5.refs_6_), channel_id=1, source_target_pairs={{0,1},{1,0},{2,3},{3,2},{4,5},{5,4},{6,7},{7,6},{8,9},{9,8},{10,11... | collective-permute-start | bytes 1572872 | tf_op jit(solution)/shard_map/ppermute | solution.py:236
  44.0 22.1 %collective-permute-start.10 = (bf16[128,1024]{1,0:T(8,128)(2,1)}, bf16[128,1024]{1,0:T(8,128)(2,1)S(1)}, u32[]{:S(2)}, u32[]{:S(2)}) collective-permute-start(bf16[128,1024]{1,0:T(8,128)(2,1)} %get-tuple-element.37), channel_id=1, source_target_pairs={{0,8},{1,9},{2,10},{3,11},{4,12},{5,13},{6,14},{7,15},{8,0},{9,1},... | collective-permute-start | bytes 786440 | tf_op jit(solution)/shard_map/ppermute | solution.py:236
  45.8 0.8 %copy-start.1 = (bf16[256,1024]{1,0:T(8,128)(2,1)}, bf16[256,1024]{1,0:T(8,128)(2,1)S(1)}, u32[]{:S(2)}) copy-start(bf16[256,1024]{1,0:T(8,128)(2,1)S(1)} %collective-permute-done.9.refs_7_) | copy-start | bytes 1572868
  52.0 5.7 %copy-start.9 = (f32[16,128]{1,0:T(8,128)S(1)}, f32[16,128]{1,0:T(8,128)}, u32[]{:S(2)}) copy-start(f32[16,128]{1,0:T(8,128)} %get-tuple-element.38) | copy-start | bytes 24580
  52.0 7.5 %copy-start.10 = (f32[16,128]{1,0:T(8,128)S(1)}, f32[16,128]{1,0:T(8,128)}, u32[]{:S(2)}) copy-start(f32[16,128]{1,0:T(8,128)} %get-tuple-element.42) | copy-start | bytes 24580
  52.0 21.8 %collective-permute-start.12 = (bf16[128,1024]{1,0:T(8,128)(2,1)}, bf16[128,1024]{1,0:T(8,128)(2,1)S(1)}, u32[]{:S(2)}, u32[]{:S(2)}) collective-permute-start(bf16[128,1024]{1,0:T(8,128)(2,1)} %get-tuple-element.41), channel_id=1, source_target_pairs={{0,8},{1,9},{2,10},{3,11},{4,12},{5,13},{6,14},{7,15},{8,0},{9,1},... | collective-permute-start | bytes 786440 | tf_op jit(solution)/shard_map/ppermute | solution.py:236
  57.7 13.1 %collective-permute-start.11 = (f32[16,128]{1,0:T(8,128)S(1)}, f32[16,128]{1,0:T(8,128)S(1)}, u32[]{:S(2)}, u32[]{:S(2)}) collective-permute-start(f32[16,128]{1,0:T(8,128)S(1)} %copy-done.9), channel_id=1, source_target_pairs={{0,8},{1,9},{2,10},{3,11},{4,12},{5,13},{6,14},{7,15},{8,0},{9,1},... | collective-permute-start | bytes 24584 | tf_op jit(solution)/shard_map/ppermute | solution.py:236
  59.6 14.2 %collective-permute-start.13 = (f32[16,128]{1,0:T(8,128)S(1)}, f32[16,128]{1,0:T(8,128)S(1)}, u32[]{:S(2)}, u32[]{:S(2)}) collective-permute-start(f32[16,128]{1,0:T(8,128)S(1)} %copy-done.10), channel_id=1, source_target_pairs={{0,8},{1,9},{2,10},{3,11},{4,12},{5,13},{6,14},{7,15},{8,0},{9,1},... | collective-permute-start | bytes 24584 | tf_op jit(solution)/shard_map/ppermute | solution.py:236
  66.1 4.7 %copy-start.3 = (bf16[128,1024]{1,0:T(8,128)(2,1)}, bf16[128,1024]{1,0:T(8,128)(2,1)S(1)}, u32[]{:S(2)}) copy-start(bf16[128,1024]{1,0:T(8,128)(2,1)S(1)} %collective-permute-done.10.refs_2_) | copy-start | bytes 786436
  70.8 0.6 copy-start.8
  73.8 0.6 copy-start.6
  74.4 0.7 copy-start.2

commit v2 on v1

v2 whole, which is shorter than its diff:
```python
import functools

import jax
import jax.numpy as jnp
from jax import lax
from jax.experimental import pallas as pl
from jax.experimental.pallas import tpu as pltpu
from jax.sharding import PartitionSpec as P

HD = 128
HEADS = 8
TILE = 128
TW = 8
NEAR = 27
STEP = 4
COL = STEP * HD
C2 = HD ** (-0.5) * 1.4426950408889634
NONE = -1e30
STAT_ROWS = 8
TERMS = 3
VMEM = 20 * 2**20

ANYWHERE = pl.BlockSpec(memory_space=pl.ANY)
IN_SMEM = pl.BlockSpec(memory_space=pltpu.SMEM)
IN_VMEM = pl.BlockSpec(memory_space=pltpu.VMEM)


def is_small():
    return lax.axis_size("uly") == 2 and lax.axis_size("blk") == 2 * TW


def frame_of(at):
    if is_small():
        g = lax.axis_index("uly")
        return 1 - g if at == 0 else g
    return at


def slots_of(at):
    if is_small():
        outward = 1 - 2 * lax.axis_index("uly")
        return ((0, 0), (1, -outward), (2, outward)) if at == 0 else ((0, outward), (1, 0))
    return ((0, 0), (1, 1), (2, -1)) if at == 0 else ((0, -1), (1, 0), (3, 1))


def rows_of(at):
    return pl.ds(pl.multiple_of(frame_of(at) * TILE, TILE), TILE)


def pack_kernel(key, value, both, border, sems):
    moves = []
    for row, (at, source) in enumerate(((1, key), (0, key), (0, value), (1, value))):
        moves.append((source.at[rows_of(at)], both.at[pl.ds(row * TILE, TILE)]))
    for half, source in enumerate((key, value)):
        moves.append((source.at[rows_of(0)], border.at[pl.ds(half * TILE, TILE)]))
    copies = [pltpu.make_async_copy(*move, sems.at[i]) for i, move in enumerate(moves)]
    for copy in copies:
        copy.start()
    for copy in copies:
        copy.wait()


def pack(key, value):
    def rows(tiles):
        return jax.ShapeDtypeStruct((tiles * TILE, HEADS * HD), key.dtype)

    return pl.pallas_call(
        pack_kernel,
        out_shape=(rows(4), rows(2)),
        in_specs=[ANYWHERE] * 2,
        out_specs=(IN_VMEM,) * 2,
        scratch_shapes=[pltpu.SemaphoreType.DMA((6,))],
        compiler_params=pltpu.CompilerParams(vmem_limit_bytes=VMEM),
        cost_estimate=pl.CostEstimate(flops=0, bytes_accessed=2**21, transcendentals=0),
        name="pack_kv",
    )(key, value)


def attend_kernel(at, which, height_step, places, travels, n_live, *refs):
    live, query, refs = refs[:n_live], refs[n_live], refs[n_live + 1 :]
    out, stats_out = (refs[-1], None) if travels else refs[-2:]
    step = pl.program_id(0)
    g, s = lax.axis_index("uly"), lax.axis_index("blk")
    height = 2 * (s // TW) - 1 if height_step is None else height_step
    width = 1 - 2 * (s % 2)
    offsets = {
        (slot, c): 9 * (frame_step + 1) + 3 * (height + 1) + width_step + 1
        for slot, frame_step in slots_of(at)
        for c, width_step in enumerate((0, width, -width))
    }

    def is_live(h, offset):
        head = step * STEP + h
        if is_small():
            held = HEADS // 2
            place = (which * held + lax.rem(head, held), 2 * g + frame_of(at), 0, offset)
            own_head = lax.div(head, held) == g
            return jnp.where(own_head, live[0][place], live[1][place]) > 0
        return live[0][head, frame_of(at), 0, offset] > 0

    heads = range(STEP)
    cols = [slice(h * HD, (h + 1) * HD) for h in heads]
    scores, highest = {}, {}
    for h in heads:
        q = query[rows_of(at), cols[h]]
        for block, (k_row, _, tiles) in enumerate(places):
            keys = refs[block][k_row : k_row + len(tiles) * TILE, cols[h]]
            score = lax.dot_general(
                q, keys, (((1,), (1,)), ((), ())), preferred_element_type=jnp.float32
            )
            for i, t in enumerate(tiles):
                part = score[:, i * TILE : (i + 1) * TILE]
                part = part + jnp.where(is_live(h, offsets[t]), 0.0, NONE)
                scores[h, t] = part
                highest[h] = jnp.maximum(highest[h], part) if h in highest else part
    top = {h: jnp.max(highest[h], axis=1, keepdims=True) for h in heads}
    shift = {h: top[h] * C2 for h in heads}
    mixed, sums = {}, {}
    for h in heads:
        for block, (_, v_row, tiles) in enumerate(places):
            weights = []
            for t in reversed(tiles):
                w = jnp.exp2(scores[h, t] * C2 - shift[h])
                sums[h] = sums[h] + w if h in sums else w
                weights.append(w.astype(jnp.bfloat16))
            values = refs[block][v_row : v_row + len(tiles) * TILE, cols[h]]
            o = jnp.dot(
                weights[0] if len(weights) == 1 else jnp.concatenate(weights, axis=1),
                values,
                preferred_element_type=jnp.float32,
            )
            mixed[h] = mixed[h] + o if h in mixed else o
    total = {h: jnp.sum(sums[h], axis=1, keepdims=True) for h in heads}
    lane = lax.broadcasted_iota(jnp.int32, (TILE, HD), 1)
    stats = jnp.zeros((TILE, HD), jnp.float32)
    for h in heads:
        if travels:
            any_live = top[h] > 0.5 * NONE
            total[h] = jnp.where(any_live, total[h], 0.0)
            mixed[h] = mixed[h] * jnp.where(any_live, 1.0 / total[h], 0.0)
        out[:TILE, cols[h]] = mixed[h].astype(out.dtype)
        stats = jnp.where(lane == h, top[h], stats)
        stats = jnp.where(lane == STEP + h, total[h], stats)
    stats = jnp.transpose(stats)[:STAT_ROWS]
    if travels:
        for term in range(TERMS):
            rounded = stats.astype(jnp.bfloat16)
            out[TILE:, cols[term]] = rounded
            stats = stats - rounded.astype(jnp.float32)
        out[TILE:, cols[TERMS]] = jnp.zeros((STAT_ROWS, HD), jnp.bfloat16)
    else:
        stats_out[...] = stats


def attend(at, which, height_step, live, query, both, beyond, travels, name, after):
    blocks = list(both)
    places = [(0, 2 * TILE, ((1, c), (0, c))) for c in range(3)]
    for slot, _ in slots_of(at)[2:]:
        blocks += beyond[slot - 2]
        places += [(0, TILE, ((slot, c),)) for c in range(3)]
    pairs = sum(len(tiles) for _, _, tiles in places) * HEADS
    steps = HEADS // STEP
    if travels:
        out_shape = jax.ShapeDtypeStruct((TILE + STAT_ROWS, HEADS * HD), jnp.bfloat16)
        out_specs = pl.BlockSpec((TILE + STAT_ROWS, COL), lambda j: (0, j))
    else:
        out_shape = (
            jax.ShapeDtypeStruct((TILE, HEADS * HD), jnp.float32),
            jax.ShapeDtypeStruct((steps * STAT_ROWS, HD), jnp.float32),
        )
        out_specs = (
            pl.BlockSpec((TILE, COL), lambda j: (0, j)),
            pl.BlockSpec((STAT_ROWS, HD), lambda j: (j, 0)),
        )
    return pl.pallas_call(
        functools.partial(attend_kernel, at, which, height_step, places, travels, len(live)),
        out_shape=out_shape,
        grid=(steps,),
        in_specs=[IN_SMEM] * len(live)
        + [pl.BlockSpec((array.shape[0], COL), lambda j: (0, j)) for array in [query] + blocks]
        + [ANYWHERE] * len(after),
        out_specs=out_specs,
        compiler_params=pltpu.CompilerParams(vmem_limit_bytes=VMEM),
        cost_estimate=pl.CostEstimate(
            flops=4 * pairs * TILE * TILE * HD,
            bytes_accessed=(pairs // HEADS + 2) * 2 * TILE * HEADS * HD * 2,
            transcendentals=pairs * TILE * TILE,
        ),
        name=name,
    )(*live, query, *blocks, *after)


def split_stats(per_step):
    tops = jnp.concatenate([stats[:STEP] for stats in per_step], axis=0)
    totals = jnp.concatenate([stats[STEP : 2 * STEP] for stats in per_step], axis=0)
    return tops, totals


def own_stats(ref):
    steps = range(HEADS // STEP)
    return split_stats([ref[step * STAT_ROWS : (step + 1) * STAT_ROWS] for step in steps])


def travelled_stats(ref):
    per_step = []
    for step in range(HEADS // STEP):
        first = step * COL
        terms = [ref[TILE:, first + HD * t : first + HD * (t + 1)] for t in range(TERMS)]
        per_step.append(sum(term.astype(jnp.float32) for term in terms))
    return split_stats(per_step)


def combine_kernel(at, n_more, *refs):
    out, made, sem = refs[-3:]
    top, total = own_stats(refs[1])
    more = []
    best = top
    for m in range(n_more):
        top2, total2 = travelled_stats(refs[2 + m])
        top2 = jnp.where(total2 > 0.0, top2, NONE)
        more.append((top2, total2))
        best = jnp.maximum(best, top2)
    own = jnp.exp2((top - best) * C2)
    weights = [own]
    whole = total * own
    for top2, total2 in more:
        w = jnp.exp2((top2 - best) * C2) * total2
        weights.append(w)
        whole = whole + w
    inverse = 1.0 / whole
    weights = [w * inverse for w in weights]
    fill = TILE - HEADS * len(weights)
    columns = jnp.transpose(
        jnp.concatenate(weights + [jnp.zeros((fill, HD), jnp.float32)], axis=0)
    )
    for h in range(HEADS):
        cols = slice(h * HD, (h + 1) * HD)
        value = refs[0][:, cols] * columns[:, h : h + 1]
        for m in range(n_more):
            c = (m + 1) * HEADS + h
            value = value + refs[2 + m][:TILE, cols].astype(jnp.float32) * columns[:, c : c + 1]
        made[:, cols] = value.astype(made.dtype)
    copy = pltpu.make_async_copy(made, out.at[rows_of(at)], sem)
    copy.start()
    copy.wait()


def combine(at, parts, n_more, into=None):
    specs = [IN_VMEM] * len(parts)
    extra, aliases = [], {}
    if into is not None:
        specs.append(ANYWHERE)
        extra, aliases = [into], {len(parts): 0}
    return pl.pallas_call(
        functools.partial(combine_kernel, at, n_more),
        out_shape=jax.ShapeDtypeStruct((2 * TILE, HEADS * HD), jnp.bfloat16),
        in_specs=specs,
        out_specs=ANYWHERE,
        scratch_shapes=[
            pltpu.VMEM((TILE, HEADS * HD), jnp.bfloat16),
            pltpu.SemaphoreType.DMA,
        ],
        input_output_aliases=aliases,
        compiler_params=pltpu.CompilerParams(vmem_limit_bytes=VMEM),
        name="combine",
    )(*parts, *extra)


def local(query, key, value, live):
    n_uly, n_blk = lax.axis_size("uly"), lax.axis_size("blk")
    high = n_blk // TW

    def blk_move(block, pairs):
        return lax.ppermute(block, "blk", pairs)

    def uly_shift(block, distance):
        pairs = [(i, i + distance) for i in range(n_uly) if 0 <= i + distance < n_uly]
        return lax.ppermute(block, "uly", pairs)

    def uly_swap(block):
        return lax.ppermute(block, "uly", [(0, 1), (1, 0)])

    def halo(both, border):
        if is_small():
            return [uly_swap(border)]
        after = jnp.concatenate([both[:TILE], both[3 * TILE :]], axis=0)
        return [uly_shift(after, 1), uly_shift(border_of(both), -1)]

    def border_of(both):
        return both[TILE : 3 * TILE]

    mate_pairs = [(i, i ^ 1) for i in range(n_blk)]
    outer_pairs = [(i, i - 1) for i in range(0, n_blk, 2) if i % TW > 0]
    outer_pairs += [(i, i + 1) for i in range(1, n_blk, 2) if i % TW < TW - 1]

    if high == 2:
        swap = [(i, (i + TW) % n_blk) for i in range(n_blk)]
        beside = [(swap, swap, None)]
    else:
        down = [(i, i + TW) for i in range(n_blk - TW)]
        up = [(i + TW, i) for i in range(n_blk - TW)]
        beside = [(down, up, 1), (up, down, -1)]

    both, border = pack(key, value)
    if is_small():
        far_live = blk_move(live, beside[0][0])
        far_live, query, both = lax.optimization_barrier((far_live, query, both))
        held = ((0, len(live), 0), (0, 0, 0), (0, 0, 0), (0, 0, 0))
        below = ((len(live), 0, 0), (0, 0, 0), (0, 0, 0), (0, 0, 0))
        live = lax.pad(live, 0, held) + lax.pad(far_live, 0, below)
        other_live = uly_swap(live)
        border, other_live = lax.optimization_barrier((border, other_live))
        own_live, far_live = [live, other_live], [[live, other_live]]
    else:
        own_live = [lax.all_to_all(live, "uly", split_axis=1, concat_axis=0, tiled=True)]
        far_live = [[blk_move(own_live[0], there)] for there, _, _ in beside]
    far_queries = [blk_move(query, there) for there, _, _ in beside]
    other = blk_move(both, outer_pairs)
    mate = blk_move(both, mate_pairs)
    own_halo = halo(both, border)
    other_halo = halo(other, border_of(other))

    def attend_beside(at, after):
        return [
            attend(at, 1, height_step, masks, block, blocks, beyond, True, "attend_beside", after)
            for block, masks, (_, _, height_step) in zip(far_queries, far_live, beside)
        ]

    blocks, beyond = (both, mate, other), []
    made = [None, None]
    after = []
    if is_small():
        made[1] = attend_beside(1, [])
        own_halo, after = lax.optimization_barrier((own_halo, made[1]))
    mate_halo = [blk_move(block, mate_pairs) for block in own_halo]
    beyond += [list(halos) for halos in zip(own_halo, mate_halo, other_halo)]
    if not is_small():
        made[1] = attend_beside(1, [])
    made[0] = attend_beside(0, after)
    returned = [
        [blk_move(part, back) for part, (_, back, _) in zip(made[at], beside)] for at in range(2)
    ]
    own = [
        attend(at, 0, 0, own_live, query, blocks, beyond, False, "attend_own", [])
        for at in range(2)
    ]
    own, returned[1] = lax.optimization_barrier((own, returned[1]))
    out = None
    for at in (1, 0):
        out = combine(at, list(own[at]) + returned[at], len(beside), out)
    return out


def solution(mesh):
    return jax.shard_map(
        local,
        mesh=mesh,
        in_specs=(
            P(("uly", "blk"), None),
            P(("uly", "blk"), None),
            P(("uly", "blk"), None),
            P("uly", None, "blk", None),
        ),
        out_specs=P(("uly", "blk"), None),
        check_vma=False,
    )
```

time: 77.6 us -> 68.3 us (0.88)
  Pallas kernels: 26.5 us -> 16.2 us
  waiting for transfers between devices: 25.9 us -> 34.1 us
  starting transfers between devices: 21.4 us -> 15.6 us
  local copies, waits for them, and re-layouts: 3.39 us -> 2.12 us
    pallas_call x5, Pallas kernels: 21.9 us -> 13.7 us  [the longest x4 13.6 us: attend(): pl.pallas_call(functools.partial(attend_kernel, at, which, height_step, p...]
    ppermute x11 -> x7, waiting for transfers between devices: 23.8 us -> 31.9 us  [blk_move(): return lax.ppermute(block, 'blk', pairs)]
    ppermute x11 -> x7, starting transfers between devices: 16.2 us -> 11.9 us  [blk_move(): return lax.ppermute(block, 'blk', pairs)]
    pallas_call x2, Pallas kernels: 4.67 us -> 2.43 us  [combine(): pl.pallas_call(functools.partial(combine_kernel, at, n_more), out_shape=j...]
    ppermute x3, starting transfers between devices: 5.21 us -> 3.68 us  [uly_swap(): return lax.ppermute(block, 'uly', [(0, 1), (1, 0)])]
    unnamed x22 -> x8, local copies, waits for them, and re-layouts: 3.28 us -> 2.09 us
  transfers between devices with their start and end apart: 14 -> 10, of which waited for: 5 -> 5; matrix products, arithmetic and copies ran while one was open for 0% -> 0% of each run, Pallas kernels for 28% -> 22%
where the time goes in v2:
time: 68.3 us; the launch traced here: 68.1 us
  waiting for transfers between devices  34.1 us (50%)
  Pallas kernels  16.2 us (24%)
  starting transfers between devices  15.6 us (23%)
  local copies, waits for them, and re-layouts  2.12 us (3%)
    ppermute x7, waiting for transfers between devices, blk_move(): return lax.ppermute(block, 'blk', pairs)  31.9 us
    pallas_call x4, Pallas kernels, attend(): pl.pallas_call(functools.partial(attend_kernel, at, which, height_step, p...  13.6 us
    ppermute x7, starting transfers between devices, blk_move(): return lax.ppermute(block, 'blk', pairs)  11.9 us
    ppermute x3, starting transfers between devices, uly_swap(): return lax.ppermute(block, 'uly', [(0, 1), (1, 0)])  3.68 us
    pallas_call x2, Pallas kernels, combine(): pl.pallas_call(functools.partial(combine_kernel, at, n_more), out_shape=j...  2.43 us
    ppermute x3, waiting for transfers between devices, uly_swap(): return lax.ppermute(block, 'uly', [(0, 1), (1, 0)])  2.22 us
    unnamed x8, local copies, waits for them, and re-layouts  2.09 us
  transfers between devices with their start and end apart: 10, of which 5 were waited for; matrix products, arithmetic and copies ran while one was open for 0% of the time, Pallas kernels for 22%

profile of v2, /device:TPU:0, one launch (start us, length us, event | category | flops | bytes accessed | tf_op | source)
XLA Modules:
  0.0 68.1 jit_solution(629475602399553573)
XLA Ops:
  0.0 0.0 copy-start
  0.0 4.0 %collective-permute-start = (s32[4,4,1,27]{3,2,1,0:T(1,128)}, s32[4,4,1,27]{3,2,1,0:T(1,128)S(1)}, u32[]{:S(2)}, u32[]{:S(2)}) collective-permute-start(s32[4,4,1,27]{3,2,1,0:T(1,128)} %param.7), channel_id=1, source_target_pairs={{0,8},{1,9},{2,10},{3,11},{4,12},{5,13},{6,14},{7,15},{8,0},{9,1},... | collective-permute-start | bytes 5192 | tf_op jit(solution)/shard_map/ppermute | solution.py:274
  4.0 0.0 copy-start.1
  4.0 1.0 %copy-done.1 = bf16[256,1024]{1,0:T(8,128)(2,1)S(1)} copy-done((bf16[256,1024]{1,0:T(8,128)(2,1)S(1)}, bf16[256,1024]{1,0:T(8,128)(2,1)}, u32[]{:S(2)}) %copy-start.1) | copy-done | bytes 524312
  5.1 0.0 copy-start.2
  5.1 1.0 %copy-done.2 = bf16[256,1024]{1,0:T(8,128)(2,1)S(1)} copy-done((bf16[256,1024]{1,0:T(8,128)(2,1)S(1)}, bf16[256,1024]{1,0:T(8,128)(2,1)}, u32[]{:S(2)}) %copy-start.2) | copy-done | bytes 524312
  6.1 0.0 copy-start.3
  6.1 0.2 pack_kv.1
  6.3 0.0 collective-permute-done
  6.3 0.7 %collective-permute-start.3 = (bf16[512,1024]{1,0:T(8,128)(2,1)S(1)}, bf16[512,1024]{1,0:T(8,128)(2,1)S(1)}, u32[]{:S(2)}, u32[]{:S(2)}) collective-permute-start(bf16[512,1024]{1,0:T(8,128)(2,1)S(1)} %get-tuple-element.28.refs_3_), channel_id=1, source_target_pairs={{2,1},{4,3},{6,5},{10,9},{12,11},{14,13},{1,2},{3,4},{5,6},{9,10},... | collective-permute-start | bytes 3145736 | tf_op jit(solution)/shard_map/ppermute | solution.py:274
  7.1 2.9 %collective-permute-start.2 = (bf16[512,1024]{1,0:T(8,128)(2,1)S(1)}, bf16[512,1024]{1,0:T(8,128)(2,1)S(1)}, u32[]{:S(2)}, u32[]{:S(2)}) collective-permute-start(bf16[512,1024]{1,0:T(8,128)(2,1)S(1)} %get-tuple-element.28.refs_3_), channel_id=1, source_target_pairs={{0,1},{1,0},{2,3},{3,2},{4,5},{5,4},{6,7},{7,6},{8,9},{9,8},{10,11... | collective-permute-start | bytes 3145736 | tf_op jit(solution)/shard_map/ppermute | solution.py:274
  9.9 0.0 copy-done
  9.9 2.5 %collective-permute-start.5 = (bf16[256,1024]{1,0:T(8,128)(2,1)S(1)}, bf16[256,1024]{1,0:T(8,128)(2,1)S(1)}, u32[]{:S(2)}, u32[]{:S(2)}) collective-permute-start(bf16[256,1024]{1,0:T(8,128)(2,1)S(1)} %copy-done), channel_id=1, source_target_pairs={{0,8},{1,9},{2,10},{3,11},{4,12},{5,13},{6,14},{7,15},{8,0},{9,1},... | collective-permute-start | bytes 1572872 | tf_op jit(solution)/shard_map/ppermute | solution.py:274
  12.4 0.0 copy-done.3
  12.4 1.6 %collective-permute-start.1 = (s32[8,4,1,27]{3,2,1,0:T(1,128)S(1)}, s32[8,4,1,27]{3,2,1,0:T(1,128)S(1)}, u32[]{:S(2)}, u32[]{:S(2)}) collective-permute-start(s32[8,4,1,27]{3,2,1,0:T(1,128)S(1)} %pad_add_fusion.refs_0_), channel_id=1, source_target_pairs={{0,16},{16,0},{1,17},{17,1},{2,18},{18,2},{3,19},{19,3},{4,20},{20... | collective-permute-start | bytes 10376 | tf_op jit(solution)/shard_map/ppermute | solution.py:281
  14.0 2.2 %collective-permute-done.1.refs_1_ = s32[8,4,1,27]{3,2,1,0:T(1,128)S(1)} collective-permute-done((s32[8,4,1,27]{3,2,1,0:T(1,128)S(1)}, s32[8,4,1,27]{3,2,1,0:T(1,128)S(1)}, u32[]{:S(2)}, u32[]{:S(2)}) %collective-permute-start.1) | collective-permute-done | bytes 3488 | tf_op jit(solution)/shard_map/ppermute | solution.py:281
  16.2 1.5 %collective-permute-start.4 = (bf16[256,1024]{1,0:T(8,128)(2,1)S(1)}, bf16[256,1024]{1,0:T(8,128)(2,1)S(1)}, u32[]{:S(2)}, u32[]{:S(2)}) collective-permute-start(bf16[256,1024]{1,0:T(8,128)(2,1)S(1)} %get-tuple-element.29), channel_id=1, source_target_pairs={{0,16},{16,0},{1,17},{17,1},{2,18},{18,2},{3,19},{19,3},{4,20},{20... | collective-permute-start | bytes 1572872 | tf_op jit(solution)/shard_map/ppermute | solution.py:281
  17.7 0.0 collective-permute-done.3.refs_5_
  17.8 0.6 collective-permute-start.7
  18.3 17.7 %collective-permute-done.5.refs_2_ = bf16[256,1024]{1,0:T(8,128)(2,1)S(1)} collective-permute-done((bf16[256,1024]{1,0:T(8,128)(2,1)S(1)}, bf16[256,1024]{1,0:T(8,128)(2,1)S(1)}, u32[]{:S(2)}, u32[]{:S(2)}) %collective-permute-start.5) | collective-permute-done | bytes 524320 | tf_op jit(solution)/shard_map/ppermute | solution.py:274
  36.0 0.0 collective-permute-done.2.refs_4_
  36.0 2.9 %attend_beside.2.refs_9_ = bf16[136,1024]{1,0:T(8,128)(2,1)S(1)} custom-call(s32[8,4,1,27]{3,2,1,0:T(1,128)S(1)} %pad_add_fusion.refs_0_, s32[8,4,1,27]{3,2,1,0:T(1,128)S(1)} %collective-permute-done.1.refs_1_, bf16[256,1024]{1,0:T(8,128)(2,1)S(1)} %collective-permute-done.5.refs_2_, bf16[512,1024]{1,0:T(8,128)(2,1)S(1)} %get-tuple-element.28.refs_3_, ...), custom_call_target="tpu_custom_call" | custom-call | flops 402653184 | bytes 4194304 | tf_op jit(solution)/shard_map/attend_beside/pallas_call | solution.py:175
  38.9 0.0 collective-permute-done.4.refs_6_
  38.9 0.1 collective-permute-start.6
  39.0 0.6 collective-permute-start.8
  39.6 0.0 collective-permute-done.7.refs_8_
  39.6 1.3 %collective-permute-done.6.refs_7_ = bf16[256,1024]{1,0:T(8,128)(2,1)S(1)} collective-permute-done((bf16[256,1024]{1,0:T(8,128)(2,1)S(1)}, bf16[256,1024]{1,0:T(8,128)(2,1)S(1)}, u32[]{:S(2)}, u32[]{:S(2)}) %collective-permute-start.6) | collective-permute-done | bytes 524320 | tf_op jit(solution)/shard_map/ppermute | solution.py:274
  40.9 3.9 %attend_beside.3 = bf16[136,1024]{1,0:T(8,128)(2,1)S(1)} custom-call(s32[8,4,1,27]{3,2,1,0:T(1,128)S(1)} %pad_add_fusion.refs_0_, s32[8,4,1,27]{3,2,1,0:T(1,128)S(1)} %collective-permute-done.1.refs_1_, bf16[256,1024]{1,0:T(8,128)(2,1)S(1)} %collective-permute-done.5.refs_2_, bf16[512,1024]{1,0:T(8,128)(2,1)S(1)} %get-tuple-element.28.refs_3_, ...), custom_call_target="tpu_custom_call" | custom-call | flops 603979776 | bytes 5767168 | tf_op jit(solution)/shard_map/attend_beside/pallas_call | solution.py:175
  44.8 1.2 %collective-permute-start.9 = (bf16[136,1024]{1,0:T(8,128)(2,1)S(1)}, bf16[136,1024]{1,0:T(8,128)(2,1)S(1)}, u32[]{:S(2)}, u32[]{:S(2)}) collective-permute-start(bf16[136,1024]{1,0:T(8,128)(2,1)S(1)} %attend_beside.3), channel_id=1, source_target_pairs={{0,8},{1,9},{2,10},{3,11},{4,12},{5,13},{6,14},{7,15},{8,0},{9,1},... | collective-permute-start | bytes 835592 | tf_op jit(solution)/shard_map/ppermute | solution.py:274
  46.0 2.9 %attend_own.3 = (f32[128,1024]{1,0:T(8,128)S(1)}, f32[16,128]{1,0:T(8,128)S(1)}) custom-call(s32[8,4,1,27]{3,2,1,0:T(1,128)S(1)} %pad_add_fusion.refs_0_, s32[8,4,1,27]{3,2,1,0:T(1,128)S(1)} %collective-permute-done.1.refs_1_, bf16[256,1024]{1,0:T(8,128)(2,1)S(1)} %copy-done, bf16[512,1024]{1,0:T(8,128)(2,1)S(1)} %get-tuple-element.28.refs_3_, ...), custom_call_target="tpu_custom_call" | custom-call | flops 402653184 | bytes 4194304 | tf_op jit(solution)/shard_map/attend_own/pallas_call | solution.py:175
  48.9 3.9 %attend_own.2 = (f32[128,1024]{1,0:T(8,128)S(1)}, f32[16,128]{1,0:T(8,128)S(1)}) custom-call(s32[8,4,1,27]{3,2,1,0:T(1,128)S(1)} %pad_add_fusion.refs_0_, s32[8,4,1,27]{3,2,1,0:T(1,128)S(1)} %collective-permute-done.1.refs_1_, bf16[256,1024]{1,0:T(8,128)(2,1)S(1)} %copy-done, bf16[512,1024]{1,0:T(8,128)(2,1)S(1)} %get-tuple-element.28.refs_3_, ...), custom_call_target="tpu_custom_call" | custom-call | flops 603979776 | bytes 5767168 | tf_op jit(solution)/shard_map/attend_own/pallas_call | solution.py:175
  52.8 2.7 %collective-permute-done.8.refs_2_ = bf16[136,1024]{1,0:T(8,128)(2,1)S(1)} collective-permute-done((bf16[136,1024]{1,0:T(8,128)(2,1)S(1)}, bf16[136,1024]{1,0:T(8,128)(2,1)S(1)}, u32[]{:S(2)}, u32[]{:S(2)}) %collective-permute-start.8) | collective-permute-done | bytes 278560 | tf_op jit(solution)/shard_map/ppermute | solution.py:274
  55.4 1.2 %combine.2.refs_3_ = bf16[256,1024]{1,0:T(8,128)(2,1)} custom-call(f32[128,1024]{1,0:T(8,128)S(1)} %get-tuple-element.38.refs_0_, f32[16,128]{1,0:T(8,128)S(1)} %get-tuple-element.39.refs_1_, bf16[136,1024]{1,0:T(8,128)(2,1)S(1)} %collective-permute-done.8.refs_2_), custom_call_target="tpu_custom_call" | custom-call | tf_op jit(solution)/shard_map/combine/pallas_call | solution.py:254
  56.6 10.3 %collective-permute-done.9.refs_2_ = bf16[136,1024]{1,0:T(8,128)(2,1)S(1)} collective-permute-done((bf16[136,1024]{1,0:T(8,128)(2,1)S(1)}, bf16[136,1024]{1,0:T(8,128)(2,1)S(1)}, u32[]{:S(2)}, u32[]{:S(2)}) %collective-permute-start.9) | collective-permute-done | bytes 278560 | tf_op jit(solution)/shard_map/ppermute | solution.py:274
  66.9 1.2 %combine.3 = bf16[256,1024]{1,0:T(8,128)(2,1)} custom-call(f32[128,1024]{1,0:T(8,128)S(1)} %get-tuple-element.35.refs_0_, f32[16,128]{1,0:T(8,128)S(1)} %get-tuple-element.36.refs_1_, bf16[136,1024]{1,0:T(8,128)(2,1)S(1)} %collective-permute-done.9.refs_2_, bf16[256,1024]{1,0:T(8,128)(2,1)} %combine.2.refs_3_), custom_call_target="tpu_custom_call", output_to_operand_aliasing={{}: (3, {})} | custom-call | tf_op jit(solution)/shard_map/combine/pallas_call | solution.py:254
  (2 shorter events, 0.1 us)
Async XLA Ops:
  0.0 9.9 %copy-start = (bf16[256,1024]{1,0:T(8,128)(2,1)S(1)}, bf16[256,1024]{1,0:T(8,128)(2,1)}, u32[]{:S(2)}) copy-start(bf16[256,1024]{1,0:T(8,128)(2,1)} %refs_2_.1) | copy-start | bytes 1572868
  0.0 6.3 %collective-permute-start = (s32[4,4,1,27]{3,2,1,0:T(1,128)}, s32[4,4,1,27]{3,2,1,0:T(1,128)S(1)}, u32[]{:S(2)}, u32[]{:S(2)}) collective-permute-start(s32[4,4,1,27]{3,2,1,0:T(1,128)} %param.7), channel_id=1, source_target_pairs={{0,8},{1,9},{2,10},{3,11},{4,12},{5,13},{6,14},{7,15},{8,0},{9,1},... | collective-permute-start | bytes 5192 | tf_op jit(solution)/shard_map/ppermute | solution.py:274
  4.0 1.0 %copy-start.1 = (bf16[256,1024]{1,0:T(8,128)(2,1)S(1)}, bf16[256,1024]{1,0:T(8,128)(2,1)}, u32[]{:S(2)}) copy-start(bf16[256,1024]{1,0:T(8,128)(2,1)} %key.1) | copy-start | bytes 1572868
  5.1 1.0 %copy-start.2 = (bf16[256,1024]{1,0:T(8,128)(2,1)S(1)}, bf16[256,1024]{1,0:T(8,128)(2,1)}, u32[]{:S(2)}) copy-start(bf16[256,1024]{1,0:T(8,128)(2,1)} %value.1) | copy-start | bytes 1572868
  6.1 6.3 %copy-start.3 = (s32[4,4,1,27]{3,2,1,0:T(1,128)S(1)}, s32[4,4,1,27]{3,2,1,0:T(1,128)}, u32[]{:S(2)}) copy-start(s32[4,4,1,27]{3,2,1,0:T(1,128)} %param.7) | copy-start | bytes 5188
  6.3 11.4 %collective-permute-start.3 = (bf16[512,1024]{1,0:T(8,128)(2,1)S(1)}, bf16[512,1024]{1,0:T(8,128)(2,1)S(1)}, u32[]{:S(2)}, u32[]{:S(2)}) collective-permute-start(bf16[512,1024]{1,0:T(8,128)(2,1)S(1)} %get-tuple-element.28.refs_3_), channel_id=1, source_target_pairs={{2,1},{4,3},{6,5},{10,9},{12,11},{14,13},{1,2},{3,4},{5,6},{9,10},... | collective-permute-start | bytes 3145736 | tf_op jit(solution)/shard_map/ppermute | solution.py:274
  7.1 29.0 %collective-permute-start.2 = (bf16[512,1024]{1,0:T(8,128)(2,1)S(1)}, bf16[512,1024]{1,0:T(8,128)(2,1)S(1)}, u32[]{:S(2)}, u32[]{:S(2)}) collective-permute-start(bf16[512,1024]{1,0:T(8,128)(2,1)S(1)} %get-tuple-element.28.refs_3_), channel_id=1, source_target_pairs={{0,1},{1,0},{2,3},{3,2},{4,5},{5,4},{6,7},{7,6},{8,9},{9,8},{10,11... | collective-permute-start | bytes 3145736 | tf_op jit(solution)/shard_map/ppermute | solution.py:274
  9.9 26.1 %collective-permute-start.5 = (bf16[256,1024]{1,0:T(8,128)(2,1)S(1)}, bf16[256,1024]{1,0:T(8,128)(2,1)S(1)}, u32[]{:S(2)}, u32[]{:S(2)}) collective-permute-start(bf16[256,1024]{1,0:T(8,128)(2,1)S(1)} %copy-done), channel_id=1, source_target_pairs={{0,8},{1,9},{2,10},{3,11},{4,12},{5,13},{6,14},{7,15},{8,0},{9,1},... | collective-permute-start | bytes 1572872 | tf_op jit(solution)/shard_map/ppermute | solution.py:274
  12.4 3.8 %collective-permute-start.1 = (s32[8,4,1,27]{3,2,1,0:T(1,128)S(1)}, s32[8,4,1,27]{3,2,1,0:T(1,128)S(1)}, u32[]{:S(2)}, u32[]{:S(2)}) collective-permute-start(s32[8,4,1,27]{3,2,1,0:T(1,128)S(1)} %pad_add_fusion.refs_0_), channel_id=1, source_target_pairs={{0,16},{16,0},{1,17},{17,1},{2,18},{18,2},{3,19},{19,3},{4,20},{20... | collective-permute-start | bytes 10376 | tf_op jit(solution)/shard_map/ppermute | solution.py:281
  16.2 22.7 %collective-permute-start.4 = (bf16[256,1024]{1,0:T(8,128)(2,1)S(1)}, bf16[256,1024]{1,0:T(8,128)(2,1)S(1)}, u32[]{:S(2)}, u32[]{:S(2)}) collective-permute-start(bf16[256,1024]{1,0:T(8,128)(2,1)S(1)} %get-tuple-element.29), channel_id=1, source_target_pairs={{0,16},{16,0},{1,17},{17,1},{2,18},{18,2},{3,19},{19,3},{4,20},{20... | collective-permute-start | bytes 1572872 | tf_op jit(solution)/shard_map/ppermute | solution.py:281
  17.8 21.9 %collective-permute-start.7 = (bf16[256,1024]{1,0:T(8,128)(2,1)S(1)}, bf16[256,1024]{1,0:T(8,128)(2,1)S(1)}, u32[]{:S(2)}, u32[]{:S(2)}) collective-permute-start(bf16[256,1024]{1,0:T(8,128)(2,1)S(1)} %slice.4), channel_id=1, source_target_pairs={{0,16},{16,0},{1,17},{17,1},{2,18},{18,2},{3,19},{19,3},{4,20},{20... | collective-permute-start | bytes 1572872 | tf_op jit(solution)/shard_map/ppermute | solution.py:281
  38.9 2.0 %collective-permute-start.6 = (bf16[256,1024]{1,0:T(8,128)(2,1)S(1)}, bf16[256,1024]{1,0:T(8,128)(2,1)S(1)}, u32[]{:S(2)}, u32[]{:S(2)}) collective-permute-start(bf16[256,1024]{1,0:T(8,128)(2,1)S(1)} %collective-permute-done.4.refs_6_), channel_id=1, source_target_pairs={{0,1},{1,0},{2,3},{3,2},{4,5},{5,4},{6,7},{7,6},{8,9},{9,8},{10,11... | collective-permute-start | bytes 1572872 | tf_op jit(solution)/shard_map/ppermute | solution.py:274
  39.0 16.4 %collective-permute-start.8 = (bf16[136,1024]{1,0:T(8,128)(2,1)S(1)}, bf16[136,1024]{1,0:T(8,128)(2,1)S(1)}, u32[]{:S(2)}, u32[]{:S(2)}) collective-permute-start(bf16[136,1024]{1,0:T(8,128)(2,1)S(1)} %attend_beside.2.refs_9_), channel_id=1, source_target_pairs={{0,8},{1,9},{2,10},{3,11},{4,12},{5,13},{6,14},{7,15},{8,0},{9,1},... | collective-permute-start | bytes 835592 | tf_op jit(solution)/shard_map/ppermute | solution.py:274
  44.8 22.1 %collective-permute-start.9 = (bf16[136,1024]{1,0:T(8,128)(2,1)S(1)}, bf16[136,1024]{1,0:T(8,128)(2,1)S(1)}, u32[]{:S(2)}, u32[]{:S(2)}) collective-permute-start(bf16[136,1024]{1,0:T(8,128)(2,1)S(1)} %attend_beside.3), channel_id=1, source_target_pairs={{0,8},{1,9},{2,10},{3,11},{4,12},{5,13},{6,14},{7,15},{8,0},{9,1},... | collective-permute-start | bytes 835592 | tf_op jit(solution)/shard_map/ppermute | solution.py:274

commit v3 on v2

v3 whole, which is shorter than its diff:
```python
import functools

import jax
import jax.numpy as jnp
from jax import lax
from jax.experimental import pallas as pl
from jax.experimental.pallas import tpu as pltpu
from jax.sharding import PartitionSpec as P

HD = 128
HEADS = 8
TILE = 128
TW = 8
NEAR = 27
STEP = 4
COL = STEP * HD
C2 = HD ** (-0.5) * 1.4426950408889634
NONE = -1e30
STAT_ROWS = 8
TERMS = 3
VMEM = 20 * 2**20

ANYWHERE = pl.BlockSpec(memory_space=pl.ANY)
IN_SMEM = pl.BlockSpec(memory_space=pltpu.SMEM)
IN_VMEM = pl.BlockSpec(memory_space=pltpu.VMEM)


def is_small():
    return lax.axis_size("uly") == 2 and lax.axis_size("blk") == 2 * TW


def frame_of(at):
    if is_small():
        g = lax.axis_index("uly")
        return 1 - g if at == 0 else g
    return at


def slots_of(at):
    if is_small():
        outward = 1 - 2 * lax.axis_index("uly")
        return ((0, 0), (1, -outward), (2, outward)) if at == 0 else ((0, outward), (1, 0))
    return ((0, 0), (1, 1), (2, -1)) if at == 0 else ((0, -1), (1, 0), (3, 1))


def rows_of(at):
    return pl.ds(pl.multiple_of(frame_of(at) * TILE, TILE), TILE)


def pack_kernel(key, value, both, border, inner, sems):
    loads = {}
    for row, (at, half, source) in enumerate(((1, 0, key), (0, 0, key), (0, 1, value), (1, 1, value))):
        to = both.at[pl.ds(row * TILE, TILE)]
        loads[at, half] = pltpu.make_async_copy(source.at[rows_of(at)], to, sems.at[row])
    for at in range(2):
        for half in range(2):
            loads[at, half].start()
    for half in range(2):
        loads[0, half].wait()
    border[...] = both[TILE : 3 * TILE]
    for half in range(2):
        loads[1, half].wait()
    inner[:TILE] = both[:TILE]
    inner[TILE:] = both[3 * TILE :]


def pack(key, value):
    def rows(tiles):
        return jax.ShapeDtypeStruct((tiles * TILE, HEADS * HD), key.dtype)

    return pl.pallas_call(
        pack_kernel,
        out_shape=(rows(4), rows(2), rows(2)),
        in_specs=[pl.BlockSpec(memory_space=pltpu.HBM)] * 2,
        out_specs=(IN_VMEM,) * 3,
        scratch_shapes=[pltpu.SemaphoreType.DMA((4,))],
        compiler_params=pltpu.CompilerParams(vmem_limit_bytes=VMEM),
        cost_estimate=pl.CostEstimate(flops=0, bytes_accessed=2**21, transcendentals=0),
        name="pack_kv",
    )(key, value)


def attend_kernel(at, which, height_step, places, travels, n_live, *refs):
    live, query, refs = refs[:n_live], refs[n_live], refs[n_live + 1 :]
    out, stats_out = (refs[-1], None) if travels else refs[-2:]
    g, s = lax.axis_index("uly"), lax.axis_index("blk")
    height = 2 * (s // TW) - 1 if height_step is None else height_step
    width = 1 - 2 * (s % 2)
    offsets = {
        (slot, c): 9 * (frame_step + 1) + 3 * (height + 1) + width_step + 1
        for slot, frame_step in slots_of(at)
        for c, width_step in enumerate((0, width, -width))
    }
    rows = rows_of(at)
    lane = lax.broadcasted_iota(jnp.int32, (TILE, HD), 1)

    def is_live(head, offset):
        if is_small():
            held = HEADS // 2
            place = (which * held + head % held, 2 * g + frame_of(at), 0, offset)
            return jnp.where(g == head // held, live[0][place], live[1][place]) > 0
        return live[0][head, frame_of(at), 0, offset] > 0

    cols = [slice(h * HD, (h + 1) * HD) for h in range(HEADS)]
    for step in range(HEADS // STEP):
        heads = range(step * STEP, (step + 1) * STEP)
        scores, highest = {}, {}
        for h in heads:
            q = query[rows, cols[h]]
            for block, (k_row, _, tiles) in enumerate(places):
                keys = refs[block][k_row : k_row + len(tiles) * TILE, cols[h]]
                score = lax.dot_general(
                    q, keys, (((1,), (1,)), ((), ())), preferred_element_type=jnp.float32
                )
                for i, t in enumerate(tiles):
                    part = score[:, i * TILE : (i + 1) * TILE]
                    part = part + jnp.where(is_live(h, offsets[t]), 0.0, NONE)
                    scores[h, t] = part
                    highest[h] = jnp.maximum(highest[h], part) if h in highest else part
        top = {h: jnp.max(highest[h], axis=1, keepdims=True) for h in heads}
        shift = {h: top[h] * C2 for h in heads}
        mixed, sums = {}, {}
        for h in heads:
            for block, (_, v_row, tiles) in enumerate(places):
                weights = []
                for t in reversed(tiles):
                    w = jnp.exp2(scores[h, t] * C2 - shift[h])
                    sums[h] = sums[h] + w if h in sums else w
                    weights.append(w.astype(jnp.bfloat16))
                values = refs[block][v_row : v_row + len(tiles) * TILE, cols[h]]
                o = jnp.dot(
                    weights[0] if len(weights) == 1 else jnp.concatenate(weights, axis=1),
                    values,
                    preferred_element_type=jnp.float32,
                )
                mixed[h] = mixed[h] + o if h in mixed else o
        total = {h: jnp.sum(sums[h], axis=1, keepdims=True) for h in heads}
        stats = jnp.zeros((TILE, HD), jnp.float32)
        for i, h in enumerate(heads):
            if travels:
                any_live = top[h] > 0.5 * NONE
                total[h] = jnp.where(any_live, total[h], 0.0)
                mixed[h] = mixed[h] * jnp.where(any_live, 1.0 / total[h], 0.0)
            out[:TILE, cols[h]] = mixed[h].astype(out.dtype)
            stats = jnp.where(lane == i, top[h], stats)
            stats = jnp.where(lane == STEP + i, total[h], stats)
        stats = jnp.transpose(stats)[:STAT_ROWS]
        if travels:
            for term in range(TERMS):
                rounded = stats.astype(jnp.bfloat16)
                out[TILE:, cols[heads[term]]] = rounded
                stats = stats - rounded.astype(jnp.float32)
            out[TILE:, cols[heads[TERMS]]] = jnp.zeros((STAT_ROWS, HD), jnp.bfloat16)
        else:
            stats_out[step * STAT_ROWS : (step + 1) * STAT_ROWS] = stats


def attend(at, which, height_step, live, query, both, beyond, travels, name, after):
    blocks = list(both)
    places = [(0, 2 * TILE, ((1, c), (0, c))) for c in range(2)]
    places += [(0, TILE, ((slot, 2),)) for slot in range(2)]
    for slot, _ in slots_of(at)[2:]:
        blocks += beyond[slot - 2]
        places += [(0, TILE, ((slot, c),)) for c in range(3)]
    pairs = sum(len(tiles) for _, _, tiles in places) * HEADS
    steps = HEADS // STEP
    if travels:
        out_shape = jax.ShapeDtypeStruct((TILE + STAT_ROWS, HEADS * HD), jnp.bfloat16)
    else:
        out_shape = (
            jax.ShapeDtypeStruct((TILE, HEADS * HD), jnp.float32),
            jax.ShapeDtypeStruct((steps * STAT_ROWS, HD), jnp.float32),
        )
    return pl.pallas_call(
        functools.partial(attend_kernel, at, which, height_step, places, travels, len(live)),
        out_shape=out_shape,
        in_specs=[IN_SMEM] * len(live) + [IN_VMEM] * (1 + len(blocks)) + [ANYWHERE] * len(after),
        out_specs=IN_VMEM if travels else (IN_VMEM, IN_VMEM),
        compiler_params=pltpu.CompilerParams(vmem_limit_bytes=VMEM),
        cost_estimate=pl.CostEstimate(
            flops=4 * pairs * TILE * TILE * HD,
            bytes_accessed=(pairs // HEADS + 2) * 2 * TILE * HEADS * HD * 2,
            transcendentals=pairs * TILE * TILE,
        ),
        name=name,
    )(*live, query, *blocks, *after)


def split_stats(per_step):
    tops = jnp.concatenate([stats[:STEP] for stats in per_step], axis=0)
    totals = jnp.concatenate([stats[STEP : 2 * STEP] for stats in per_step], axis=0)
    return tops, totals


def own_stats(ref):
    steps = range(HEADS // STEP)
    return split_stats([ref[step * STAT_ROWS : (step + 1) * STAT_ROWS] for step in steps])


def travelled_stats(ref):
    per_step = []
    for step in range(HEADS // STEP):
        first = step * COL
        terms = [ref[TILE:, first + HD * t : first + HD * (t + 1)] for t in range(TERMS)]
        per_step.append(sum(term.astype(jnp.float32) for term in terms))
    return split_stats(per_step)


def combine_kernel(at, n_more, *refs):
    out, made, sem = refs[-3:]
    travelled, (mine, stats) = refs[:n_more], refs[n_more : n_more + 2]
    top, total = own_stats(stats)
    more = []
    best = top
    for m in range(n_more):
        top2, total2 = travelled_stats(travelled[m])
        top2 = jnp.where(total2 > 0.0, top2, NONE)
        more.append((top2, total2))
        best = jnp.maximum(best, top2)
    own = jnp.exp2((top - best) * C2)
    weights = [own]
    whole = total * own
    for top2, total2 in more:
        w = jnp.exp2((top2 - best) * C2) * total2
        weights.append(w)
        whole = whole + w
    inverse = 1.0 / whole
    weights = [w * inverse for w in weights]
    fill = TILE - HEADS * len(weights)
    columns = jnp.transpose(
        jnp.concatenate(weights + [jnp.zeros((fill, HD), jnp.float32)], axis=0)
    )
    for h in range(HEADS):
        cols = slice(h * HD, (h + 1) * HD)
        value = mine[:, cols] * columns[:, h : h + 1]
        for m in range(n_more):
            c = (m + 1) * HEADS + h
            value = value + travelled[m][:TILE, cols].astype(jnp.float32) * columns[:, c : c + 1]
        made[:, cols] = value.astype(made.dtype)
    copy = pltpu.make_async_copy(made, out.at[rows_of(at)], sem)
    copy.start()
    copy.wait()


def combine(at, parts, n_more, into=None):
    specs = [IN_VMEM] * len(parts)
    extra, aliases = [], {}
    if into is not None:
        specs.append(ANYWHERE)
        extra, aliases = [into], {len(parts): 0}
    return pl.pallas_call(
        functools.partial(combine_kernel, at, n_more),
        out_shape=jax.ShapeDtypeStruct((2 * TILE, HEADS * HD), jnp.bfloat16),
        in_specs=specs,
        out_specs=ANYWHERE,
        scratch_shapes=[
            pltpu.VMEM((TILE, HEADS * HD), jnp.bfloat16),
            pltpu.SemaphoreType.DMA,
        ],
        input_output_aliases=aliases,
        compiler_params=pltpu.CompilerParams(vmem_limit_bytes=VMEM),
        name="combine",
    )(*parts, *extra)


def local(query, key, value, live):
    n_uly, n_blk = lax.axis_size("uly"), lax.axis_size("blk")
    high = n_blk // TW

    def blk_move(block, pairs):
        return lax.ppermute(block, "blk", pairs)

    def uly_shift(block, distance):
        pairs = [(i, i + distance) for i in range(n_uly) if 0 <= i + distance < n_uly]
        return lax.ppermute(block, "uly", pairs)

    def uly_swap(block):
        return lax.ppermute(block, "uly", [(0, 1), (1, 0)])

    def halo(first, second):
        if is_small():
            return [uly_swap(first)]
        return [uly_shift(second, 1), uly_shift(first, -1)]

    mate_pairs = [(i, i ^ 1) for i in range(n_blk)]
    outer_pairs = [(i, i - 1) for i in range(0, n_blk, 2) if i % TW > 0]
    outer_pairs += [(i, i + 1) for i in range(1, n_blk, 2) if i % TW < TW - 1]

    if high == 2:
        swap = [(i, (i + TW) % n_blk) for i in range(n_blk)]
        beside = [(swap, swap, None)]
    else:
        down = [(i, i + TW) for i in range(n_blk - TW)]
        up = [(i + TW, i) for i in range(n_blk - TW)]
        beside = [(down, up, 1), (up, down, -1)]

    key, value = (pltpu.with_memory_space_constraint(a, pltpu.HBM) for a in (key, value))
    both, border, inner = pack(key, value)
    if is_small():
        far_live = blk_move(live, beside[0][0])
        far_live, query, both, border, inner = lax.optimization_barrier(
            (far_live, query, both, border, inner)
        )
        held = ((0, len(live), 0), (0, 0, 0), (0, 0, 0), (0, 0, 0))
        below = ((len(live), 0, 0), (0, 0, 0), (0, 0, 0), (0, 0, 0))
        live = lax.pad(live, 0, held) + lax.pad(far_live, 0, below)
        other_live = uly_swap(live)
        other_first = border
        border, other_live = lax.optimization_barrier((border, other_live))
        own_live, far_live = [live, other_live], [[live, other_live]]
    else:
        other_first = border
        own_live = [lax.all_to_all(live, "uly", split_axis=1, concat_axis=0, tiled=True)]
        far_live = [[blk_move(own_live[0], there)] for there, _, _ in beside]
    far_queries = [blk_move(query, there) for there, _, _ in beside]
    other_border = blk_move(other_first, outer_pairs)
    other_inner = blk_move(inner, outer_pairs)
    mate = blk_move(both, mate_pairs)
    own_halo = halo(border, inner)
    if is_small():
        token = blk_move(other_border[:TILE], mate_pairs)
        other_border, token = lax.optimization_barrier((other_border, token))
    other_halo = halo(other_border, other_inner)

    def attend_beside(at, after):
        return [
            attend(at, 1, height_step, masks, block, blocks, beyond, True, "attend_beside", after)
            for block, masks, (_, _, height_step) in zip(far_queries, far_live, beside)
        ]

    blocks, beyond = (both, mate, other_border, other_inner), []
    made = [None, None]
    after = []
    if is_small():
        made[1] = attend_beside(1, [])
        own_halo, after = lax.optimization_barrier((own_halo, made[1]))
        after = after + [token]
    mate_halo = [blk_move(block, mate_pairs) for block in own_halo]
    beyond += [list(halos) for halos in zip(own_halo, mate_halo, other_halo)]
    if not is_small():
        made[1] = attend_beside(1, [])
    made[0] = attend_beside(0, after)
    returned = [
        [blk_move(part, back) for part, (_, back, _) in zip(made[at], beside)] for at in range(2)
    ]
    own = [
        attend(at, 0, 0, own_live, query, blocks, beyond, False, "attend_own", [])
        for at in range(2)
    ]
    returned[1], own = lax.optimization_barrier((returned[1], own))
    out = None
    for at in (1, 0):
        out = combine(at, returned[at] + list(own[at]), len(beside), out)
    return out


def solution(mesh):
    return jax.shard_map(
        local,
        mesh=mesh,
        in_specs=(
            P(("uly", "blk"), None),
            P(("uly", "blk"), None),
            P(("uly", "blk"), None),
            P("uly", None, "blk", None),
        ),
        out_specs=P(("uly", "blk"), None),
        check_vma=False,
    )
```

time: 68.3 us -> 65.4 us (0.958)
  waiting for transfers between devices: 34.1 us -> 28.6 us
  starting transfers between devices: 15.6 us -> 19.5 us
  local copies, waits for them, and re-layouts: 2.12 us -> 0.03 us
    ppermute x7 -> x9, waiting for transfers between devices: 31.9 us -> 25.4 us  [blk_move(): return lax.ppermute(block, 'blk', pairs)]
    ppermute x7 -> x9, starting transfers between devices: 11.9 us -> 15.7 us  [blk_move(): return lax.ppermute(block, 'blk', pairs)]
    unnamed x8 -> x4, local copies, waits for them, and re-layouts: 2.09 us -> 0.01 us
    pallas_call x1, Pallas kernels: 0.17 us -> 1.27 us  [pack(): pl.pallas_call(pack_kernel, out_shape=(rows(4), rows(2), rows(2)), in_spe...]
    ppermute x3, waiting for transfers between devices: 2.22 us -> 3.24 us  [uly_swap(): return lax.ppermute(block, 'uly', [(0, 1), (1, 0)])]
  transfers between devices with their start and end apart: 10 -> 12, of which waited for: 5 -> 8; matrix products, arithmetic and copies ran while one was open for 0% -> 0% of each run, Pallas kernels for 22% -> 24%
where the time goes in v3:
time: 65.4 us; the launch traced here: 65 us
  waiting for transfers between devices  28.6 us (44%)
  starting transfers between devices  19.5 us (30%)
  Pallas kernels  16.7 us (26%)
    ppermute x9, waiting for transfers between devices, blk_move(): return lax.ppermute(block, 'blk', pairs)  25.4 us
    ppermute x9, starting transfers between devices, blk_move(): return lax.ppermute(block, 'blk', pairs)  15.7 us
    pallas_call x4, Pallas kernels, attend(): pl.pallas_call(functools.partial(attend_kernel, at, which, height_step, p...  13 us
    ppermute x3, starting transfers between devices, uly_swap(): return lax.ppermute(block, 'uly', [(0, 1), (1, 0)])  3.79 us
    ppermute x3, waiting for transfers between devices, uly_swap(): return lax.ppermute(block, 'uly', [(0, 1), (1, 0)])  3.24 us
    pallas_call x2, Pallas kernels, combine(): pl.pallas_call(functools.partial(combine_kernel, at, n_more), out_shape=j...  2.43 us
  transfers between devices with their start and end apart: 12, of which 8 were waited for; matrix products, arithmetic and copies ran while one was open for 0% of the time, Pallas kernels for 24%

profile of v3, /device:TPU:0, one launch (start us, length us, event | category | flops | bytes accessed | tf_op | source)
XLA Modules:
  0.0 65.0 jit_solution(15031943667415832460)
XLA Ops:
  0.0 0.0 copy-start
  0.0 4.0 %collective-permute-start = (s32[4,4,1,27]{3,2,1,0:T(1,128)}, s32[4,4,1,27]{3,2,1,0:T(1,128)S(1)}, u32[]{:S(2)}, u32[]{:S(2)}) collective-permute-start(s32[4,4,1,27]{3,2,1,0:T(1,128)} %param.7), channel_id=1, source_target_pairs={{0,8},{1,9},{2,10},{3,11},{4,12},{5,13},{6,14},{7,15},{8,0},{9,1},... | collective-permute-start | bytes 5192 | tf_op jit(solution)/shard_map/ppermute | solution.py:271
  4.0 0.0 copy-start.1
  4.0 1.3 %pack_kv.1 = (bf16[512,1024]{1,0:T(8,128)(2,1)S(1)}, bf16[256,1024]{1,0:T(8,128)(2,1)S(1)}, bf16[256,1024]{1,0:T(8,128)(2,1)S(1)}) custom-call(bf16[256,1024]{1,0:T(8,128)(2,1)} %key.1, bf16[256,1024]{1,0:T(8,128)(2,1)} %value.1), custom_call_target="tpu_custom_call" | custom-call | bytes 2097152 | tf_op jit(solution)/shard_map/pack_kv/pallas_call | solution.py:71
  5.3 0.6 collective-permute-done
  5.9 0.0 collective-permute-start.3
  5.9 0.7 %collective-permute-start.4 = (bf16[256,1024]{1,0:T(8,128)(2,1)S(1)}, bf16[256,1024]{1,0:T(8,128)(2,1)S(1)}, u32[]{:S(2)}, u32[]{:S(2)}) collective-permute-start(bf16[256,1024]{1,0:T(8,128)(2,1)S(1)} %get-tuple-element.38), channel_id=1, source_target_pairs={{2,1},{4,3},{6,5},{10,9},{12,11},{14,13},{1,2},{3,4},{5,6},{9,10},... | collective-permute-start | bytes 1572872 | tf_op jit(solution)/shard_map/ppermute | solution.py:271
  6.6 0.0 copy-done
  6.6 3.0 %collective-permute-start.2 = (bf16[256,1024]{1,0:T(8,128)(2,1)S(1)}, bf16[256,1024]{1,0:T(8,128)(2,1)S(1)}, u32[]{:S(2)}, u32[]{:S(2)}) collective-permute-start(bf16[256,1024]{1,0:T(8,128)(2,1)S(1)} %copy-done), channel_id=1, source_target_pairs={{0,8},{1,9},{2,10},{3,11},{4,12},{5,13},{6,14},{7,15},{8,0},{9,1},... | collective-permute-start | bytes 1572872 | tf_op jit(solution)/shard_map/ppermute | solution.py:271
  9.6 0.7 %collective-permute-start.6 = (bf16[256,1024]{1,0:T(8,128)(2,1)S(1)}, bf16[256,1024]{1,0:T(8,128)(2,1)S(1)}, u32[]{:S(2)}, u32[]{:S(2)}) collective-permute-start(bf16[256,1024]{1,0:T(8,128)(2,1)S(1)} %get-tuple-element.37), channel_id=1, source_target_pairs={{2,1},{4,3},{6,5},{10,9},{12,11},{14,13},{1,2},{3,4},{5,6},{9,10},... | collective-permute-start | bytes 1572872 | tf_op jit(solution)/shard_map/ppermute | solution.py:271
  10.3 0.0 copy-done.1
  10.3 1.6 %collective-permute-start.1 = (s32[8,4,1,27]{3,2,1,0:T(1,128)S(1)}, s32[8,4,1,27]{3,2,1,0:T(1,128)S(1)}, u32[]{:S(2)}, u32[]{:S(2)}) collective-permute-start(s32[8,4,1,27]{3,2,1,0:T(1,128)S(1)} %pad_add_fusion.refs_0_), channel_id=1, source_target_pairs={{0,16},{16,0},{1,17},{17,1},{2,18},{18,2},{3,19},{19,3},{4,20},{20... | collective-permute-start | bytes 10376 | tf_op jit(solution)/shard_map/ppermute | solution.py:278
  11.9 2.2 %collective-permute-done.1.refs_1_ = s32[8,4,1,27]{3,2,1,0:T(1,128)S(1)} collective-permute-done((s32[8,4,1,27]{3,2,1,0:T(1,128)S(1)}, s32[8,4,1,27]{3,2,1,0:T(1,128)S(1)}, u32[]{:S(2)}, u32[]{:S(2)}) %collective-permute-start.1) | collective-permute-done | bytes 3488 | tf_op jit(solution)/shard_map/ppermute | solution.py:278
  14.1 1.5 %collective-permute-start.7 = (bf16[256,1024]{1,0:T(8,128)(2,1)S(1)}, bf16[256,1024]{1,0:T(8,128)(2,1)S(1)}, u32[]{:S(2)}, u32[]{:S(2)}) collective-permute-start(bf16[256,1024]{1,0:T(8,128)(2,1)S(1)} %get-tuple-element.38), channel_id=1, source_target_pairs={{0,16},{16,0},{1,17},{17,1},{2,18},{18,2},{3,19},{19,3},{4,20},{20... | collective-permute-start | bytes 1572872 | tf_op jit(solution)/shard_map/ppermute | solution.py:278
  15.6 0.0 collective-permute-done.4.refs_5_
  15.6 3.8 %collective-permute-start.5 = (bf16[128,1024]{1,0:T(8,128)(2,1)S(1)}, bf16[128,1024]{1,0:T(8,128)(2,1)S(1)}, u32[]{:S(2)}, u32[]{:S(2)}) collective-permute-start(bf16[128,1024]{1,0:T(8,128)(2,1)S(1)} %slice.4), channel_id=1, source_target_pairs={{0,1},{1,0},{2,3},{3,2},{4,5},{5,4},{6,7},{7,6},{8,9},{9,8},{10,11... | collective-permute-start | bytes 786440 | tf_op jit(solution)/shard_map/ppermute | solution.py:271
  19.4 1.2 %collective-permute-done.5.refs_11_ = bf16[128,1024]{1,0:T(8,128)(2,1)S(1)} collective-permute-done((bf16[128,1024]{1,0:T(8,128)(2,1)S(1)}, bf16[128,1024]{1,0:T(8,128)(2,1)S(1)}, u32[]{:S(2)}, u32[]{:S(2)}) %collective-permute-start.5) | collective-permute-done | bytes 262176 | tf_op jit(solution)/shard_map/ppermute | solution.py:271
  20.6 0.7 %collective-permute-start.9 = (bf16[256,1024]{1,0:T(8,128)(2,1)S(1)}, bf16[256,1024]{1,0:T(8,128)(2,1)S(1)}, u32[]{:S(2)}, u32[]{:S(2)}) collective-permute-start(bf16[256,1024]{1,0:T(8,128)(2,1)S(1)} %collective-permute-done.4.refs_5_), channel_id=1, source_target_pairs={{0,16},{16,0},{1,17},{17,1},{2,18},{18,2},{3,19},{19,3},{4,20},{20... | collective-permute-start | bytes 1572872 | tf_op jit(solution)/shard_map/ppermute | solution.py:278
  21.2 10.1 %collective-permute-done.2.refs_2_ = bf16[256,1024]{1,0:T(8,128)(2,1)S(1)} collective-permute-done((bf16[256,1024]{1,0:T(8,128)(2,1)S(1)}, bf16[256,1024]{1,0:T(8,128)(2,1)S(1)}, u32[]{:S(2)}, u32[]{:S(2)}) %collective-permute-start.2) | collective-permute-done | bytes 524320 | tf_op jit(solution)/shard_map/ppermute | solution.py:271
  31.3 0.0 collective-permute-done.6.refs_6_
  31.3 0.0 collective-permute-done.3.refs_4_
  31.4 2.9 %attend_beside.2.refs_10_ = bf16[136,1024]{1,0:T(8,128)(2,1)S(1)} custom-call(s32[8,4,1,27]{3,2,1,0:T(1,128)S(1)} %pad_add_fusion.refs_0_, s32[8,4,1,27]{3,2,1,0:T(1,128)S(1)} %collective-permute-done.1.refs_1_, bf16[256,1024]{1,0:T(8,128)(2,1)S(1)} %collective-permute-done.2.refs_2_, bf16[512,1024]{1,0:T(8,128)(2,1)S(1)} %get-tuple-element.35.refs_3_, ...), custom_call_target="tpu_custom_call" | custom-call | flops 402653184 | bytes 4194304 | tf_op jit(solution)/shard_map/attend_beside/pallas_call | solution.py:174
  34.2 0.0 collective-permute-done.7.refs_7_
  34.2 2.1 %collective-permute-start.8 = (bf16[256,1024]{1,0:T(8,128)(2,1)S(1)}, bf16[256,1024]{1,0:T(8,128)(2,1)S(1)}, u32[]{:S(2)}, u32[]{:S(2)}) collective-permute-start(bf16[256,1024]{1,0:T(8,128)(2,1)S(1)} %collective-permute-done.7.refs_7_), channel_id=1, source_target_pairs={{0,1},{1,0},{2,3},{3,2},{4,5},{5,4},{6,7},{7,6},{8,9},{9,8},{10,11... | collective-permute-start | bytes 1572872 | tf_op jit(solution)/shard_map/ppermute | solution.py:271
  36.3 0.0 collective-permute-start.11
  36.3 1.0 %collective-permute-done.9.refs_9_ = bf16[256,1024]{1,0:T(8,128)(2,1)S(1)} collective-permute-done((bf16[256,1024]{1,0:T(8,128)(2,1)S(1)}, bf16[256,1024]{1,0:T(8,128)(2,1)S(1)}, u32[]{:S(2)}, u32[]{:S(2)}) %collective-permute-start.9) | collective-permute-done | bytes 524320 | tf_op jit(solution)/shard_map/ppermute | solution.py:278
  37.4 0.5 collective-permute-done.8.refs_8_
  37.9 3.7 %attend_beside.3 = bf16[136,1024]{1,0:T(8,128)(2,1)S(1)} custom-call(s32[8,4,1,27]{3,2,1,0:T(1,128)S(1)} %pad_add_fusion.refs_0_, s32[8,4,1,27]{3,2,1,0:T(1,128)S(1)} %collective-permute-done.1.refs_1_, bf16[256,1024]{1,0:T(8,128)(2,1)S(1)} %collective-permute-done.2.refs_2_, bf16[512,1024]{1,0:T(8,128)(2,1)S(1)} %get-tuple-element.35.refs_3_, ...), custom_call_target="tpu_custom_call" | custom-call | flops 603979776 | bytes 5767168 | tf_op jit(solution)/shard_map/attend_beside/pallas_call | solution.py:174
  41.6 1.5 %collective-permute-start.10 = (bf16[136,1024]{1,0:T(8,128)(2,1)S(1)}, bf16[136,1024]{1,0:T(8,128)(2,1)S(1)}, u32[]{:S(2)}, u32[]{:S(2)}) collective-permute-start(bf16[136,1024]{1,0:T(8,128)(2,1)S(1)} %attend_beside.3), channel_id=1, source_target_pairs={{0,8},{1,9},{2,10},{3,11},{4,12},{5,13},{6,14},{7,15},{8,0},{9,1},... | collective-permute-start | bytes 835592 | tf_op jit(solution)/shard_map/ppermute | solution.py:271
  43.1 2.8 %attend_own.3 = (f32[128,1024]{1,0:T(8,128)S(1)}, f32[16,128]{1,0:T(8,128)S(1)}) custom-call(s32[8,4,1,27]{3,2,1,0:T(1,128)S(1)} %pad_add_fusion.refs_0_, s32[8,4,1,27]{3,2,1,0:T(1,128)S(1)} %collective-permute-done.1.refs_1_, bf16[256,1024]{1,0:T(8,128)(2,1)S(1)} %copy-done, bf16[512,1024]{1,0:T(8,128)(2,1)S(1)} %get-tuple-element.35.refs_3_, ...), custom_call_target="tpu_custom_call" | custom-call | flops 402653184 | bytes 4194304 | tf_op jit(solution)/shard_map/attend_own/pallas_call | solution.py:174
  45.9 3.6 %attend_own.2 = (f32[128,1024]{1,0:T(8,128)S(1)}, f32[16,128]{1,0:T(8,128)S(1)}) custom-call(s32[8,4,1,27]{3,2,1,0:T(1,128)S(1)} %pad_add_fusion.refs_0_, s32[8,4,1,27]{3,2,1,0:T(1,128)S(1)} %collective-permute-done.1.refs_1_, bf16[256,1024]{1,0:T(8,128)(2,1)S(1)} %copy-done, bf16[512,1024]{1,0:T(8,128)(2,1)S(1)} %get-tuple-element.35.refs_3_, ...), custom_call_target="tpu_custom_call" | custom-call | flops 603979776 | bytes 5767168 | tf_op jit(solution)/shard_map/attend_own/pallas_call | solution.py:174
  49.5 9.2 %collective-permute-done.11.refs_0_ = bf16[136,1024]{1,0:T(8,128)(2,1)S(1)} collective-permute-done((bf16[136,1024]{1,0:T(8,128)(2,1)S(1)}, bf16[136,1024]{1,0:T(8,128)(2,1)S(1)}, u32[]{:S(2)}, u32[]{:S(2)}) %collective-permute-start.11) | collective-permute-done | bytes 278560 | tf_op jit(solution)/shard_map/ppermute | solution.py:271
  58.7 1.2 %combine.2.refs_3_ = bf16[256,1024]{1,0:T(8,128)(2,1)} custom-call(bf16[136,1024]{1,0:T(8,128)(2,1)S(1)} %collective-permute-done.11.refs_0_, f32[128,1024]{1,0:T(8,128)S(1)} %get-tuple-element.49.refs_1_, f32[16,128]{1,0:T(8,128)S(1)} %get-tuple-element.50.refs_2_), custom_call_target="tpu_custom_call" | custom-call | tf_op jit(solution)/shard_map/combine/pallas_call | solution.py:251
  59.9 3.9 %collective-permute-done.10.refs_0_ = bf16[136,1024]{1,0:T(8,128)(2,1)S(1)} collective-permute-done((bf16[136,1024]{1,0:T(8,128)(2,1)S(1)}, bf16[136,1024]{1,0:T(8,128)(2,1)S(1)}, u32[]{:S(2)}, u32[]{:S(2)}) %collective-permute-start.10) | collective-permute-done | bytes 278560 | tf_op jit(solution)/shard_map/ppermute | solution.py:271
  63.8 1.2 %combine.3 = bf16[256,1024]{1,0:T(8,128)(2,1)} custom-call(bf16[136,1024]{1,0:T(8,128)(2,1)S(1)} %collective-permute-done.10.refs_0_, f32[128,1024]{1,0:T(8,128)S(1)} %get-tuple-element.46.refs_1_, f32[16,128]{1,0:T(8,128)S(1)} %get-tuple-element.47.refs_2_, bf16[256,1024]{1,0:T(8,128)(2,1)} %combine.2.refs_3_), custom_call_target="tpu_custom_call", output_to_operand_aliasing={{}: (3, {})} | custom-call | tf_op jit(solution)/shard_map/combine/pallas_call | solution.py:251
  (2 shorter events, 0.0 us)
Async XLA Ops:
  0.0 6.6 %copy-start = (bf16[256,1024]{1,0:T(8,128)(2,1)S(1)}, bf16[256,1024]{1,0:T(8,128)(2,1)}, u32[]{:S(2)}) copy-start(bf16[256,1024]{1,0:T(8,128)(2,1)} %refs_2_.1) | copy-start | bytes 1572868
  0.0 5.9 %collective-permute-start = (s32[4,4,1,27]{3,2,1,0:T(1,128)}, s32[4,4,1,27]{3,2,1,0:T(1,128)S(1)}, u32[]{:S(2)}, u32[]{:S(2)}) collective-permute-start(s32[4,4,1,27]{3,2,1,0:T(1,128)} %param.7), channel_id=1, source_target_pairs={{0,8},{1,9},{2,10},{3,11},{4,12},{5,13},{6,14},{7,15},{8,0},{9,1},... | collective-permute-start | bytes 5192 | tf_op jit(solution)/shard_map/ppermute | solution.py:271
  4.0 6.2 %copy-start.1 = (s32[4,4,1,27]{3,2,1,0:T(1,128)S(1)}, s32[4,4,1,27]{3,2,1,0:T(1,128)}, u32[]{:S(2)}) copy-start(s32[4,4,1,27]{3,2,1,0:T(1,128)} %param.7) | copy-start | bytes 5188
  5.9 25.5 %collective-permute-start.3 = (bf16[512,1024]{1,0:T(8,128)(2,1)S(1)}, bf16[512,1024]{1,0:T(8,128)(2,1)S(1)}, u32[]{:S(2)}, u32[]{:S(2)}) collective-permute-start(bf16[512,1024]{1,0:T(8,128)(2,1)S(1)} %get-tuple-element.35.refs_3_), channel_id=1, source_target_pairs={{0,1},{1,0},{2,3},{3,2},{4,5},{5,4},{6,7},{7,6},{8,9},{9,8},{10,11... | collective-permute-start | bytes 3145736 | tf_op jit(solution)/shard_map/ppermute | solution.py:271
  5.9 9.7 %collective-permute-start.4 = (bf16[256,1024]{1,0:T(8,128)(2,1)S(1)}, bf16[256,1024]{1,0:T(8,128)(2,1)S(1)}, u32[]{:S(2)}, u32[]{:S(2)}) collective-permute-start(bf16[256,1024]{1,0:T(8,128)(2,1)S(1)} %get-tuple-element.38), channel_id=1, source_target_pairs={{2,1},{4,3},{6,5},{10,9},{12,11},{14,13},{1,2},{3,4},{5,6},{9,10},... | collective-permute-start | bytes 1572872 | tf_op jit(solution)/shard_map/ppermute | solution.py:271
  6.6 24.8 %collective-permute-start.2 = (bf16[256,1024]{1,0:T(8,128)(2,1)S(1)}, bf16[256,1024]{1,0:T(8,128)(2,1)S(1)}, u32[]{:S(2)}, u32[]{:S(2)}) collective-permute-start(bf16[256,1024]{1,0:T(8,128)(2,1)S(1)} %copy-done), channel_id=1, source_target_pairs={{0,8},{1,9},{2,10},{3,11},{4,12},{5,13},{6,14},{7,15},{8,0},{9,1},... | collective-permute-start | bytes 1572872 | tf_op jit(solution)/shard_map/ppermute | solution.py:271
  9.6 21.8 %collective-permute-start.6 = (bf16[256,1024]{1,0:T(8,128)(2,1)S(1)}, bf16[256,1024]{1,0:T(8,128)(2,1)S(1)}, u32[]{:S(2)}, u32[]{:S(2)}) collective-permute-start(bf16[256,1024]{1,0:T(8,128)(2,1)S(1)} %get-tuple-element.37), channel_id=1, source_target_pairs={{2,1},{4,3},{6,5},{10,9},{12,11},{14,13},{1,2},{3,4},{5,6},{9,10},... | collective-permute-start | bytes 1572872 | tf_op jit(solution)/shard_map/ppermute | solution.py:271
  10.3 3.8 %collective-permute-start.1 = (s32[8,4,1,27]{3,2,1,0:T(1,128)S(1)}, s32[8,4,1,27]{3,2,1,0:T(1,128)S(1)}, u32[]{:S(2)}, u32[]{:S(2)}) collective-permute-start(s32[8,4,1,27]{3,2,1,0:T(1,128)S(1)} %pad_add_fusion.refs_0_), channel_id=1, source_target_pairs={{0,16},{16,0},{1,17},{17,1},{2,18},{18,2},{3,19},{19,3},{4,20},{20... | collective-permute-start | bytes 10376 | tf_op jit(solution)/shard_map/ppermute | solution.py:278
  14.1 20.1 %collective-permute-start.7 = (bf16[256,1024]{1,0:T(8,128)(2,1)S(1)}, bf16[256,1024]{1,0:T(8,128)(2,1)S(1)}, u32[]{:S(2)}, u32[]{:S(2)}) collective-permute-start(bf16[256,1024]{1,0:T(8,128)(2,1)S(1)} %get-tuple-element.38), channel_id=1, source_target_pairs={{0,16},{16,0},{1,17},{17,1},{2,18},{18,2},{3,19},{19,3},{4,20},{20... | collective-permute-start | bytes 1572872 | tf_op jit(solution)/shard_map/ppermute | solution.py:278
  15.6 4.9 %collective-permute-start.5 = (bf16[128,1024]{1,0:T(8,128)(2,1)S(1)}, bf16[128,1024]{1,0:T(8,128)(2,1)S(1)}, u32[]{:S(2)}, u32[]{:S(2)}) collective-permute-start(bf16[128,1024]{1,0:T(8,128)(2,1)S(1)} %slice.4), channel_id=1, source_target_pairs={{0,1},{1,0},{2,3},{3,2},{4,5},{5,4},{6,7},{7,6},{8,9},{9,8},{10,11... | collective-permute-start | bytes 786440 | tf_op jit(solution)/shard_map/ppermute | solution.py:271
  20.6 16.8 %collective-permute-start.9 = (bf16[256,1024]{1,0:T(8,128)(2,1)S(1)}, bf16[256,1024]{1,0:T(8,128)(2,1)S(1)}, u32[]{:S(2)}, u32[]{:S(2)}) collective-permute-start(bf16[256,1024]{1,0:T(8,128)(2,1)S(1)} %collective-permute-done.4.refs_5_), channel_id=1, source_target_pairs={{0,16},{16,0},{1,17},{17,1},{2,18},{18,2},{3,19},{19,3},{4,20},{20... | collective-permute-start | bytes 1572872 | tf_op jit(solution)/shard_map/ppermute | solution.py:278
  34.2 3.7 %collective-permute-start.8 = (bf16[256,1024]{1,0:T(8,128)(2,1)S(1)}, bf16[256,1024]{1,0:T(8,128)(2,1)S(1)}, u32[]{:S(2)}, u32[]{:S(2)}) collective-permute-start(bf16[256,1024]{1,0:T(8,128)(2,1)S(1)} %collective-permute-done.7.refs_7_), channel_id=1, source_target_pairs={{0,1},{1,0},{2,3},{3,2},{4,5},{5,4},{6,7},{7,6},{8,9},{9,8},{10,11... | collective-permute-start | bytes 1572872 | tf_op jit(solution)/shard_map/ppermute | solution.py:271
  36.3 22.3 %collective-permute-start.11 = (bf16[136,1024]{1,0:T(8,128)(2,1)S(1)}, bf16[136,1024]{1,0:T(8,128)(2,1)S(1)}, u32[]{:S(2)}, u32[]{:S(2)}) collective-permute-start(bf16[136,1024]{1,0:T(8,128)(2,1)S(1)} %attend_beside.2.refs_10_), channel_id=1, source_target_pairs={{0,8},{1,9},{2,10},{3,11},{4,12},{5,13},{6,14},{7,15},{8,0},{9,1},... | collective-permute-start | bytes 835592 | tf_op jit(solution)/shard_map/ppermute | solution.py:271
  41.6 22.2 %collective-permute-start.10 = (bf16[136,1024]{1,0:T(8,128)(2,1)S(1)}, bf16[136,1024]{1,0:T(8,128)(2,1)S(1)}, u32[]{:S(2)}, u32[]{:S(2)}) collective-permute-start(bf16[136,1024]{1,0:T(8,128)(2,1)S(1)} %attend_beside.3), channel_id=1, source_target_pairs={{0,8},{1,9},{2,10},{3,11},{4,12},{5,13},{6,14},{7,15},{8,0},{9,1},... | collective-permute-start | bytes 835592 | tf_op jit(solution)/shard_map/ppermute | solution.py:271

commit v4 on v3

--- a/solution.py
+++ b/solution.py
@@ -80,26 +80,51 @@
     )(key, value)
 
 
-def attend_kernel(at, which, height_step, places, travels, n_live, *refs):
-    live, query, refs = refs[:n_live], refs[n_live], refs[n_live + 1 :]
-    out, stats_out = (refs[-1], None) if travels else refs[-2:]
+def bias_kernel(which, height_step, n_live, *refs):
+    live, out = refs[:n_live], refs[n_live]
     g, s = lax.axis_index("uly"), lax.axis_index("blk")
     height = 2 * (s // TW) - 1 if height_step is None else height_step
     width = 1 - 2 * (s % 2)
-    offsets = {
-        (slot, c): 9 * (frame_step + 1) + 3 * (height + 1) + width_step + 1
-        for slot, frame_step in slots_of(at)
-        for c, width_step in enumerate((0, width, -width))
-    }
-    rows = rows_of(at)
-    lane = lax.broadcasted_iota(jnp.int32, (TILE, HD), 1)
-
-    def is_live(head, offset):
+
+    def is_live(at, head, offset):
         if is_small():
             held = HEADS // 2
             place = (which * held + head % held, 2 * g + frame_of(at), 0, offset)
             return jnp.where(g == head // held, live[0][place], live[1][place]) > 0
         return live[0][head, frame_of(at), 0, offset] > 0
+
+    for at in range(2):
+        for slot, frame_step in slots_of(at):
+            for c, width_step in enumerate((0, width, -width)):
+                offset = 9 * (frame_step + 1) + 3 * (height + 1) + width_step + 1
+                for head in range(HEADS):
+                    row = bias_row(at, slot, c, head)
+                    bias = jnp.where(is_live(at, head, offset), 0.0, NONE)
+                    out[row : row + 1] = jnp.full((1, HD), bias, jnp.float32)
+
+
+def bias_row(at, slot, c, head):
+    counts = [len(slots_of(part)) for part in range(2)]
+    order = [number for number, _ in slots_of(at)].index(slot)
+    return ((counts[0] * HEADS if at else 0) + head * counts[at] + order) * 3 + c
+
+
+def biases(which, height_step, live, name):
+    rows = sum(len(slots_of(at)) for at in range(2)) * HEADS * 3
+    return pl.pallas_call(
+        functools.partial(bias_kernel, which, height_step, len(live)),
+        out_shape=jax.ShapeDtypeStruct((rows, HD), jnp.float32),
+        in_specs=[IN_SMEM] * len(live),
+        out_specs=IN_VMEM,
+        compiler_params=pltpu.CompilerParams(vmem_limit_bytes=VMEM),
+        name=name,
+    )(*live)
+
+
+def attend_kernel(at, places, travels, bias, query, *refs):
+    out, stats_out = (refs[-1], None) if travels else refs[-2:]
+    rows = rows_of(at)
+    lane = lax.broadcasted_iota(jnp.int32, (TILE, HD), 1)
 
     cols = [slice(h * HD, (h + 1) * HD) for h in range(HEADS)]
     for step in range(HEADS // STEP):
@@ -114,7 +139,8 @@
                 )
                 for i, t in enumerate(tiles):
                     part = score[:, i * TILE : (i + 1) * TILE]
-                    part = part + jnp.where(is_live(h, offsets[t]), 0.0, NONE)
+                    row = bias_row(at, *t, h)
+                    part = part + bias[row : row + 1]
                     scores[h, t] = part
                     highest[h] = jnp.maximum(highest[h], part) if h in highest else part
         top = {h: jnp.max(highest[h], axis=1, keepdims=True) for h in heads}
@@ -155,7 +181,7 @@
             stats_out[step * STAT_ROWS : (step + 1) * STAT_ROWS] = stats
 
 
-def attend(at, which, height_step, live, query, both, beyond, travels, name, after):
+def attend(at, bias, query, both, beyond, travels, name, after):
     blocks = list(both)
     places = [(0, 2 * TILE, ((1, c), (0, c))) for c in range(2)]
     places += [(0, TILE, ((slot, 2),)) for slot in range(2)]
@@ -172,9 +198,9 @@
             jax.ShapeDtypeStruct((steps * STAT_ROWS, HD), jnp.float32),
         )
     return pl.pallas_call(
-        functools.partial(attend_kernel, at, which, height_step, places, travels, len(live)),
+        functools.partial(attend_kernel, at, places, travels),
         out_shape=out_shape,
-        in_specs=[IN_SMEM] * len(live) + [IN_VMEM] * (1 + len(blocks)) + [ANYWHERE] * len(after),
+        in_specs=[IN_VMEM] * (2 + len(blocks)) + [ANYWHERE] * len(after),
         out_specs=IN_VMEM if travels else (IN_VMEM, IN_VMEM),
         compiler_params=pltpu.CompilerParams(vmem_limit_bytes=VMEM),
         cost_estimate=pl.CostEstimate(
@@ -183,7 +209,7 @@
             transcendentals=pairs * TILE * TILE,
         ),
         name=name,
-    )(*live, query, *blocks, *after)
+    )(bias, query, *blocks, *after)
 
 
 def split_stats(per_step):
@@ -306,12 +332,17 @@
         live = lax.pad(live, 0, held) + lax.pad(far_live, 0, below)
         other_live = uly_swap(live)
         other_first = border
-        border, other_live = lax.optimization_barrier((border, other_live))
-        own_live, far_live = [live, other_live], [[live, other_live]]
+        far_bias = [biases(1, None, (live, other_live), "bias_beside")]
+        border, far_bias = lax.optimization_barrier((border, far_bias))
+        own_bias = biases(0, 0, (live, other_live), "bias_own")
     else:
         other_first = border
-        own_live = [lax.all_to_all(live, "uly", split_axis=1, concat_axis=0, tiled=True)]
-        far_live = [[blk_move(own_live[0], there)] for there, _, _ in beside]
+        own_live = lax.all_to_all(live, "uly", split_axis=1, concat_axis=0, tiled=True)
+        own_bias = biases(0, 0, (own_live,), "bias_own")
+        far_bias = [
+            biases(1, height_step, (blk_move(own_live, there),), "bias_beside")
+            for there, _, height_step in beside
+        ]
     far_queries = [blk_move(query, there) for there, _, _ in beside]
     other_border = blk_move(other_first, outer_pairs)
     other_inner = blk_move(inner, outer_pairs)
@@ -324,8 +355,8 @@
 
     def attend_beside(at, after):
         return [
-            attend(at, 1, height_step, masks, block, blocks, beyond, True, "attend_beside", after)
-            for block, masks, (_, _, height_step) in zip(far_queries, far_live, beside)
+            attend(at, bias, block, blocks, beyond, True, "attend_beside", after)
+            for block, bias in zip(far_queries, far_bias)
         ]
 
     blocks, beyond = (both, mate, other_border, other_inner), []
@@ -344,7 +375,7 @@
         [blk_move(part, back) for part, (_, back, _) in zip(made[at], beside)] for at in range(2)
     ]
     own = [
-        attend(at, 0, 0, own_live, query, blocks, beyond, False, "attend_own", [])
+        attend(at, own_bias, query, blocks, beyond, False, "attend_own", [])
         for at in range(2)
     ]
     returned[1], own = lax.optimization_barrier((returned[1], own))

time: 65.4 us -> 64.5 us (0.986)
  starting transfers between devices: 19.5 us -> 17.9 us
  waiting for transfers between devices: 28.6 us -> 30.2 us
  Pallas kernels: 16.7 us -> 15.8 us
    ppermute x3, waiting for transfers between devices: 3.24 us -> 5.46 us  [uly_swap(): return lax.ppermute(block, 'uly', [(0, 1), (1, 0)])]
    ppermute x9, starting transfers between devices: 15.7 us -> 14.2 us  [blk_move(): return lax.ppermute(block, 'blk', pairs)]
    pallas_call x4 -> x6, Pallas kernels: 13 us -> 12.1 us  [the longest x4 9.43 us: attend(): pl.pallas_call(functools.partial(attend_kernel, at, places, travels), out...]
  transfers between devices with their start and end apart: 12 -> 12, of which waited for: 8 -> 7; matrix products, arithmetic and copies ran while one was open for 0% -> 0% of each run, Pallas kernels for 24% -> 23%
where the time goes in v4:
time: 64.5 us; the launch traced here: 64 us
  waiting for transfers between devices  30.2 us (47%)
  starting transfers between devices  17.9 us (28%)
  Pallas kernels  15.8 us (24%)
    ppermute x9, waiting for transfers between devices, blk_move(): return lax.ppermute(block, 'blk', pairs)  24.8 us
    ppermute x9, starting transfers between devices, blk_move(): return lax.ppermute(block, 'blk', pairs)  14.2 us
    pallas_call x4, Pallas kernels, attend(): pl.pallas_call(functools.partial(attend_kernel, at, places, travels), out...  9.43 us
    ppermute x3, waiting for transfers between devices, uly_swap(): return lax.ppermute(block, 'uly', [(0, 1), (1, 0)])  5.46 us
    ppermute x3, starting transfers between devices, uly_swap(): return lax.ppermute(block, 'uly', [(0, 1), (1, 0)])  3.69 us
    pallas_call x2, Pallas kernels, biases(): pl.pallas_call(functools.partial(bias_kernel, which, height_step, len(liv...  2.66 us
    pallas_call x2, Pallas kernels, combine(): pl.pallas_call(functools.partial(combine_kernel, at, n_more), out_shape=j...  2.43 us
  transfers between devices with their start and end apart: 12, of which 7 were waited for; matrix products, arithmetic and copies ran while one was open for 0% of the time, Pallas kernels for 23%

profile of v4, /device:TPU:0, one launch (start us, length us, event | category | flops | bytes accessed | tf_op | source)
XLA Modules:
  0.0 64.0 jit_solution(6844138874082958351)
XLA Ops:
  0.0 0.0 copy-start
  0.0 4.0 %collective-permute-start = (s32[4,4,1,27]{3,2,1,0:T(1,128)}, s32[4,4,1,27]{3,2,1,0:T(1,128)S(1)}, u32[]{:S(2)}, u32[]{:S(2)}) collective-permute-start(s32[4,4,1,27]{3,2,1,0:T(1,128)} %param.7), channel_id=1, source_target_pairs={{0,8},{1,9},{2,10},{3,11},{4,12},{5,13},{6,14},{7,15},{8,0},{9,1},... | collective-permute-start | bytes 5192 | tf_op jit(solution)/shard_map/ppermute | solution.py:297
  4.0 0.0 copy-start.1
  4.0 1.3 %pack_kv.1 = (bf16[512,1024]{1,0:T(8,128)(2,1)S(1)}, bf16[256,1024]{1,0:T(8,128)(2,1)S(1)}, bf16[256,1024]{1,0:T(8,128)(2,1)S(1)}) custom-call(bf16[256,1024]{1,0:T(8,128)(2,1)} %key.1, bf16[256,1024]{1,0:T(8,128)(2,1)} %value.1), custom_call_target="tpu_custom_call" | custom-call | bytes 2097152 | tf_op jit(solution)/shard_map/pack_kv/pallas_call | solution.py:71
  5.3 0.6 collective-permute-done
  5.9 0.0 collective-permute-start.3
  5.9 0.7 %collective-permute-start.4 = (bf16[256,1024]{1,0:T(8,128)(2,1)S(1)}, bf16[256,1024]{1,0:T(8,128)(2,1)S(1)}, u32[]{:S(2)}, u32[]{:S(2)}) collective-permute-start(bf16[256,1024]{1,0:T(8,128)(2,1)S(1)} %get-tuple-element.38), channel_id=1, source_target_pairs={{2,1},{4,3},{6,5},{10,9},{12,11},{14,13},{1,2},{3,4},{5,6},{9,10},... | collective-permute-start | bytes 1572872 | tf_op jit(solution)/shard_map/ppermute | solution.py:297
  6.6 0.0 copy-done
  6.6 3.0 %collective-permute-start.2 = (bf16[256,1024]{1,0:T(8,128)(2,1)S(1)}, bf16[256,1024]{1,0:T(8,128)(2,1)S(1)}, u32[]{:S(2)}, u32[]{:S(2)}) collective-permute-start(bf16[256,1024]{1,0:T(8,128)(2,1)S(1)} %copy-done), channel_id=1, source_target_pairs={{0,8},{1,9},{2,10},{3,11},{4,12},{5,13},{6,14},{7,15},{8,0},{9,1},... | collective-permute-start | bytes 1572872 | tf_op jit(solution)/shard_map/ppermute | solution.py:297
  9.6 0.7 %collective-permute-start.6 = (bf16[256,1024]{1,0:T(8,128)(2,1)S(1)}, bf16[256,1024]{1,0:T(8,128)(2,1)S(1)}, u32[]{:S(2)}, u32[]{:S(2)}) collective-permute-start(bf16[256,1024]{1,0:T(8,128)(2,1)S(1)} %get-tuple-element.37), channel_id=1, source_target_pairs={{2,1},{4,3},{6,5},{10,9},{12,11},{14,13},{1,2},{3,4},{5,6},{9,10},... | collective-permute-start | bytes 1572872 | tf_op jit(solution)/shard_map/ppermute | solution.py:297
  10.3 0.0 copy-done.1
  10.3 1.6 %collective-permute-start.1 = (s32[8,4,1,27]{3,2,1,0:T(1,128)S(1)}, s32[8,4,1,27]{3,2,1,0:T(1,128)S(1)}, u32[]{:S(2)}, u32[]{:S(2)}) collective-permute-start(s32[8,4,1,27]{3,2,1,0:T(1,128)S(1)} %pad_add_fusion.refs_0_), channel_id=1, source_target_pairs={{0,16},{16,0},{1,17},{17,1},{2,18},{18,2},{3,19},{19,3},{4,20},{20... | collective-permute-start | bytes 10376 | tf_op jit(solution)/shard_map/ppermute | solution.py:304
  11.9 2.2 %collective-permute-done.1.refs_1_ = s32[8,4,1,27]{3,2,1,0:T(1,128)S(1)} collective-permute-done((s32[8,4,1,27]{3,2,1,0:T(1,128)S(1)}, s32[8,4,1,27]{3,2,1,0:T(1,128)S(1)}, u32[]{:S(2)}, u32[]{:S(2)}) %collective-permute-start.1) | collective-permute-done | bytes 3488 | tf_op jit(solution)/shard_map/ppermute | solution.py:304
  14.1 1.3 %bias_beside.1.bias = f32[120,128]{1,0:T(8,128)S(1)} custom-call(s32[8,4,1,27]{3,2,1,0:T(1,128)S(1)} %pad_add_fusion.refs_0_, s32[8,4,1,27]{3,2,1,0:T(1,128)S(1)} %collective-permute-done.1.refs_1_), custom_call_target="tpu_custom_call" | custom-call | tf_op jit(solution)/shard_map/bias_beside/pallas_call | solution.py:114
  15.4 1.6 %collective-permute-start.7 = (bf16[256,1024]{1,0:T(8,128)(2,1)S(1)}, bf16[256,1024]{1,0:T(8,128)(2,1)S(1)}, u32[]{:S(2)}, u32[]{:S(2)}) collective-permute-start(bf16[256,1024]{1,0:T(8,128)(2,1)S(1)} %get-tuple-element.38), channel_id=1, source_target_pairs={{0,16},{16,0},{1,17},{17,1},{2,18},{18,2},{3,19},{19,3},{4,20},{20... | collective-permute-start | bytes 1572872 | tf_op jit(solution)/shard_map/ppermute | solution.py:304
  17.0 0.0 collective-permute-done.4.refs_2_
  17.1 3.6 %collective-permute-start.5 = (bf16[128,1024]{1,0:T(8,128)(2,1)S(1)}, bf16[128,1024]{1,0:T(8,128)(2,1)S(1)}, u32[]{:S(2)}, u32[]{:S(2)}) collective-permute-start(bf16[128,1024]{1,0:T(8,128)(2,1)S(1)} %slice.4), channel_id=1, source_target_pairs={{0,1},{1,0},{2,3},{3,2},{4,5},{5,4},{6,7},{7,6},{8,9},{9,8},{10,11... | collective-permute-start | bytes 786440 | tf_op jit(solution)/shard_map/ppermute | solution.py:297
  20.7 1.2 %collective-permute-done.5.refs_8_ = bf16[128,1024]{1,0:T(8,128)(2,1)S(1)} collective-permute-done((bf16[128,1024]{1,0:T(8,128)(2,1)S(1)}, bf16[128,1024]{1,0:T(8,128)(2,1)S(1)}, u32[]{:S(2)}, u32[]{:S(2)}) %collective-permute-start.5) | collective-permute-done | bytes 262176 | tf_op jit(solution)/shard_map/ppermute | solution.py:297
  21.8 0.5 collective-permute-start.9
  22.3 9.0 %collective-permute-done.2.query = bf16[256,1024]{1,0:T(8,128)(2,1)S(1)} collective-permute-done((bf16[256,1024]{1,0:T(8,128)(2,1)S(1)}, bf16[256,1024]{1,0:T(8,128)(2,1)S(1)}, u32[]{:S(2)}, u32[]{:S(2)}) %collective-permute-start.2) | collective-permute-done | bytes 524320 | tf_op jit(solution)/shard_map/ppermute | solution.py:297
  31.3 0.0 collective-permute-done.6.refs_3_
  31.3 0.0 collective-permute-done.3.refs_1_
  31.4 1.9 %attend_beside.2.refs_7_ = bf16[136,1024]{1,0:T(8,128)(2,1)S(1)} custom-call(f32[120,128]{1,0:T(8,128)S(1)} %bias_beside.1.bias, bf16[256,1024]{1,0:T(8,128)(2,1)S(1)} %collective-permute-done.2.query, bf16[512,1024]{1,0:T(8,128)(2,1)S(1)} %get-tuple-element.35.refs_0_, bf16[512,1024]{1,0:T(8,128)(2,1)S(1)} %collective-permute-done.3.refs_1_, ...), custom_call_target="tpu_custom_call" | custom-call | flops 402653184 | bytes 4194304 | tf_op jit(solution)/shard_map/attend_beside/pallas_call | solution.py:200
  33.3 0.0 collective-permute-done.7.refs_4_
  33.3 2.1 %collective-permute-start.8 = (bf16[256,1024]{1,0:T(8,128)(2,1)S(1)}, bf16[256,1024]{1,0:T(8,128)(2,1)S(1)}, u32[]{:S(2)}, u32[]{:S(2)}) collective-permute-start(bf16[256,1024]{1,0:T(8,128)(2,1)S(1)} %collective-permute-done.7.refs_4_), channel_id=1, source_target_pairs={{0,1},{1,0},{2,3},{3,2},{4,5},{5,4},{6,7},{7,6},{8,9},{9,8},{10,11... | collective-permute-start | bytes 1572872 | tf_op jit(solution)/shard_map/ppermute | solution.py:297
  35.4 0.0 collective-permute-start.11
  35.4 3.2 %collective-permute-done.9.refs_6_ = bf16[256,1024]{1,0:T(8,128)(2,1)S(1)} collective-permute-done((bf16[256,1024]{1,0:T(8,128)(2,1)S(1)}, bf16[256,1024]{1,0:T(8,128)(2,1)S(1)}, u32[]{:S(2)}, u32[]{:S(2)}) %collective-permute-start.9) | collective-permute-done | bytes 524320 | tf_op jit(solution)/shard_map/ppermute | solution.py:304
  38.6 0.0 collective-permute-done.8.refs_5_
  38.6 2.9 %attend_beside.3 = bf16[136,1024]{1,0:T(8,128)(2,1)S(1)} custom-call(f32[120,128]{1,0:T(8,128)S(1)} %bias_beside.1.bias, bf16[256,1024]{1,0:T(8,128)(2,1)S(1)} %collective-permute-done.2.query, bf16[512,1024]{1,0:T(8,128)(2,1)S(1)} %get-tuple-element.35.refs_0_, bf16[512,1024]{1,0:T(8,128)(2,1)S(1)} %collective-permute-done.3.refs_1_, ...), custom_call_target="tpu_custom_call" | custom-call | flops 603979776 | bytes 5767168 | tf_op jit(solution)/shard_map/attend_beside/pallas_call | solution.py:200
  41.5 0.1 collective-permute-start.10
  41.6 1.3 %bias_own.1.bias = f32[120,128]{1,0:T(8,128)S(1)} custom-call(s32[8,4,1,27]{3,2,1,0:T(1,128)S(1)} %pad_add_fusion.refs_0_, s32[8,4,1,27]{3,2,1,0:T(1,128)S(1)} %collective-permute-done.1.refs_1_), custom_call_target="tpu_custom_call" | custom-call | tf_op jit(solution)/shard_map/bias_own/pallas_call | solution.py:114
  42.9 1.9 %attend_own.3 = (f32[128,1024]{1,0:T(8,128)S(1)}, f32[16,128]{1,0:T(8,128)S(1)}) custom-call(f32[120,128]{1,0:T(8,128)S(1)} %bias_own.1.bias, bf16[256,1024]{1,0:T(8,128)(2,1)S(1)} %copy-done, bf16[512,1024]{1,0:T(8,128)(2,1)S(1)} %get-tuple-element.35.refs_0_, bf16[512,1024]{1,0:T(8,128)(2,1)S(1)} %collective-permute-done.3.refs_1_, ...), custom_call_target="tpu_custom_call" | custom-call | flops 402653184 | bytes 4194304 | tf_op jit(solution)/shard_map/attend_own/pallas_call | solution.py:200
  44.7 2.8 %attend_own.2 = (f32[128,1024]{1,0:T(8,128)S(1)}, f32[16,128]{1,0:T(8,128)S(1)}) custom-call(f32[120,128]{1,0:T(8,128)S(1)} %bias_own.1.bias, bf16[256,1024]{1,0:T(8,128)(2,1)S(1)} %copy-done, bf16[512,1024]{1,0:T(8,128)(2,1)S(1)} %get-tuple-element.35.refs_0_, bf16[512,1024]{1,0:T(8,128)(2,1)S(1)} %collective-permute-done.3.refs_1_, ...), custom_call_target="tpu_custom_call" | custom-call | flops 603979776 | bytes 5767168 | tf_op jit(solution)/shard_map/attend_own/pallas_call | solution.py:200
  47.5 10.2 %collective-permute-done.11.refs_0_ = bf16[136,1024]{1,0:T(8,128)(2,1)S(1)} collective-permute-done((bf16[136,1024]{1,0:T(8,128)(2,1)S(1)}, bf16[136,1024]{1,0:T(8,128)(2,1)S(1)}, u32[]{:S(2)}, u32[]{:S(2)}) %collective-permute-start.11) | collective-permute-done | bytes 278560 | tf_op jit(solution)/shard_map/ppermute | solution.py:297
  57.7 1.2 %combine.2.refs_3_ = bf16[256,1024]{1,0:T(8,128)(2,1)} custom-call(bf16[136,1024]{1,0:T(8,128)(2,1)S(1)} %collective-permute-done.11.refs_0_, f32[128,1024]{1,0:T(8,128)S(1)} %get-tuple-element.49.refs_1_, f32[16,128]{1,0:T(8,128)S(1)} %get-tuple-element.50.refs_2_), custom_call_target="tpu_custom_call" | custom-call | tf_op jit(solution)/shard_map/combine/pallas_call | solution.py:277
  59.0 3.9 %collective-permute-done.10.refs_0_ = bf16[136,1024]{1,0:T(8,128)(2,1)S(1)} collective-permute-done((bf16[136,1024]{1,0:T(8,128)(2,1)S(1)}, bf16[136,1024]{1,0:T(8,128)(2,1)S(1)}, u32[]{:S(2)}, u32[]{:S(2)}) %collective-permute-start.10) | collective-permute-done | bytes 278560 | tf_op jit(solution)/shard_map/ppermute | solution.py:297
  62.8 1.2 %combine.3 = bf16[256,1024]{1,0:T(8,128)(2,1)} custom-call(bf16[136,1024]{1,0:T(8,128)(2,1)S(1)} %collective-permute-done.10.refs_0_, f32[128,1024]{1,0:T(8,128)S(1)} %get-tuple-element.46.refs_1_, f32[16,128]{1,0:T(8,128)S(1)} %get-tuple-element.47.refs_2_, bf16[256,1024]{1,0:T(8,128)(2,1)} %combine.2.refs_3_), custom_call_target="tpu_custom_call", output_to_operand_aliasing={{}: (3, {})} | custom-call | tf_op jit(solution)/shard_map/combine/pallas_call | solution.py:277
  (2 shorter events, 0.0 us)
Async XLA Ops:
  0.0 6.6 %copy-start = (bf16[256,1024]{1,0:T(8,128)(2,1)S(1)}, bf16[256,1024]{1,0:T(8,128)(2,1)}, u32[]{:S(2)}) copy-start(bf16[256,1024]{1,0:T(8,128)(2,1)} %query.1) | copy-start | bytes 1572868
  0.0 5.9 %collective-permute-start = (s32[4,4,1,27]{3,2,1,0:T(1,128)}, s32[4,4,1,27]{3,2,1,0:T(1,128)S(1)}, u32[]{:S(2)}, u32[]{:S(2)}) collective-permute-start(s32[4,4,1,27]{3,2,1,0:T(1,128)} %param.7), channel_id=1, source_target_pairs={{0,8},{1,9},{2,10},{3,11},{4,12},{5,13},{6,14},{7,15},{8,0},{9,1},... | collective-permute-start | bytes 5192 | tf_op jit(solution)/shard_map/ppermute | solution.py:297
  4.0 6.2 %copy-start.1 = (s32[4,4,1,27]{3,2,1,0:T(1,128)S(1)}, s32[4,4,1,27]{3,2,1,0:T(1,128)}, u32[]{:S(2)}) copy-start(s32[4,4,1,27]{3,2,1,0:T(1,128)} %param.7) | copy-start | bytes 5188
  5.9 25.5 %collective-permute-start.3 = (bf16[512,1024]{1,0:T(8,128)(2,1)S(1)}, bf16[512,1024]{1,0:T(8,128)(2,1)S(1)}, u32[]{:S(2)}, u32[]{:S(2)}) collective-permute-start(bf16[512,1024]{1,0:T(8,128)(2,1)S(1)} %get-tuple-element.35.refs_0_), channel_id=1, source_target_pairs={{0,1},{1,0},{2,3},{3,2},{4,5},{5,4},{6,7},{7,6},{8,9},{9,8},{10,11... | collective-permute-start | bytes 3145736 | tf_op jit(solution)/shard_map/ppermute | solution.py:297
  5.9 11.1 %collective-permute-start.4 = (bf16[256,1024]{1,0:T(8,128)(2,1)S(1)}, bf16[256,1024]{1,0:T(8,128)(2,1)S(1)}, u32[]{:S(2)}, u32[]{:S(2)}) collective-permute-start(bf16[256,1024]{1,0:T(8,128)(2,1)S(1)} %get-tuple-element.38), channel_id=1, source_target_pairs={{2,1},{4,3},{6,5},{10,9},{12,11},{14,13},{1,2},{3,4},{5,6},{9,10},... | collective-permute-start | bytes 1572872 | tf_op jit(solution)/shard_map/ppermute | solution.py:297
  6.6 24.8 %collective-permute-start.2 = (bf16[256,1024]{1,0:T(8,128)(2,1)S(1)}, bf16[256,1024]{1,0:T(8,128)(2,1)S(1)}, u32[]{:S(2)}, u32[]{:S(2)}) collective-permute-start(bf16[256,1024]{1,0:T(8,128)(2,1)S(1)} %copy-done), channel_id=1, source_target_pairs={{0,8},{1,9},{2,10},{3,11},{4,12},{5,13},{6,14},{7,15},{8,0},{9,1},... | collective-permute-start | bytes 1572872 | tf_op jit(solution)/shard_map/ppermute | solution.py:297
  9.6 21.8 %collective-permute-start.6 = (bf16[256,1024]{1,0:T(8,128)(2,1)S(1)}, bf16[256,1024]{1,0:T(8,128)(2,1)S(1)}, u32[]{:S(2)}, u32[]{:S(2)}) collective-permute-start(bf16[256,1024]{1,0:T(8,128)(2,1)S(1)} %get-tuple-element.37), channel_id=1, source_target_pairs={{2,1},{4,3},{6,5},{10,9},{12,11},{14,13},{1,2},{3,4},{5,6},{9,10},... | collective-permute-start | bytes 1572872 | tf_op jit(solution)/shard_map/ppermute | solution.py:297
  10.3 3.8 %collective-permute-start.1 = (s32[8,4,1,27]{3,2,1,0:T(1,128)S(1)}, s32[8,4,1,27]{3,2,1,0:T(1,128)S(1)}, u32[]{:S(2)}, u32[]{:S(2)}) collective-permute-start(s32[8,4,1,27]{3,2,1,0:T(1,128)S(1)} %pad_add_fusion.refs_0_), channel_id=1, source_target_pairs={{0,16},{16,0},{1,17},{17,1},{2,18},{18,2},{3,19},{19,3},{4,20},{20... | collective-permute-start | bytes 10376 | tf_op jit(solution)/shard_map/ppermute | solution.py:304
  15.4 17.8 %collective-permute-start.7 = (bf16[256,1024]{1,0:T(8,128)(2,1)S(1)}, bf16[256,1024]{1,0:T(8,128)(2,1)S(1)}, u32[]{:S(2)}, u32[]{:S(2)}) collective-permute-start(bf16[256,1024]{1,0:T(8,128)(2,1)S(1)} %get-tuple-element.38), channel_id=1, source_target_pairs={{0,16},{16,0},{1,17},{17,1},{2,18},{18,2},{3,19},{19,3},{4,20},{20... | collective-permute-start | bytes 1572872 | tf_op jit(solution)/shard_map/ppermute | solution.py:304
  17.1 4.8 %collective-permute-start.5 = (bf16[128,1024]{1,0:T(8,128)(2,1)S(1)}, bf16[128,1024]{1,0:T(8,128)(2,1)S(1)}, u32[]{:S(2)}, u32[]{:S(2)}) collective-permute-start(bf16[128,1024]{1,0:T(8,128)(2,1)S(1)} %slice.4), channel_id=1, source_target_pairs={{0,1},{1,0},{2,3},{3,2},{4,5},{5,4},{6,7},{7,6},{8,9},{9,8},{10,11... | collective-permute-start | bytes 786440 | tf_op jit(solution)/shard_map/ppermute | solution.py:297
  21.8 16.8 %collective-permute-start.9 = (bf16[256,1024]{1,0:T(8,128)(2,1)S(1)}, bf16[256,1024]{1,0:T(8,128)(2,1)S(1)}, u32[]{:S(2)}, u32[]{:S(2)}) collective-permute-start(bf16[256,1024]{1,0:T(8,128)(2,1)S(1)} %collective-permute-done.4.refs_2_), channel_id=1, source_target_pairs={{0,16},{16,0},{1,17},{17,1},{2,18},{18,2},{3,19},{19,3},{4,20},{20... | collective-permute-start | bytes 1572872 | tf_op jit(solution)/shard_map/ppermute | solution.py:304
  33.3 5.4 %collective-permute-start.8 = (bf16[256,1024]{1,0:T(8,128)(2,1)S(1)}, bf16[256,1024]{1,0:T(8,128)(2,1)S(1)}, u32[]{:S(2)}, u32[]{:S(2)}) collective-permute-start(bf16[256,1024]{1,0:T(8,128)(2,1)S(1)} %collective-permute-done.7.refs_4_), channel_id=1, source_target_pairs={{0,1},{1,0},{2,3},{3,2},{4,5},{5,4},{6,7},{7,6},{8,9},{9,8},{10,11... | collective-permute-start | bytes 1572872 | tf_op jit(solution)/shard_map/ppermute | solution.py:297
  35.4 22.3 %collective-permute-start.11 = (bf16[136,1024]{1,0:T(8,128)(2,1)S(1)}, bf16[136,1024]{1,0:T(8,128)(2,1)S(1)}, u32[]{:S(2)}, u32[]{:S(2)}) collective-permute-start(bf16[136,1024]{1,0:T(8,128)(2,1)S(1)} %attend_beside.2.refs_7_), channel_id=1, source_target_pairs={{0,8},{1,9},{2,10},{3,11},{4,12},{5,13},{6,14},{7,15},{8,0},{9,1},... | collective-permute-start | bytes 835592 | tf_op jit(solution)/shard_map/ppermute | solution.py:297
  41.5 21.3 %collective-permute-start.10 = (bf16[136,1024]{1,0:T(8,128)(2,1)S(1)}, bf16[136,1024]{1,0:T(8,128)(2,1)S(1)}, u32[]{:S(2)}, u32[]{:S(2)}) collective-permute-start(bf16[136,1024]{1,0:T(8,128)(2,1)S(1)} %attend_beside.3), channel_id=1, source_target_pairs={{0,8},{1,9},{2,10},{3,11},{4,12},{5,13},{6,14},{7,15},{8,0},{9,1},... | collective-permute-start | bytes 835592 | tf_op jit(solution)/shard_map/ppermute | solution.py:297

commit v5 on v4

--- a/solution.py
+++ b/solution.py
@@ -332,8 +332,8 @@
         live = lax.pad(live, 0, held) + lax.pad(far_live, 0, below)
         other_live = uly_swap(live)
         other_first = border
+        border, other_live = lax.optimization_barrier((border, other_live))
         far_bias = [biases(1, None, (live, other_live), "bias_beside")]
-        border, far_bias = lax.optimization_barrier((border, far_bias))
         own_bias = biases(0, 0, (live, other_live), "bias_own")
     else:
         other_first = border
@@ -349,6 +349,7 @@
     mate = blk_move(both, mate_pairs)
     own_halo = halo(border, inner)
     if is_small():
+        other_border, far_bias = lax.optimization_barrier((other_border, far_bias))
         token = blk_move(other_border[:TILE], mate_pairs)
         other_border, token = lax.optimization_barrier((other_border, token))
     other_halo = halo(other_border, other_inner)

time: 64.5 us -> 64.5 us (level)
  starting transfers between devices: 17.9 us -> 19.1 us
  waiting for transfers between devices: 30.2 us -> 29 us
    ppermute x9, starting transfers between devices: 14.2 us -> 15.5 us  [blk_move(): return lax.ppermute(block, 'blk', pairs)]
    ppermute x3, waiting for transfers between devices: 5.46 us -> 4.2 us  [uly_swap(): return lax.ppermute(block, 'uly', [(0, 1), (1, 0)])]
where the time goes in v5:
time: 64.5 us; the launch traced here: 64 us
  waiting for transfers between devices  29 us (45%)
  starting transfers between devices  19.1 us (30%)
  Pallas kernels  15.8 us (24%)
    ppermute x9, waiting for transfers between devices, blk_move(): return lax.ppermute(block, 'blk', pairs)  24.8 us
    ppermute x9, starting transfers between devices, blk_move(): return lax.ppermute(block, 'blk', pairs)  15.5 us
    pallas_call x4, Pallas kernels, attend(): pl.pallas_call(functools.partial(attend_kernel, at, places, travels), out...  9.42 us
    ppermute x3, waiting for transfers between devices, uly_swap(): return lax.ppermute(block, 'uly', [(0, 1), (1, 0)])  4.2 us
    ppermute x3, starting transfers between devices, uly_swap(): return lax.ppermute(block, 'uly', [(0, 1), (1, 0)])  3.62 us
    pallas_call x2, Pallas kernels, biases(): pl.pallas_call(functools.partial(bias_kernel, which, height_step, len(liv...  2.65 us
    pallas_call x2, Pallas kernels, combine(): pl.pallas_call(functools.partial(combine_kernel, at, n_more), out_shape=j...  2.43 us
  transfers between devices with their start and end apart: 12, of which 7 were waited for; matrix products, arithmetic and copies ran while one was open for 0% of the time, Pallas kernels for 23%

profile of v5, /device:TPU:0, one launch (start us, length us, event | category | flops | bytes accessed | tf_op | source)
XLA Modules:
  0.0 64.0 jit_solution(4442445697934946527)
XLA Ops:
  0.0 0.0 copy-start
  0.0 4.0 %collective-permute-start = (s32[4,4,1,27]{3,2,1,0:T(1,128)}, s32[4,4,1,27]{3,2,1,0:T(1,128)S(1)}, u32[]{:S(2)}, u32[]{:S(2)}) collective-permute-start(s32[4,4,1,27]{3,2,1,0:T(1,128)} %param.7), channel_id=1, source_target_pairs={{0,8},{1,9},{2,10},{3,11},{4,12},{5,13},{6,14},{7,15},{8,0},{9,1},... | collective-permute-start | bytes 5192 | tf_op jit(solution)/shard_map/ppermute | solution.py:297
  4.0 0.0 copy-start.1
  4.0 1.3 %pack_kv.1 = (bf16[512,1024]{1,0:T(8,128)(2,1)S(1)}, bf16[256,1024]{1,0:T(8,128)(2,1)S(1)}, bf16[256,1024]{1,0:T(8,128)(2,1)S(1)}) custom-call(bf16[256,1024]{1,0:T(8,128)(2,1)} %key.1, bf16[256,1024]{1,0:T(8,128)(2,1)} %value.1), custom_call_target="tpu_custom_call" | custom-call | bytes 2097152 | tf_op jit(solution)/shard_map/pack_kv/pallas_call | solution.py:71
  5.3 0.6 collective-permute-done
  5.9 0.0 collective-permute-start.4
  5.9 0.7 %collective-permute-start.1 = (bf16[256,1024]{1,0:T(8,128)(2,1)S(1)}, bf16[256,1024]{1,0:T(8,128)(2,1)S(1)}, u32[]{:S(2)}, u32[]{:S(2)}) collective-permute-start(bf16[256,1024]{1,0:T(8,128)(2,1)S(1)} %get-tuple-element.42), channel_id=1, source_target_pairs={{2,1},{4,3},{6,5},{10,9},{12,11},{14,13},{1,2},{3,4},{5,6},{9,10},... | collective-permute-start | bytes 1572872 | tf_op jit(solution)/shard_map/ppermute | solution.py:297
  6.6 0.0 copy-done
  6.6 3.0 %collective-permute-start.3 = (bf16[256,1024]{1,0:T(8,128)(2,1)S(1)}, bf16[256,1024]{1,0:T(8,128)(2,1)S(1)}, u32[]{:S(2)}, u32[]{:S(2)}) collective-permute-start(bf16[256,1024]{1,0:T(8,128)(2,1)S(1)} %copy-done), channel_id=1, source_target_pairs={{0,8},{1,9},{2,10},{3,11},{4,12},{5,13},{6,14},{7,15},{8,0},{9,1},... | collective-permute-start | bytes 1572872 | tf_op jit(solution)/shard_map/ppermute | solution.py:297
  9.6 0.7 %collective-permute-start.6 = (bf16[256,1024]{1,0:T(8,128)(2,1)S(1)}, bf16[256,1024]{1,0:T(8,128)(2,1)S(1)}, u32[]{:S(2)}, u32[]{:S(2)}) collective-permute-start(bf16[256,1024]{1,0:T(8,128)(2,1)S(1)} %get-tuple-element.41), channel_id=1, source_target_pairs={{2,1},{4,3},{6,5},{10,9},{12,11},{14,13},{1,2},{3,4},{5,6},{9,10},... | collective-permute-start | bytes 1572872 | tf_op jit(solution)/shard_map/ppermute | solution.py:297
  10.3 0.0 copy-done.1
  10.3 1.6 %collective-permute-start.2 = (s32[8,4,1,27]{3,2,1,0:T(1,128)S(1)}, s32[8,4,1,27]{3,2,1,0:T(1,128)S(1)}, u32[]{:S(2)}, u32[]{:S(2)}) collective-permute-start(s32[8,4,1,27]{3,2,1,0:T(1,128)S(1)} %pad_add_fusion.refs_0_), channel_id=1, source_target_pairs={{0,16},{16,0},{1,17},{17,1},{2,18},{18,2},{3,19},{19,3},{4,20},{20... | collective-permute-start | bytes 10376 | tf_op jit(solution)/shard_map/ppermute | solution.py:304
  11.9 2.2 %collective-permute-done.2.refs_1_ = s32[8,4,1,27]{3,2,1,0:T(1,128)S(1)} collective-permute-done((s32[8,4,1,27]{3,2,1,0:T(1,128)S(1)}, s32[8,4,1,27]{3,2,1,0:T(1,128)S(1)}, u32[]{:S(2)}, u32[]{:S(2)}) %collective-permute-start.2) | collective-permute-done | bytes 3488 | tf_op jit(solution)/shard_map/ppermute | solution.py:304
  14.1 1.5 %collective-permute-start.7 = (bf16[256,1024]{1,0:T(8,128)(2,1)S(1)}, bf16[256,1024]{1,0:T(8,128)(2,1)S(1)}, u32[]{:S(2)}, u32[]{:S(2)}) collective-permute-start(bf16[256,1024]{1,0:T(8,128)(2,1)S(1)} %get-tuple-element.42), channel_id=1, source_target_pairs={{0,16},{16,0},{1,17},{17,1},{2,18},{18,2},{3,19},{19,3},{4,20},{20... | collective-permute-start | bytes 1572872 | tf_op jit(solution)/shard_map/ppermute | solution.py:304
  15.6 1.3 %bias_beside.1.bias = f32[120,128]{1,0:T(8,128)S(1)} custom-call(s32[8,4,1,27]{3,2,1,0:T(1,128)S(1)} %pad_add_fusion.refs_0_, s32[8,4,1,27]{3,2,1,0:T(1,128)S(1)} %collective-permute-done.2.refs_1_), custom_call_target="tpu_custom_call" | custom-call | tf_op jit(solution)/shard_map/bias_beside/pallas_call | solution.py:114
  17.0 0.0 collective-permute-done.1.refs_2_
  17.0 3.8 %collective-permute-start.5 = (bf16[128,1024]{1,0:T(8,128)(2,1)S(1)}, bf16[128,1024]{1,0:T(8,128)(2,1)S(1)}, u32[]{:S(2)}, u32[]{:S(2)}) collective-permute-start(bf16[128,1024]{1,0:T(8,128)(2,1)S(1)} %slice.3), channel_id=1, source_target_pairs={{0,1},{1,0},{2,3},{3,2},{4,5},{5,4},{6,7},{7,6},{8,9},{9,8},{10,11... | collective-permute-start | bytes 786440 | tf_op jit(solution)/shard_map/ppermute | solution.py:297
  20.8 1.2 %collective-permute-done.5.refs_8_ = bf16[128,1024]{1,0:T(8,128)(2,1)S(1)} collective-permute-done((bf16[128,1024]{1,0:T(8,128)(2,1)S(1)}, bf16[128,1024]{1,0:T(8,128)(2,1)S(1)}, u32[]{:S(2)}, u32[]{:S(2)}) %collective-permute-start.5) | collective-permute-done | bytes 262176 | tf_op jit(solution)/shard_map/ppermute | solution.py:297
  21.9 0.5 collective-permute-start.9
  22.4 8.9 %collective-permute-done.3.query = bf16[256,1024]{1,0:T(8,128)(2,1)S(1)} collective-permute-done((bf16[256,1024]{1,0:T(8,128)(2,1)S(1)}, bf16[256,1024]{1,0:T(8,128)(2,1)S(1)}, u32[]{:S(2)}, u32[]{:S(2)}) %collective-permute-start.3) | collective-permute-done | bytes 524320 | tf_op jit(solution)/shard_map/ppermute | solution.py:297
  31.3 0.0 collective-permute-done.6.refs_3_
  31.3 0.0 collective-permute-done.4.refs_1_
  31.4 1.9 %attend_beside.2.refs_7_ = bf16[136,1024]{1,0:T(8,128)(2,1)S(1)} custom-call(f32[120,128]{1,0:T(8,128)S(1)} %bias_beside.1.bias, bf16[256,1024]{1,0:T(8,128)(2,1)S(1)} %collective-permute-done.3.query, bf16[512,1024]{1,0:T(8,128)(2,1)S(1)} %get-tuple-element.38.refs_0_, bf16[512,1024]{1,0:T(8,128)(2,1)S(1)} %collective-permute-done.4.refs_1_, ...), custom_call_target="tpu_custom_call" | custom-call | flops 402653184 | bytes 4194304 | tf_op jit(solution)/shard_map/attend_beside/pallas_call | solution.py:200
  33.3 0.0 collective-permute-done.7.refs_4_
  33.3 2.1 %collective-permute-start.8 = (bf16[256,1024]{1,0:T(8,128)(2,1)S(1)}, bf16[256,1024]{1,0:T(8,128)(2,1)S(1)}, u32[]{:S(2)}, u32[]{:S(2)}) collective-permute-start(bf16[256,1024]{1,0:T(8,128)(2,1)S(1)} %collective-permute-done.7.refs_4_), channel_id=1, source_target_pairs={{0,1},{1,0},{2,3},{3,2},{4,5},{5,4},{6,7},{7,6},{8,9},{9,8},{10,11... | collective-permute-start | bytes 1572872 | tf_op jit(solution)/shard_map/ppermute | solution.py:297
  35.4 0.0 collective-permute-start.11
  35.4 2.0 %collective-permute-done.9.refs_6_ = bf16[256,1024]{1,0:T(8,128)(2,1)S(1)} collective-permute-done((bf16[256,1024]{1,0:T(8,128)(2,1)S(1)}, bf16[256,1024]{1,0:T(8,128)(2,1)S(1)}, u32[]{:S(2)}, u32[]{:S(2)}) %collective-permute-start.9) | collective-permute-done | bytes 524320 | tf_op jit(solution)/shard_map/ppermute | solution.py:304
  37.4 0.0 collective-permute-done.8.refs_5_
  37.4 2.9 %attend_beside.3 = bf16[136,1024]{1,0:T(8,128)(2,1)S(1)} custom-call(f32[120,128]{1,0:T(8,128)S(1)} %bias_beside.1.bias, bf16[256,1024]{1,0:T(8,128)(2,1)S(1)} %collective-permute-done.3.query, bf16[512,1024]{1,0:T(8,128)(2,1)S(1)} %get-tuple-element.38.refs_0_, bf16[512,1024]{1,0:T(8,128)(2,1)S(1)} %collective-permute-done.4.refs_1_, ...), custom_call_target="tpu_custom_call" | custom-call | flops 603979776 | bytes 5767168 | tf_op jit(solution)/shard_map/attend_beside/pallas_call | solution.py:200
  40.2 1.2 %collective-permute-start.10 = (bf16[136,1024]{1,0:T(8,128)(2,1)S(1)}, bf16[136,1024]{1,0:T(8,128)(2,1)S(1)}, u32[]{:S(2)}, u32[]{:S(2)}) collective-permute-start(bf16[136,1024]{1,0:T(8,128)(2,1)S(1)} %attend_beside.3), channel_id=1, source_target_pairs={{0,8},{1,9},{2,10},{3,11},{4,12},{5,13},{6,14},{7,15},{8,0},{9,1},... | collective-permute-start | bytes 835592 | tf_op jit(solution)/shard_map/ppermute | solution.py:297
  41.4 1.3 %bias_own.1.bias = f32[120,128]{1,0:T(8,128)S(1)} custom-call(s32[8,4,1,27]{3,2,1,0:T(1,128)S(1)} %pad_add_fusion.refs_0_, s32[8,4,1,27]{3,2,1,0:T(1,128)S(1)} %collective-permute-done.2.refs_1_), custom_call_target="tpu_custom_call" | custom-call | tf_op jit(solution)/shard_map/bias_own/pallas_call | solution.py:114
  42.8 1.9 %attend_own.3 = (f32[128,1024]{1,0:T(8,128)S(1)}, f32[16,128]{1,0:T(8,128)S(1)}) custom-call(f32[120,128]{1,0:T(8,128)S(1)} %bias_own.1.bias, bf16[256,1024]{1,0:T(8,128)(2,1)S(1)} %copy-done, bf16[512,1024]{1,0:T(8,128)(2,1)S(1)} %get-tuple-element.38.refs_0_, bf16[512,1024]{1,0:T(8,128)(2,1)S(1)} %collective-permute-done.4.refs_1_, ...), custom_call_target="tpu_custom_call" | custom-call | flops 402653184 | bytes 4194304 | tf_op jit(solution)/shard_map/attend_own/pallas_call | solution.py:200
  44.6 2.8 %attend_own.2 = (f32[128,1024]{1,0:T(8,128)S(1)}, f32[16,128]{1,0:T(8,128)S(1)}) custom-call(f32[120,128]{1,0:T(8,128)S(1)} %bias_own.1.bias, bf16[256,1024]{1,0:T(8,128)(2,1)S(1)} %copy-done, bf16[512,1024]{1,0:T(8,128)(2,1)S(1)} %get-tuple-element.38.refs_0_, bf16[512,1024]{1,0:T(8,128)(2,1)S(1)} %collective-permute-done.4.refs_1_, ...), custom_call_target="tpu_custom_call" | custom-call | flops 603979776 | bytes 5767168 | tf_op jit(solution)/shard_map/attend_own/pallas_call | solution.py:200
  47.4 10.3 %collective-permute-done.11.refs_0_ = bf16[136,1024]{1,0:T(8,128)(2,1)S(1)} collective-permute-done((bf16[136,1024]{1,0:T(8,128)(2,1)S(1)}, bf16[136,1024]{1,0:T(8,128)(2,1)S(1)}, u32[]{:S(2)}, u32[]{:S(2)}) %collective-permute-start.11) | collective-permute-done | bytes 278560 | tf_op jit(solution)/shard_map/ppermute | solution.py:297
  57.7 1.2 %combine.2.refs_3_ = bf16[256,1024]{1,0:T(8,128)(2,1)} custom-call(bf16[136,1024]{1,0:T(8,128)(2,1)S(1)} %collective-permute-done.11.refs_0_, f32[128,1024]{1,0:T(8,128)S(1)} %get-tuple-element.53.refs_1_, f32[16,128]{1,0:T(8,128)S(1)} %get-tuple-element.54.refs_2_), custom_call_target="tpu_custom_call" | custom-call | tf_op jit(solution)/shard_map/combine/pallas_call | solution.py:277
  59.0 3.9 %collective-permute-done.10.refs_0_ = bf16[136,1024]{1,0:T(8,128)(2,1)S(1)} collective-permute-done((bf16[136,1024]{1,0:T(8,128)(2,1)S(1)}, bf16[136,1024]{1,0:T(8,128)(2,1)S(1)}, u32[]{:S(2)}, u32[]{:S(2)}) %collective-permute-start.10) | collective-permute-done | bytes 278560 | tf_op jit(solution)/shard_map/ppermute | solution.py:297
  62.8 1.2 %combine.3 = bf16[256,1024]{1,0:T(8,128)(2,1)} custom-call(bf16[136,1024]{1,0:T(8,128)(2,1)S(1)} %collective-permute-done.10.refs_0_, f32[128,1024]{1,0:T(8,128)S(1)} %get-tuple-element.50.refs_1_, f32[16,128]{1,0:T(8,128)S(1)} %get-tuple-element.51.refs_2_, bf16[256,1024]{1,0:T(8,128)(2,1)} %combine.2.refs_3_), custom_call_target="tpu_custom_call", output_to_operand_aliasing={{}: (3, {})} | custom-call | tf_op jit(solution)/shard_map/combine/pallas_call | solution.py:277
  (2 shorter events, 0.0 us)
Async XLA Ops:
  0.0 6.6 %copy-start = (bf16[256,1024]{1,0:T(8,128)(2,1)S(1)}, bf16[256,1024]{1,0:T(8,128)(2,1)}, u32[]{:S(2)}) copy-start(bf16[256,1024]{1,0:T(8,128)(2,1)} %query.1) | copy-start | bytes 1572868
  0.0 5.9 %collective-permute-start = (s32[4,4,1,27]{3,2,1,0:T(1,128)}, s32[4,4,1,27]{3,2,1,0:T(1,128)S(1)}, u32[]{:S(2)}, u32[]{:S(2)}) collective-permute-start(s32[4,4,1,27]{3,2,1,0:T(1,128)} %param.7), channel_id=1, source_target_pairs={{0,8},{1,9},{2,10},{3,11},{4,12},{5,13},{6,14},{7,15},{8,0},{9,1},... | collective-permute-start | bytes 5192 | tf_op jit(solution)/shard_map/ppermute | solution.py:297
  4.0 6.2 %copy-start.1 = (s32[4,4,1,27]{3,2,1,0:T(1,128)S(1)}, s32[4,4,1,27]{3,2,1,0:T(1,128)}, u32[]{:S(2)}) copy-start(s32[4,4,1,27]{3,2,1,0:T(1,128)} %param.7) | copy-start | bytes 5188
  5.9 25.5 %collective-permute-start.4 = (bf16[512,1024]{1,0:T(8,128)(2,1)S(1)}, bf16[512,1024]{1,0:T(8,128)(2,1)S(1)}, u32[]{:S(2)}, u32[]{:S(2)}) collective-permute-start(bf16[512,1024]{1,0:T(8,128)(2,1)S(1)} %get-tuple-element.38.refs_0_), channel_id=1, source_target_pairs={{0,1},{1,0},{2,3},{3,2},{4,5},{5,4},{6,7},{7,6},{8,9},{9,8},{10,11... | collective-permute-start | bytes 3145736 | tf_op jit(solution)/shard_map/ppermute | solution.py:297
  5.9 11.1 %collective-permute-start.1 = (bf16[256,1024]{1,0:T(8,128)(2,1)S(1)}, bf16[256,1024]{1,0:T(8,128)(2,1)S(1)}, u32[]{:S(2)}, u32[]{:S(2)}) collective-permute-start(bf16[256,1024]{1,0:T(8,128)(2,1)S(1)} %get-tuple-element.42), channel_id=1, source_target_pairs={{2,1},{4,3},{6,5},{10,9},{12,11},{14,13},{1,2},{3,4},{5,6},{9,10},... | collective-permute-start | bytes 1572872 | tf_op jit(solution)/shard_map/ppermute | solution.py:297
  6.6 24.8 %collective-permute-start.3 = (bf16[256,1024]{1,0:T(8,128)(2,1)S(1)}, bf16[256,1024]{1,0:T(8,128)(2,1)S(1)}, u32[]{:S(2)}, u32[]{:S(2)}) collective-permute-start(bf16[256,1024]{1,0:T(8,128)(2,1)S(1)} %copy-done), channel_id=1, source_target_pairs={{0,8},{1,9},{2,10},{3,11},{4,12},{5,13},{6,14},{7,15},{8,0},{9,1},... | collective-permute-start | bytes 1572872 | tf_op jit(solution)/shard_map/ppermute | solution.py:297
  9.6 21.8 %collective-permute-start.6 = (bf16[256,1024]{1,0:T(8,128)(2,1)S(1)}, bf16[256,1024]{1,0:T(8,128)(2,1)S(1)}, u32[]{:S(2)}, u32[]{:S(2)}) collective-permute-start(bf16[256,1024]{1,0:T(8,128)(2,1)S(1)} %get-tuple-element.41), channel_id=1, source_target_pairs={{2,1},{4,3},{6,5},{10,9},{12,11},{14,13},{1,2},{3,4},{5,6},{9,10},... | collective-permute-start | bytes 1572872 | tf_op jit(solution)/shard_map/ppermute | solution.py:297
  10.3 3.8 %collective-permute-start.2 = (s32[8,4,1,27]{3,2,1,0:T(1,128)S(1)}, s32[8,4,1,27]{3,2,1,0:T(1,128)S(1)}, u32[]{:S(2)}, u32[]{:S(2)}) collective-permute-start(s32[8,4,1,27]{3,2,1,0:T(1,128)S(1)} %pad_add_fusion.refs_0_), channel_id=1, source_target_pairs={{0,16},{16,0},{1,17},{17,1},{2,18},{18,2},{3,19},{19,3},{4,20},{20... | collective-permute-start | bytes 10376 | tf_op jit(solution)/shard_map/ppermute | solution.py:304
  14.1 19.2 %collective-permute-start.7 = (bf16[256,1024]{1,0:T(8,128)(2,1)S(1)}, bf16[256,1024]{1,0:T(8,128)(2,1)S(1)}, u32[]{:S(2)}, u32[]{:S(2)}) collective-permute-start(bf16[256,1024]{1,0:T(8,128)(2,1)S(1)} %get-tuple-element.42), channel_id=1, source_target_pairs={{0,16},{16,0},{1,17},{17,1},{2,18},{18,2},{3,19},{19,3},{4,20},{20... | collective-permute-start | bytes 1572872 | tf_op jit(solution)/shard_map/ppermute | solution.py:304
  17.0 4.9 %collective-permute-start.5 = (bf16[128,1024]{1,0:T(8,128)(2,1)S(1)}, bf16[128,1024]{1,0:T(8,128)(2,1)S(1)}, u32[]{:S(2)}, u32[]{:S(2)}) collective-permute-start(bf16[128,1024]{1,0:T(8,128)(2,1)S(1)} %slice.3), channel_id=1, source_target_pairs={{0,1},{1,0},{2,3},{3,2},{4,5},{5,4},{6,7},{7,6},{8,9},{9,8},{10,11... | collective-permute-start | bytes 786440 | tf_op jit(solution)/shard_map/ppermute | solution.py:297
  21.9 15.4 %collective-permute-start.9 = (bf16[256,1024]{1,0:T(8,128)(2,1)S(1)}, bf16[256,1024]{1,0:T(8,128)(2,1)S(1)}, u32[]{:S(2)}, u32[]{:S(2)}) collective-permute-start(bf16[256,1024]{1,0:T(8,128)(2,1)S(1)} %collective-permute-done.1.refs_2_), channel_id=1, source_target_pairs={{0,16},{16,0},{1,17},{17,1},{2,18},{18,2},{3,19},{19,3},{4,20},{20... | collective-permute-start | bytes 1572872 | tf_op jit(solution)/shard_map/ppermute | solution.py:304
  33.3 4.1 %collective-permute-start.8 = (bf16[256,1024]{1,0:T(8,128)(2,1)S(1)}, bf16[256,1024]{1,0:T(8,128)(2,1)S(1)}, u32[]{:S(2)}, u32[]{:S(2)}) collective-permute-start(bf16[256,1024]{1,0:T(8,128)(2,1)S(1)} %collective-permute-done.7.refs_4_), channel_id=1, source_target_pairs={{0,1},{1,0},{2,3},{3,2},{4,5},{5,4},{6,7},{7,6},{8,9},{9,8},{10,11... | collective-permute-start | bytes 1572872 | tf_op jit(solution)/shard_map/ppermute | solution.py:297
  35.4 22.3 %collective-permute-start.11 = (bf16[136,1024]{1,0:T(8,128)(2,1)S(1)}, bf16[136,1024]{1,0:T(8,128)(2,1)S(1)}, u32[]{:S(2)}, u32[]{:S(2)}) collective-permute-start(bf16[136,1024]{1,0:T(8,128)(2,1)S(1)} %attend_beside.2.refs_7_), channel_id=1, source_target_pairs={{0,8},{1,9},{2,10},{3,11},{4,12},{5,13},{6,14},{7,15},{8,0},{9,1},... | collective-permute-start | bytes 835592 | tf_op jit(solution)/shard_map/ppermute | solution.py:297
  40.2 22.6 %collective-permute-start.10 = (bf16[136,1024]{1,0:T(8,128)(2,1)S(1)}, bf16[136,1024]{1,0:T(8,128)(2,1)S(1)}, u32[]{:S(2)}, u32[]{:S(2)}) collective-permute-start(bf16[136,1024]{1,0:T(8,128)(2,1)S(1)} %attend_beside.3), channel_id=1, source_target_pairs={{0,8},{1,9},{2,10},{3,11},{4,12},{5,13},{6,14},{7,15},{8,0},{9,1},... | collective-permute-start | bytes 835592 | tf_op jit(solution)/shard_map/ppermute | solution.py:297

commit v6 on v5

--- a/solution.py
+++ b/solution.py
@@ -16,7 +16,7 @@
 COL = STEP * HD
 C2 = HD ** (-0.5) * 1.4426950408889634
 NONE = -1e30
-STAT_ROWS = 8
+STAT_ROWS = 16
 TERMS = 3
 VMEM = 20 * 2**20
 

time: 64.5 us -> 65.9 us (1.022)
  waiting for transfers between devices: 29 us -> 30.4 us
    ppermute x9, waiting for transfers between devices: 24.8 us -> 26.3 us  [blk_move(): return lax.ppermute(block, 'blk', pairs)]
  transfers between devices with their start and end apart: 12 -> 12, of which waited for: 7 -> 7; matrix products, arithmetic and copies ran while one was open for 0% -> 0% of each run, Pallas kernels for 23% -> 22%
where the time goes in v6:
time: 65.9 us; the launch traced here: 65.5 us
  waiting for transfers between devices  30.4 us (46%)
  starting transfers between devices  19.1 us (29%)
  Pallas kernels  15.8 us (24%)
    ppermute x9, waiting for transfers between devices, blk_move(): return lax.ppermute(block, 'blk', pairs)  26.3 us
    ppermute x9, starting transfers between devices, blk_move(): return lax.ppermute(block, 'blk', pairs)  15.5 us
    pallas_call x4, Pallas kernels, attend(): pl.pallas_call(functools.partial(attend_kernel, at, places, travels), out...  9.48 us
    ppermute x3, waiting for transfers between devices, uly_swap(): return lax.ppermute(block, 'uly', [(0, 1), (1, 0)])  4.15 us
    ppermute x3, starting transfers between devices, uly_swap(): return lax.ppermute(block, 'uly', [(0, 1), (1, 0)])  3.62 us
    pallas_call x2, Pallas kernels, biases(): pl.pallas_call(functools.partial(bias_kernel, which, height_step, len(liv...  2.65 us
    pallas_call x2, Pallas kernels, combine(): pl.pallas_call(functools.partial(combine_kernel, at, n_more), out_shape=j...  2.43 us
  transfers between devices with their start and end apart: 12, of which 7 were waited for; matrix products, arithmetic and copies ran while one was open for 0% of the time, Pallas kernels for 22%

profile of v6, /device:TPU:0, one launch (start us, length us, event | category | flops | bytes accessed | tf_op | source)
XLA Modules:
  0.0 65.5 jit_solution(14105136267938145808)
XLA Ops:
  0.0 0.0 copy-start
  0.0 4.0 %collective-permute-start = (s32[4,4,1,27]{3,2,1,0:T(1,128)}, s32[4,4,1,27]{3,2,1,0:T(1,128)S(1)}, u32[]{:S(2)}, u32[]{:S(2)}) collective-permute-start(s32[4,4,1,27]{3,2,1,0:T(1,128)} %param.7), channel_id=1, source_target_pairs={{0,8},{1,9},{2,10},{3,11},{4,12},{5,13},{6,14},{7,15},{8,0},{9,1},... | collective-permute-start | bytes 5192 | tf_op jit(solution)/shard_map/ppermute | solution.py:297
  4.0 0.0 copy-start.1
  4.0 1.3 %pack_kv.1 = (bf16[512,1024]{1,0:T(8,128)(2,1)S(1)}, bf16[256,1024]{1,0:T(8,128)(2,1)S(1)}, bf16[256,1024]{1,0:T(8,128)(2,1)S(1)}) custom-call(bf16[256,1024]{1,0:T(8,128)(2,1)} %key.1, bf16[256,1024]{1,0:T(8,128)(2,1)} %value.1), custom_call_target="tpu_custom_call" | custom-call | bytes 2097152 | tf_op jit(solution)/shard_map/pack_kv/pallas_call | solution.py:71
  5.3 0.6 collective-permute-done
  5.9 0.0 collective-permute-start.4
  5.9 0.7 %collective-permute-start.1 = (bf16[256,1024]{1,0:T(8,128)(2,1)S(1)}, bf16[256,1024]{1,0:T(8,128)(2,1)S(1)}, u32[]{:S(2)}, u32[]{:S(2)}) collective-permute-start(bf16[256,1024]{1,0:T(8,128)(2,1)S(1)} %get-tuple-element.42), channel_id=1, source_target_pairs={{2,1},{4,3},{6,5},{10,9},{12,11},{14,13},{1,2},{3,4},{5,6},{9,10},... | collective-permute-start | bytes 1572872 | tf_op jit(solution)/shard_map/ppermute | solution.py:297
  6.6 0.0 copy-done
  6.6 3.0 %collective-permute-start.3 = (bf16[256,1024]{1,0:T(8,128)(2,1)S(1)}, bf16[256,1024]{1,0:T(8,128)(2,1)S(1)}, u32[]{:S(2)}, u32[]{:S(2)}) collective-permute-start(bf16[256,1024]{1,0:T(8,128)(2,1)S(1)} %copy-done), channel_id=1, source_target_pairs={{0,8},{1,9},{2,10},{3,11},{4,12},{5,13},{6,14},{7,15},{8,0},{9,1},... | collective-permute-start | bytes 1572872 | tf_op jit(solution)/shard_map/ppermute | solution.py:297
  9.6 0.7 %collective-permute-start.6 = (bf16[256,1024]{1,0:T(8,128)(2,1)S(1)}, bf16[256,1024]{1,0:T(8,128)(2,1)S(1)}, u32[]{:S(2)}, u32[]{:S(2)}) collective-permute-start(bf16[256,1024]{1,0:T(8,128)(2,1)S(1)} %get-tuple-element.41), channel_id=1, source_target_pairs={{2,1},{4,3},{6,5},{10,9},{12,11},{14,13},{1,2},{3,4},{5,6},{9,10},... | collective-permute-start | bytes 1572872 | tf_op jit(solution)/shard_map/ppermute | solution.py:297
  10.3 0.0 copy-done.1
  10.3 1.6 %collective-permute-start.2 = (s32[8,4,1,27]{3,2,1,0:T(1,128)S(1)}, s32[8,4,1,27]{3,2,1,0:T(1,128)S(1)}, u32[]{:S(2)}, u32[]{:S(2)}) collective-permute-start(s32[8,4,1,27]{3,2,1,0:T(1,128)S(1)} %pad_add_fusion.refs_0_), channel_id=1, source_target_pairs={{0,16},{16,0},{1,17},{17,1},{2,18},{18,2},{3,19},{19,3},{4,20},{20... | collective-permute-start | bytes 10376 | tf_op jit(solution)/shard_map/ppermute | solution.py:304
  11.9 2.2 %collective-permute-done.2.refs_1_ = s32[8,4,1,27]{3,2,1,0:T(1,128)S(1)} collective-permute-done((s32[8,4,1,27]{3,2,1,0:T(1,128)S(1)}, s32[8,4,1,27]{3,2,1,0:T(1,128)S(1)}, u32[]{:S(2)}, u32[]{:S(2)}) %collective-permute-start.2) | collective-permute-done | bytes 3488 | tf_op jit(solution)/shard_map/ppermute | solution.py:304
  14.1 1.5 %collective-permute-start.7 = (bf16[256,1024]{1,0:T(8,128)(2,1)S(1)}, bf16[256,1024]{1,0:T(8,128)(2,1)S(1)}, u32[]{:S(2)}, u32[]{:S(2)}) collective-permute-start(bf16[256,1024]{1,0:T(8,128)(2,1)S(1)} %get-tuple-element.42), channel_id=1, source_target_pairs={{0,16},{16,0},{1,17},{17,1},{2,18},{18,2},{3,19},{19,3},{4,20},{20... | collective-permute-start | bytes 1572872 | tf_op jit(solution)/shard_map/ppermute | solution.py:304
  15.6 1.3 %bias_beside.1.bias = f32[120,128]{1,0:T(8,128)S(1)} custom-call(s32[8,4,1,27]{3,2,1,0:T(1,128)S(1)} %pad_add_fusion.refs_0_, s32[8,4,1,27]{3,2,1,0:T(1,128)S(1)} %collective-permute-done.2.refs_1_), custom_call_target="tpu_custom_call" | custom-call | tf_op jit(solution)/shard_map/bias_beside/pallas_call | solution.py:114
  17.0 0.0 collective-permute-done.1.refs_2_
  17.0 3.8 %collective-permute-start.5 = (bf16[128,1024]{1,0:T(8,128)(2,1)S(1)}, bf16[128,1024]{1,0:T(8,128)(2,1)S(1)}, u32[]{:S(2)}, u32[]{:S(2)}) collective-permute-start(bf16[128,1024]{1,0:T(8,128)(2,1)S(1)} %slice.3), channel_id=1, source_target_pairs={{0,1},{1,0},{2,3},{3,2},{4,5},{5,4},{6,7},{7,6},{8,9},{9,8},{10,11... | collective-permute-start | bytes 786440 | tf_op jit(solution)/shard_map/ppermute | solution.py:297
  20.8 1.2 %collective-permute-done.5.refs_8_ = bf16[128,1024]{1,0:T(8,128)(2,1)S(1)} collective-permute-done((bf16[128,1024]{1,0:T(8,128)(2,1)S(1)}, bf16[128,1024]{1,0:T(8,128)(2,1)S(1)}, u32[]{:S(2)}, u32[]{:S(2)}) %collective-permute-start.5) | collective-permute-done | bytes 262176 | tf_op jit(solution)/shard_map/ppermute | solution.py:297
  21.9 0.5 collective-permute-start.9
  22.4 8.9 %collective-permute-done.3.query = bf16[256,1024]{1,0:T(8,128)(2,1)S(1)} collective-permute-done((bf16[256,1024]{1,0:T(8,128)(2,1)S(1)}, bf16[256,1024]{1,0:T(8,128)(2,1)S(1)}, u32[]{:S(2)}, u32[]{:S(2)}) %collective-permute-start.3) | collective-permute-done | bytes 524320 | tf_op jit(solution)/shard_map/ppermute | solution.py:297
  31.3 0.0 collective-permute-done.6.refs_3_
  31.3 0.0 collective-permute-done.4.refs_1_
  31.4 1.9 %attend_beside.2.refs_7_ = bf16[144,1024]{1,0:T(8,128)(2,1)S(1)} custom-call(f32[120,128]{1,0:T(8,128)S(1)} %bias_beside.1.bias, bf16[256,1024]{1,0:T(8,128)(2,1)S(1)} %collective-permute-done.3.query, bf16[512,1024]{1,0:T(8,128)(2,1)S(1)} %get-tuple-element.38.refs_0_, bf16[512,1024]{1,0:T(8,128)(2,1)S(1)} %collective-permute-done.4.refs_1_, ...), custom_call_target="tpu_custom_call" | custom-call | flops 402653184 | bytes 4194304 | tf_op jit(solution)/shard_map/attend_beside/pallas_call | solution.py:200
  33.3 0.0 collective-permute-done.7.refs_4_
  33.3 2.1 %collective-permute-start.8 = (bf16[256,1024]{1,0:T(8,128)(2,1)S(1)}, bf16[256,1024]{1,0:T(8,128)(2,1)S(1)}, u32[]{:S(2)}, u32[]{:S(2)}) collective-permute-start(bf16[256,1024]{1,0:T(8,128)(2,1)S(1)} %collective-permute-done.7.refs_4_), channel_id=1, source_target_pairs={{0,1},{1,0},{2,3},{3,2},{4,5},{5,4},{6,7},{7,6},{8,9},{9,8},{10,11... | collective-permute-start | bytes 1572872 | tf_op jit(solution)/shard_map/ppermute | solution.py:297
  35.4 0.0 collective-permute-start.11
  35.4 1.9 %collective-permute-done.9.refs_6_ = bf16[256,1024]{1,0:T(8,128)(2,1)S(1)} collective-permute-done((bf16[256,1024]{1,0:T(8,128)(2,1)S(1)}, bf16[256,1024]{1,0:T(8,128)(2,1)S(1)}, u32[]{:S(2)}, u32[]{:S(2)}) %collective-permute-start.9) | collective-permute-done | bytes 524320 | tf_op jit(solution)/shard_map/ppermute | solution.py:304
  37.4 0.0 collective-permute-done.8.refs_5_
  37.4 2.9 %attend_beside.3 = bf16[144,1024]{1,0:T(8,128)(2,1)S(1)} custom-call(f32[120,128]{1,0:T(8,128)S(1)} %bias_beside.1.bias, bf16[256,1024]{1,0:T(8,128)(2,1)S(1)} %collective-permute-done.3.query, bf16[512,1024]{1,0:T(8,128)(2,1)S(1)} %get-tuple-element.38.refs_0_, bf16[512,1024]{1,0:T(8,128)(2,1)S(1)} %collective-permute-done.4.refs_1_, ...), custom_call_target="tpu_custom_call" | custom-call | flops 603979776 | bytes 5767168 | tf_op jit(solution)/shard_map/attend_beside/pallas_call | solution.py:200
  40.2 1.2 %collective-permute-start.10 = (bf16[144,1024]{1,0:T(8,128)(2,1)S(1)}, bf16[144,1024]{1,0:T(8,128)(2,1)S(1)}, u32[]{:S(2)}, u32[]{:S(2)}) collective-permute-start(bf16[144,1024]{1,0:T(8,128)(2,1)S(1)} %attend_beside.3), channel_id=1, source_target_pairs={{0,8},{1,9},{2,10},{3,11},{4,12},{5,13},{6,14},{7,15},{8,0},{9,1},... | collective-permute-start | bytes 884744 | tf_op jit(solution)/shard_map/ppermute | solution.py:297
  41.4 1.3 %bias_own.1.bias = f32[120,128]{1,0:T(8,128)S(1)} custom-call(s32[8,4,1,27]{3,2,1,0:T(1,128)S(1)} %pad_add_fusion.refs_0_, s32[8,4,1,27]{3,2,1,0:T(1,128)S(1)} %collective-permute-done.2.refs_1_), custom_call_target="tpu_custom_call" | custom-call | tf_op jit(solution)/shard_map/bias_own/pallas_call | solution.py:114
  42.8 1.9 %attend_own.3 = (f32[128,1024]{1,0:T(8,128)S(1)}, f32[32,128]{1,0:T(8,128)S(1)}) custom-call(f32[120,128]{1,0:T(8,128)S(1)} %bias_own.1.bias, bf16[256,1024]{1,0:T(8,128)(2,1)S(1)} %copy-done, bf16[512,1024]{1,0:T(8,128)(2,1)S(1)} %get-tuple-element.38.refs_0_, bf16[512,1024]{1,0:T(8,128)(2,1)S(1)} %collective-permute-done.4.refs_1_, ...), custom_call_target="tpu_custom_call" | custom-call | flops 402653184 | bytes 4194304 | tf_op jit(solution)/shard_map/attend_own/pallas_call | solution.py:200
  44.6 2.8 %attend_own.2 = (f32[128,1024]{1,0:T(8,128)S(1)}, f32[32,128]{1,0:T(8,128)S(1)}) custom-call(f32[120,128]{1,0:T(8,128)S(1)} %bias_own.1.bias, bf16[256,1024]{1,0:T(8,128)(2,1)S(1)} %copy-done, bf16[512,1024]{1,0:T(8,128)(2,1)S(1)} %get-tuple-element.38.refs_0_, bf16[512,1024]{1,0:T(8,128)(2,1)S(1)} %collective-permute-done.4.refs_1_, ...), custom_call_target="tpu_custom_call" | custom-call | flops 603979776 | bytes 5767168 | tf_op jit(solution)/shard_map/attend_own/pallas_call | solution.py:200
  47.4 11.4 %collective-permute-done.11.refs_0_ = bf16[144,1024]{1,0:T(8,128)(2,1)S(1)} collective-permute-done((bf16[144,1024]{1,0:T(8,128)(2,1)S(1)}, bf16[144,1024]{1,0:T(8,128)(2,1)S(1)}, u32[]{:S(2)}, u32[]{:S(2)}) %collective-permute-start.11) | collective-permute-done | bytes 294944 | tf_op jit(solution)/shard_map/ppermute | solution.py:297
  58.8 1.2 %combine.2.refs_3_ = bf16[256,1024]{1,0:T(8,128)(2,1)} custom-call(bf16[144,1024]{1,0:T(8,128)(2,1)S(1)} %collective-permute-done.11.refs_0_, f32[128,1024]{1,0:T(8,128)S(1)} %get-tuple-element.53.refs_1_, f32[32,128]{1,0:T(8,128)S(1)} %get-tuple-element.54.refs_2_), custom_call_target="tpu_custom_call" | custom-call | tf_op jit(solution)/shard_map/combine/pallas_call | solution.py:277
  60.1 4.2 %collective-permute-done.10.refs_0_ = bf16[144,1024]{1,0:T(8,128)(2,1)S(1)} collective-permute-done((bf16[144,1024]{1,0:T(8,128)(2,1)S(1)}, bf16[144,1024]{1,0:T(8,128)(2,1)S(1)}, u32[]{:S(2)}, u32[]{:S(2)}) %collective-permute-start.10) | collective-permute-done | bytes 294944 | tf_op jit(solution)/shard_map/ppermute | solution.py:297
  64.3 1.2 %combine.3 = bf16[256,1024]{1,0:T(8,128)(2,1)} custom-call(bf16[144,1024]{1,0:T(8,128)(2,1)S(1)} %collective-permute-done.10.refs_0_, f32[128,1024]{1,0:T(8,128)S(1)} %get-tuple-element.50.refs_1_, f32[32,128]{1,0:T(8,128)S(1)} %get-tuple-element.51.refs_2_, bf16[256,1024]{1,0:T(8,128)(2,1)} %combine.2.refs_3_), custom_call_target="tpu_custom_call", output_to_operand_aliasing={{}: (3, {})} | custom-call | tf_op jit(solution)/shard_map/combine/pallas_call | solution.py:277
  (2 shorter events, 0.0 us)
Async XLA Ops:
  0.0 6.6 %copy-start = (bf16[256,1024]{1,0:T(8,128)(2,1)S(1)}, bf16[256,1024]{1,0:T(8,128)(2,1)}, u32[]{:S(2)}) copy-start(bf16[256,1024]{1,0:T(8,128)(2,1)} %query.1) | copy-start | bytes 1572868
  0.0 5.9 %collective-permute-start = (s32[4,4,1,27]{3,2,1,0:T(1,128)}, s32[4,4,1,27]{3,2,1,0:T(1,128)S(1)}, u32[]{:S(2)}, u32[]{:S(2)}) collective-permute-start(s32[4,4,1,27]{3,2,1,0:T(1,128)} %param.7), channel_id=1, source_target_pairs={{0,8},{1,9},{2,10},{3,11},{4,12},{5,13},{6,14},{7,15},{8,0},{9,1},... | collective-permute-start | bytes 5192 | tf_op jit(solution)/shard_map/ppermute | solution.py:297
  4.0 6.2 %copy-start.1 = (s32[4,4,1,27]{3,2,1,0:T(1,128)S(1)}, s32[4,4,1,27]{3,2,1,0:T(1,128)}, u32[]{:S(2)}) copy-start(s32[4,4,1,27]{3,2,1,0:T(1,128)} %param.7) | copy-start | bytes 5188
  5.9 25.5 %collective-permute-start.4 = (bf16[512,1024]{1,0:T(8,128)(2,1)S(1)}, bf16[512,1024]{1,0:T(8,128)(2,1)S(1)}, u32[]{:S(2)}, u32[]{:S(2)}) collective-permute-start(bf16[512,1024]{1,0:T(8,128)(2,1)S(1)} %get-tuple-element.38.refs_0_), channel_id=1, source_target_pairs={{0,1},{1,0},{2,3},{3,2},{4,5},{5,4},{6,7},{7,6},{8,9},{9,8},{10,11... | collective-permute-start | bytes 3145736 | tf_op jit(solution)/shard_map/ppermute | solution.py:297
  5.9 11.1 %collective-permute-start.1 = (bf16[256,1024]{1,0:T(8,128)(2,1)S(1)}, bf16[256,1024]{1,0:T(8,128)(2,1)S(1)}, u32[]{:S(2)}, u32[]{:S(2)}) collective-permute-start(bf16[256,1024]{1,0:T(8,128)(2,1)S(1)} %get-tuple-element.42), channel_id=1, source_target_pairs={{2,1},{4,3},{6,5},{10,9},{12,11},{14,13},{1,2},{3,4},{5,6},{9,10},... | collective-permute-start | bytes 1572872 | tf_op jit(solution)/shard_map/ppermute | solution.py:297
  6.6 24.8 %collective-permute-start.3 = (bf16[256,1024]{1,0:T(8,128)(2,1)S(1)}, bf16[256,1024]{1,0:T(8,128)(2,1)S(1)}, u32[]{:S(2)}, u32[]{:S(2)}) collective-permute-start(bf16[256,1024]{1,0:T(8,128)(2,1)S(1)} %copy-done), channel_id=1, source_target_pairs={{0,8},{1,9},{2,10},{3,11},{4,12},{5,13},{6,14},{7,15},{8,0},{9,1},... | collective-permute-start | bytes 1572872 | tf_op jit(solution)/shard_map/ppermute | solution.py:297
  9.6 21.8 %collective-permute-start.6 = (bf16[256,1024]{1,0:T(8,128)(2,1)S(1)}, bf16[256,1024]{1,0:T(8,128)(2,1)S(1)}, u32[]{:S(2)}, u32[]{:S(2)}) collective-permute-start(bf16[256,1024]{1,0:T(8,128)(2,1)S(1)} %get-tuple-element.41), channel_id=1, source_target_pairs={{2,1},{4,3},{6,5},{10,9},{12,11},{14,13},{1,2},{3,4},{5,6},{9,10},... | collective-permute-start | bytes 1572872 | tf_op jit(solution)/shard_map/ppermute | solution.py:297
  10.3 3.8 %collective-permute-start.2 = (s32[8,4,1,27]{3,2,1,0:T(1,128)S(1)}, s32[8,4,1,27]{3,2,1,0:T(1,128)S(1)}, u32[]{:S(2)}, u32[]{:S(2)}) collective-permute-start(s32[8,4,1,27]{3,2,1,0:T(1,128)S(1)} %pad_add_fusion.refs_0_), channel_id=1, source_target_pairs={{0,16},{16,0},{1,17},{17,1},{2,18},{18,2},{3,19},{19,3},{4,20},{20... | collective-permute-start | bytes 10376 | tf_op jit(solution)/shard_map/ppermute | solution.py:304
  14.1 19.2 %collective-permute-start.7 = (bf16[256,1024]{1,0:T(8,128)(2,1)S(1)}, bf16[256,1024]{1,0:T(8,128)(2,1)S(1)}, u32[]{:S(2)}, u32[]{:S(2)}) collective-permute-start(bf16[256,1024]{1,0:T(8,128)(2,1)S(1)} %get-tuple-element.42), channel_id=1, source_target_pairs={{0,16},{16,0},{1,17},{17,1},{2,18},{18,2},{3,19},{19,3},{4,20},{20... | collective-permute-start | bytes 1572872 | tf_op jit(solution)/shard_map/ppermute | solution.py:304
  17.0 4.9 %collective-permute-start.5 = (bf16[128,1024]{1,0:T(8,128)(2,1)S(1)}, bf16[128,1024]{1,0:T(8,128)(2,1)S(1)}, u32[]{:S(2)}, u32[]{:S(2)}) collective-permute-start(bf16[128,1024]{1,0:T(8,128)(2,1)S(1)} %slice.3), channel_id=1, source_target_pairs={{0,1},{1,0},{2,3},{3,2},{4,5},{5,4},{6,7},{7,6},{8,9},{9,8},{10,11... | collective-permute-start | bytes 786440 | tf_op jit(solution)/shard_map/ppermute | solution.py:297
  21.9 15.4 %collective-permute-start.9 = (bf16[256,1024]{1,0:T(8,128)(2,1)S(1)}, bf16[256,1024]{1,0:T(8,128)(2,1)S(1)}, u32[]{:S(2)}, u32[]{:S(2)}) collective-permute-start(bf16[256,1024]{1,0:T(8,128)(2,1)S(1)} %collective-permute-done.1.refs_2_), channel_id=1, source_target_pairs={{0,16},{16,0},{1,17},{17,1},{2,18},{18,2},{3,19},{19,3},{4,20},{20... | collective-permute-start | bytes 1572872 | tf_op jit(solution)/shard_map/ppermute | solution.py:304
  33.3 4.1 %collective-permute-start.8 = (bf16[256,1024]{1,0:T(8,128)(2,1)S(1)}, bf16[256,1024]{1,0:T(8,128)(2,1)S(1)}, u32[]{:S(2)}, u32[]{:S(2)}) collective-permute-start(bf16[256,1024]{1,0:T(8,128)(2,1)S(1)} %collective-permute-done.7.refs_4_), channel_id=1, source_target_pairs={{0,1},{1,0},{2,3},{3,2},{4,5},{5,4},{6,7},{7,6},{8,9},{9,8},{10,11... | collective-permute-start | bytes 1572872 | tf_op jit(solution)/shard_map/ppermute | solution.py:297
  35.4 23.4 %collective-permute-start.11 = (bf16[144,1024]{1,0:T(8,128)(2,1)S(1)}, bf16[144,1024]{1,0:T(8,128)(2,1)S(1)}, u32[]{:S(2)}, u32[]{:S(2)}) collective-permute-start(bf16[144,1024]{1,0:T(8,128)(2,1)S(1)} %attend_beside.2.refs_7_), channel_id=1, source_target_pairs={{0,8},{1,9},{2,10},{3,11},{4,12},{5,13},{6,14},{7,15},{8,0},{9,1},... | collective-permute-start | bytes 884744 | tf_op jit(solution)/shard_map/ppermute | solution.py:297
  40.2 24.1 %collective-permute-start.10 = (bf16[144,1024]{1,0:T(8,128)(2,1)S(1)}, bf16[144,1024]{1,0:T(8,128)(2,1)S(1)}, u32[]{:S(2)}, u32[]{:S(2)}) collective-permute-start(bf16[144,1024]{1,0:T(8,128)(2,1)S(1)} %attend_beside.3), channel_id=1, source_target_pairs={{0,8},{1,9},{2,10},{3,11},{4,12},{5,13},{6,14},{7,15},{8,0},{9,1},... | collective-permute-start | bytes 884744 | tf_op jit(solution)/shard_map/ppermute | solution.py:297

commit v7 on v5

--- a/solution.py
+++ b/solution.py
@@ -350,8 +350,6 @@
     own_halo = halo(border, inner)
     if is_small():
         other_border, far_bias = lax.optimization_barrier((other_border, far_bias))
-        token = blk_move(other_border[:TILE], mate_pairs)
-        other_border, token = lax.optimization_barrier((other_border, token))
     other_halo = halo(other_border, other_inner)
 
     def attend_beside(at, after):
@@ -366,7 +364,6 @@
     if is_small():
         made[1] = attend_beside(1, [])
         own_halo, after = lax.optimization_barrier((own_halo, made[1]))
-        after = after + [token]
     mate_halo = [blk_move(block, mate_pairs) for block in own_halo]
     beyond += [list(halos) for halos in zip(own_halo, mate_halo, other_halo)]
     if not is_small():

time: 64.5 us -> 64.5 us (level)
  waiting for transfers between devices: 29 us -> 33 us
  starting transfers between devices: 19.1 us -> 15.2 us
    ppermute x9 -> x8, starting transfers between devices: 15.5 us -> 11.5 us  [blk_move(): return lax.ppermute(block, 'blk', pairs)]
    ppermute x9 -> x8, waiting for transfers between devices: 24.8 us -> 28.8 us  [blk_move(): return lax.ppermute(block, 'blk', pairs)]
  transfers between devices with their start and end apart: 12 -> 11, of which waited for: 7 -> 6; matrix products, arithmetic and copies ran while one was open for 0% -> 0% of each run, Pallas kernels for 23% -> 23%
where the time goes in v7:
time: 64.5 us; the launch traced here: 64 us
  waiting for transfers between devices  33 us (51%)
  Pallas kernels  15.8 us (24%)
  starting transfers between devices  15.2 us (24%)
    ppermute x8, waiting for transfers between devices, blk_move(): return lax.ppermute(block, 'blk', pairs)  28.8 us
    ppermute x8, starting transfers between devices, blk_move(): return lax.ppermute(block, 'blk', pairs)  11.5 us
    pallas_call x4, Pallas kernels, attend(): pl.pallas_call(functools.partial(attend_kernel, at, places, travels), out...  9.42 us
    ppermute x3, waiting for transfers between devices, uly_swap(): return lax.ppermute(block, 'uly', [(0, 1), (1, 0)])  4.2 us
    ppermute x3, starting transfers between devices, uly_swap(): return lax.ppermute(block, 'uly', [(0, 1), (1, 0)])  3.68 us
    pallas_call x2, Pallas kernels, biases(): pl.pallas_call(functools.partial(bias_kernel, which, height_step, len(liv...  2.65 us
    pallas_call x2, Pallas kernels, combine(): pl.pallas_call(functools.partial(combine_kernel, at, n_more), out_shape=j...  2.43 us
  transfers between devices with their start and end apart: 11, of which 6 were waited for; matrix products, arithmetic and copies ran while one was open for 0% of the time, Pallas kernels for 23%

profile of v7, /device:TPU:0, one launch (start us, length us, event | category | flops | bytes accessed | tf_op | source)
XLA Modules:
  0.0 64.0 jit_solution(2186392325187222564)
XLA Ops:
  0.0 0.0 copy-start
  0.0 4.0 %collective-permute-start = (s32[4,4,1,27]{3,2,1,0:T(1,128)}, s32[4,4,1,27]{3,2,1,0:T(1,128)S(1)}, u32[]{:S(2)}, u32[]{:S(2)}) collective-permute-start(s32[4,4,1,27]{3,2,1,0:T(1,128)} %param.7), channel_id=1, source_target_pairs={{0,8},{1,9},{2,10},{3,11},{4,12},{5,13},{6,14},{7,15},{8,0},{9,1},... | collective-permute-start | bytes 5192 | tf_op jit(solution)/shard_map/ppermute | solution.py:297
  4.0 0.0 copy-start.1
  4.0 1.3 %pack_kv.1 = (bf16[512,1024]{1,0:T(8,128)(2,1)S(1)}, bf16[256,1024]{1,0:T(8,128)(2,1)S(1)}, bf16[256,1024]{1,0:T(8,128)(2,1)S(1)}) custom-call(bf16[256,1024]{1,0:T(8,128)(2,1)} %key.1, bf16[256,1024]{1,0:T(8,128)(2,1)} %value.1), custom_call_target="tpu_custom_call" | custom-call | bytes 2097152 | tf_op jit(solution)/shard_map/pack_kv/pallas_call | solution.py:71
  5.3 0.6 collective-permute-done
  5.9 0.0 collective-permute-start.4
  5.9 0.7 %collective-permute-start.1 = (bf16[256,1024]{1,0:T(8,128)(2,1)S(1)}, bf16[256,1024]{1,0:T(8,128)(2,1)S(1)}, u32[]{:S(2)}, u32[]{:S(2)}) collective-permute-start(bf16[256,1024]{1,0:T(8,128)(2,1)S(1)} %get-tuple-element.39), channel_id=1, source_target_pairs={{2,1},{4,3},{6,5},{10,9},{12,11},{14,13},{1,2},{3,4},{5,6},{9,10},... | collective-permute-start | bytes 1572872 | tf_op jit(solution)/shard_map/ppermute | solution.py:297
  6.6 0.0 copy-done
  6.6 3.0 %collective-permute-start.3 = (bf16[256,1024]{1,0:T(8,128)(2,1)S(1)}, bf16[256,1024]{1,0:T(8,128)(2,1)S(1)}, u32[]{:S(2)}, u32[]{:S(2)}) collective-permute-start(bf16[256,1024]{1,0:T(8,128)(2,1)S(1)} %copy-done), channel_id=1, source_target_pairs={{0,8},{1,9},{2,10},{3,11},{4,12},{5,13},{6,14},{7,15},{8,0},{9,1},... | collective-permute-start | bytes 1572872 | tf_op jit(solution)/shard_map/ppermute | solution.py:297
  9.6 0.7 %collective-permute-start.5 = (bf16[256,1024]{1,0:T(8,128)(2,1)S(1)}, bf16[256,1024]{1,0:T(8,128)(2,1)S(1)}, u32[]{:S(2)}, u32[]{:S(2)}) collective-permute-start(bf16[256,1024]{1,0:T(8,128)(2,1)S(1)} %get-tuple-element.38), channel_id=1, source_target_pairs={{2,1},{4,3},{6,5},{10,9},{12,11},{14,13},{1,2},{3,4},{5,6},{9,10},... | collective-permute-start | bytes 1572872 | tf_op jit(solution)/shard_map/ppermute | solution.py:297
  10.3 0.0 copy-done.1
  10.3 1.6 %collective-permute-start.2 = (s32[8,4,1,27]{3,2,1,0:T(1,128)S(1)}, s32[8,4,1,27]{3,2,1,0:T(1,128)S(1)}, u32[]{:S(2)}, u32[]{:S(2)}) collective-permute-start(s32[8,4,1,27]{3,2,1,0:T(1,128)S(1)} %pad_add_fusion.refs_0_), channel_id=1, source_target_pairs={{0,16},{16,0},{1,17},{17,1},{2,18},{18,2},{3,19},{19,3},{4,20},{20... | collective-permute-start | bytes 10376 | tf_op jit(solution)/shard_map/ppermute | solution.py:304
  11.9 2.2 %collective-permute-done.2.refs_1_ = s32[8,4,1,27]{3,2,1,0:T(1,128)S(1)} collective-permute-done((s32[8,4,1,27]{3,2,1,0:T(1,128)S(1)}, s32[8,4,1,27]{3,2,1,0:T(1,128)S(1)}, u32[]{:S(2)}, u32[]{:S(2)}) %collective-permute-start.2) | collective-permute-done | bytes 3488 | tf_op jit(solution)/shard_map/ppermute | solution.py:304
  14.1 1.5 %collective-permute-start.6 = (bf16[256,1024]{1,0:T(8,128)(2,1)S(1)}, bf16[256,1024]{1,0:T(8,128)(2,1)S(1)}, u32[]{:S(2)}, u32[]{:S(2)}) collective-permute-start(bf16[256,1024]{1,0:T(8,128)(2,1)S(1)} %get-tuple-element.39), channel_id=1, source_target_pairs={{0,16},{16,0},{1,17},{17,1},{2,18},{18,2},{3,19},{19,3},{4,20},{20... | collective-permute-start | bytes 1572872 | tf_op jit(solution)/shard_map/ppermute | solution.py:304
  15.6 1.3 %bias_beside.1.bias = f32[120,128]{1,0:T(8,128)S(1)} custom-call(s32[8,4,1,27]{3,2,1,0:T(1,128)S(1)} %pad_add_fusion.refs_0_, s32[8,4,1,27]{3,2,1,0:T(1,128)S(1)} %collective-permute-done.2.refs_1_), custom_call_target="tpu_custom_call" | custom-call | tf_op jit(solution)/shard_map/bias_beside/pallas_call | solution.py:114
  17.0 0.0 collective-permute-done.1.refs_2_
  17.0 0.6 collective-permute-start.8
  17.5 13.8 %collective-permute-done.3.query = bf16[256,1024]{1,0:T(8,128)(2,1)S(1)} collective-permute-done((bf16[256,1024]{1,0:T(8,128)(2,1)S(1)}, bf16[256,1024]{1,0:T(8,128)(2,1)S(1)}, u32[]{:S(2)}, u32[]{:S(2)}) %collective-permute-start.3) | collective-permute-done | bytes 524320 | tf_op jit(solution)/shard_map/ppermute | solution.py:297
  31.3 0.0 collective-permute-done.5.refs_3_
  31.3 0.0 collective-permute-done.4.refs_1_
  31.4 1.9 %attend_beside.2.refs_7_ = bf16[136,1024]{1,0:T(8,128)(2,1)S(1)} custom-call(f32[120,128]{1,0:T(8,128)S(1)} %bias_beside.1.bias, bf16[256,1024]{1,0:T(8,128)(2,1)S(1)} %collective-permute-done.3.query, bf16[512,1024]{1,0:T(8,128)(2,1)S(1)} %get-tuple-element.36.refs_0_, bf16[512,1024]{1,0:T(8,128)(2,1)S(1)} %collective-permute-done.4.refs_1_, ...), custom_call_target="tpu_custom_call" | custom-call | flops 402653184 | bytes 4194304 | tf_op jit(solution)/shard_map/attend_beside/pallas_call | solution.py:200
  33.3 0.0 collective-permute-done.6.refs_4_
  33.3 2.1 %collective-permute-start.7 = (bf16[256,1024]{1,0:T(8,128)(2,1)S(1)}, bf16[256,1024]{1,0:T(8,128)(2,1)S(1)}, u32[]{:S(2)}, u32[]{:S(2)}) collective-permute-start(bf16[256,1024]{1,0:T(8,128)(2,1)S(1)} %collective-permute-done.6.refs_4_), channel_id=1, source_target_pairs={{0,1},{1,0},{2,3},{3,2},{4,5},{5,4},{6,7},{7,6},{8,9},{9,8},{10,11... | collective-permute-start | bytes 1572872 | tf_op jit(solution)/shard_map/ppermute | solution.py:297
  35.4 0.0 collective-permute-start.10
  35.4 2.0 %collective-permute-done.8.refs_6_ = bf16[256,1024]{1,0:T(8,128)(2,1)S(1)} collective-permute-done((bf16[256,1024]{1,0:T(8,128)(2,1)S(1)}, bf16[256,1024]{1,0:T(8,128)(2,1)S(1)}, u32[]{:S(2)}, u32[]{:S(2)}) %collective-permute-start.8) | collective-permute-done | bytes 524320 | tf_op jit(solution)/shard_map/ppermute | solution.py:304
  37.4 0.0 collective-permute-done.7.refs_5_
  37.4 2.9 %attend_beside.3 = bf16[136,1024]{1,0:T(8,128)(2,1)S(1)} custom-call(f32[120,128]{1,0:T(8,128)S(1)} %bias_beside.1.bias, bf16[256,1024]{1,0:T(8,128)(2,1)S(1)} %collective-permute-done.3.query, bf16[512,1024]{1,0:T(8,128)(2,1)S(1)} %get-tuple-element.36.refs_0_, bf16[512,1024]{1,0:T(8,128)(2,1)S(1)} %collective-permute-done.4.refs_1_, ...), custom_call_target="tpu_custom_call" | custom-call | flops 603979776 | bytes 5767168 | tf_op jit(solution)/shard_map/attend_beside/pallas_call | solution.py:200
  40.2 1.0 %collective-permute-start.9 = (bf16[136,1024]{1,0:T(8,128)(2,1)S(1)}, bf16[136,1024]{1,0:T(8,128)(2,1)S(1)}, u32[]{:S(2)}, u32[]{:S(2)}) collective-permute-start(bf16[136,1024]{1,0:T(8,128)(2,1)S(1)} %attend_beside.3), channel_id=1, source_target_pairs={{0,8},{1,9},{2,10},{3,11},{4,12},{5,13},{6,14},{7,15},{8,0},{9,1},... | collective-permute-start | bytes 835592 | tf_op jit(solution)/shard_map/ppermute | solution.py:297
  41.2 1.3 %bias_own.1.bias = f32[120,128]{1,0:T(8,128)S(1)} custom-call(s32[8,4,1,27]{3,2,1,0:T(1,128)S(1)} %pad_add_fusion.refs_0_, s32[8,4,1,27]{3,2,1,0:T(1,128)S(1)} %collective-permute-done.2.refs_1_), custom_call_target="tpu_custom_call" | custom-call | tf_op jit(solution)/shard_map/bias_own/pallas_call | solution.py:114
  42.6 1.9 %attend_own.3 = (f32[128,1024]{1,0:T(8,128)S(1)}, f32[16,128]{1,0:T(8,128)S(1)}) custom-call(f32[120,128]{1,0:T(8,128)S(1)} %bias_own.1.bias, bf16[256,1024]{1,0:T(8,128)(2,1)S(1)} %copy-done, bf16[512,1024]{1,0:T(8,128)(2,1)S(1)} %get-tuple-element.36.refs_0_, bf16[512,1024]{1,0:T(8,128)(2,1)S(1)} %collective-permute-done.4.refs_1_, ...), custom_call_target="tpu_custom_call" | custom-call | flops 402653184 | bytes 4194304 | tf_op jit(solution)/shard_map/attend_own/pallas_call | solution.py:200
  44.4 2.8 %attend_own.2 = (f32[128,1024]{1,0:T(8,128)S(1)}, f32[16,128]{1,0:T(8,128)S(1)}) custom-call(f32[120,128]{1,0:T(8,128)S(1)} %bias_own.1.bias, bf16[256,1024]{1,0:T(8,128)(2,1)S(1)} %copy-done, bf16[512,1024]{1,0:T(8,128)(2,1)S(1)} %get-tuple-element.36.refs_0_, bf16[512,1024]{1,0:T(8,128)(2,1)S(1)} %collective-permute-done.4.refs_1_, ...), custom_call_target="tpu_custom_call" | custom-call | flops 603979776 | bytes 5767168 | tf_op jit(solution)/shard_map/attend_own/pallas_call | solution.py:200
  47.2 10.5 %collective-permute-done.10.refs_0_ = bf16[136,1024]{1,0:T(8,128)(2,1)S(1)} collective-permute-done((bf16[136,1024]{1,0:T(8,128)(2,1)S(1)}, bf16[136,1024]{1,0:T(8,128)(2,1)S(1)}, u32[]{:S(2)}, u32[]{:S(2)}) %collective-permute-start.10) | collective-permute-done | bytes 278560 | tf_op jit(solution)/shard_map/ppermute | solution.py:297
  57.7 1.2 %combine.2.refs_3_ = bf16[256,1024]{1,0:T(8,128)(2,1)} custom-call(bf16[136,1024]{1,0:T(8,128)(2,1)S(1)} %collective-permute-done.10.refs_0_, f32[128,1024]{1,0:T(8,128)S(1)} %get-tuple-element.49.refs_1_, f32[16,128]{1,0:T(8,128)S(1)} %get-tuple-element.50.refs_2_), custom_call_target="tpu_custom_call" | custom-call | tf_op jit(solution)/shard_map/combine/pallas_call | solution.py:277
  59.0 3.9 %collective-permute-done.9.refs_0_ = bf16[136,1024]{1,0:T(8,128)(2,1)S(1)} collective-permute-done((bf16[136,1024]{1,0:T(8,128)(2,1)S(1)}, bf16[136,1024]{1,0:T(8,128)(2,1)S(1)}, u32[]{:S(2)}, u32[]{:S(2)}) %collective-permute-start.9) | collective-permute-done | bytes 278560 | tf_op jit(solution)/shard_map/ppermute | solution.py:297
  62.8 1.2 %combine.3 = bf16[256,1024]{1,0:T(8,128)(2,1)} custom-call(bf16[136,1024]{1,0:T(8,128)(2,1)S(1)} %collective-permute-done.9.refs_0_, f32[128,1024]{1,0:T(8,128)S(1)} %get-tuple-element.46.refs_1_, f32[16,128]{1,0:T(8,128)S(1)} %get-tuple-element.47.refs_2_, bf16[256,1024]{1,0:T(8,128)(2,1)} %combine.2.refs_3_), custom_call_target="tpu_custom_call", output_to_operand_aliasing={{}: (3, {})} | custom-call | tf_op jit(solution)/shard_map/combine/pallas_call | solution.py:277
  (1 shorter events, 0.0 us)
Async XLA Ops:
  0.0 6.6 %copy-start = (bf16[256,1024]{1,0:T(8,128)(2,1)S(1)}, bf16[256,1024]{1,0:T(8,128)(2,1)}, u32[]{:S(2)}) copy-start(bf16[256,1024]{1,0:T(8,128)(2,1)} %query.1) | copy-start | bytes 1572868
  0.0 5.9 %collective-permute-start = (s32[4,4,1,27]{3,2,1,0:T(1,128)}, s32[4,4,1,27]{3,2,1,0:T(1,128)S(1)}, u32[]{:S(2)}, u32[]{:S(2)}) collective-permute-start(s32[4,4,1,27]{3,2,1,0:T(1,128)} %param.7), channel_id=1, source_target_pairs={{0,8},{1,9},{2,10},{3,11},{4,12},{5,13},{6,14},{7,15},{8,0},{9,1},... | collective-permute-start | bytes 5192 | tf_op jit(solution)/shard_map/ppermute | solution.py:297
  4.0 6.2 %copy-start.1 = (s32[4,4,1,27]{3,2,1,0:T(1,128)S(1)}, s32[4,4,1,27]{3,2,1,0:T(1,128)}, u32[]{:S(2)}) copy-start(s32[4,4,1,27]{3,2,1,0:T(1,128)} %param.7) | copy-start | bytes 5188
  5.9 25.5 %collective-permute-start.4 = (bf16[512,1024]{1,0:T(8,128)(2,1)S(1)}, bf16[512,1024]{1,0:T(8,128)(2,1)S(1)}, u32[]{:S(2)}, u32[]{:S(2)}) collective-permute-start(bf16[512,1024]{1,0:T(8,128)(2,1)S(1)} %get-tuple-element.36.refs_0_), channel_id=1, source_target_pairs={{0,1},{1,0},{2,3},{3,2},{4,5},{5,4},{6,7},{7,6},{8,9},{9,8},{10,11... | collective-permute-start | bytes 3145736 | tf_op jit(solution)/shard_map/ppermute | solution.py:297
  5.9 11.1 %collective-permute-start.1 = (bf16[256,1024]{1,0:T(8,128)(2,1)S(1)}, bf16[256,1024]{1,0:T(8,128)(2,1)S(1)}, u32[]{:S(2)}, u32[]{:S(2)}) collective-permute-start(bf16[256,1024]{1,0:T(8,128)(2,1)S(1)} %get-tuple-element.39), channel_id=1, source_target_pairs={{2,1},{4,3},{6,5},{10,9},{12,11},{14,13},{1,2},{3,4},{5,6},{9,10},... | collective-permute-start | bytes 1572872 | tf_op jit(solution)/shard_map/ppermute | solution.py:297
  6.6 24.8 %collective-permute-start.3 = (bf16[256,1024]{1,0:T(8,128)(2,1)S(1)}, bf16[256,1024]{1,0:T(8,128)(2,1)S(1)}, u32[]{:S(2)}, u32[]{:S(2)}) collective-permute-start(bf16[256,1024]{1,0:T(8,128)(2,1)S(1)} %copy-done), channel_id=1, source_target_pairs={{0,8},{1,9},{2,10},{3,11},{4,12},{5,13},{6,14},{7,15},{8,0},{9,1},... | collective-permute-start | bytes 1572872 | tf_op jit(solution)/shard_map/ppermute | solution.py:297
  9.6 21.8 %collective-permute-start.5 = (bf16[256,1024]{1,0:T(8,128)(2,1)S(1)}, bf16[256,1024]{1,0:T(8,128)(2,1)S(1)}, u32[]{:S(2)}, u32[]{:S(2)}) collective-permute-start(bf16[256,1024]{1,0:T(8,128)(2,1)S(1)} %get-tuple-element.38), channel_id=1, source_target_pairs={{2,1},{4,3},{6,5},{10,9},{12,11},{14,13},{1,2},{3,4},{5,6},{9,10},... | collective-permute-start | bytes 1572872 | tf_op jit(solution)/shard_map/ppermute | solution.py:297
  10.3 3.8 %collective-permute-start.2 = (s32[8,4,1,27]{3,2,1,0:T(1,128)S(1)}, s32[8,4,1,27]{3,2,1,0:T(1,128)S(1)}, u32[]{:S(2)}, u32[]{:S(2)}) collective-permute-start(s32[8,4,1,27]{3,2,1,0:T(1,128)S(1)} %pad_add_fusion.refs_0_), channel_id=1, source_target_pairs={{0,16},{16,0},{1,17},{17,1},{2,18},{18,2},{3,19},{19,3},{4,20},{20... | collective-permute-start | bytes 10376 | tf_op jit(solution)/shard_map/ppermute | solution.py:304
  14.1 19.2 %collective-permute-start.6 = (bf16[256,1024]{1,0:T(8,128)(2,1)S(1)}, bf16[256,1024]{1,0:T(8,128)(2,1)S(1)}, u32[]{:S(2)}, u32[]{:S(2)}) collective-permute-start(bf16[256,1024]{1,0:T(8,128)(2,1)S(1)} %get-tuple-element.39), channel_id=1, source_target_pairs={{0,16},{16,0},{1,17},{17,1},{2,18},{18,2},{3,19},{19,3},{4,20},{20... | collective-permute-start | bytes 1572872 | tf_op jit(solution)/shard_map/ppermute | solution.py:304
  17.0 20.4 %collective-permute-start.8 = (bf16[256,1024]{1,0:T(8,128)(2,1)S(1)}, bf16[256,1024]{1,0:T(8,128)(2,1)S(1)}, u32[]{:S(2)}, u32[]{:S(2)}) collective-permute-start(bf16[256,1024]{1,0:T(8,128)(2,1)S(1)} %collective-permute-done.1.refs_2_), channel_id=1, source_target_pairs={{0,16},{16,0},{1,17},{17,1},{2,18},{18,2},{3,19},{19,3},{4,20},{20... | collective-permute-start | bytes 1572872 | tf_op jit(solution)/shard_map/ppermute | solution.py:304
  33.3 4.1 %collective-permute-start.7 = (bf16[256,1024]{1,0:T(8,128)(2,1)S(1)}, bf16[256,1024]{1,0:T(8,128)(2,1)S(1)}, u32[]{:S(2)}, u32[]{:S(2)}) collective-permute-start(bf16[256,1024]{1,0:T(8,128)(2,1)S(1)} %collective-permute-done.6.refs_4_), channel_id=1, source_target_pairs={{0,1},{1,0},{2,3},{3,2},{4,5},{5,4},{6,7},{7,6},{8,9},{9,8},{10,11... | collective-permute-start | bytes 1572872 | tf_op jit(solution)/shard_map/ppermute | solution.py:297
  35.4 22.3 %collective-permute-start.10 = (bf16[136,1024]{1,0:T(8,128)(2,1)S(1)}, bf16[136,1024]{1,0:T(8,128)(2,1)S(1)}, u32[]{:S(2)}, u32[]{:S(2)}) collective-permute-start(bf16[136,1024]{1,0:T(8,128)(2,1)S(1)} %attend_beside.2.refs_7_), channel_id=1, source_target_pairs={{0,8},{1,9},{2,10},{3,11},{4,12},{5,13},{6,14},{7,15},{8,0},{9,1},... | collective-permute-start | bytes 835592 | tf_op jit(solution)/shard_map/ppermute | solution.py:297
  40.2 22.6 %collective-permute-start.9 = (bf16[136,1024]{1,0:T(8,128)(2,1)S(1)}, bf16[136,1024]{1,0:T(8,128)(2,1)S(1)}, u32[]{:S(2)}, u32[]{:S(2)}) collective-permute-start(bf16[136,1024]{1,0:T(8,128)(2,1)S(1)} %attend_beside.3), channel_id=1, source_target_pairs={{0,8},{1,9},{2,10},{3,11},{4,12},{5,13},{6,14},{7,15},{8,0},{9,1},... | collective-permute-start | bytes 835592 | tf_op jit(solution)/shard_map/ppermute | solution.py:297

commit v8 on v5

--- a/solution.py
+++ b/solution.py
@@ -18,6 +18,7 @@
 NONE = -1e30
 STAT_ROWS = 8
 TERMS = 3
+CHUNK = 64
 VMEM = 20 * 2**20
 
 ANYWHERE = pl.BlockSpec(memory_space=pl.ANY)
@@ -233,7 +234,7 @@
 
 
 def combine_kernel(at, n_more, *refs):
-    out, made, sem = refs[-3:]
+    out, made, sems = refs[-3:]
     travelled, (mine, stats) = refs[:n_more], refs[n_more : n_more + 2]
     top, total = own_stats(stats)
     more = []
@@ -256,16 +257,23 @@
     columns = jnp.transpose(
         jnp.concatenate(weights + [jnp.zeros((fill, HD), jnp.float32)], axis=0)
     )
-    for h in range(HEADS):
-        cols = slice(h * HD, (h + 1) * HD)
-        value = mine[:, cols] * columns[:, h : h + 1]
-        for m in range(n_more):
-            c = (m + 1) * HEADS + h
-            value = value + travelled[m][:TILE, cols].astype(jnp.float32) * columns[:, c : c + 1]
-        made[:, cols] = value.astype(made.dtype)
-    copy = pltpu.make_async_copy(made, out.at[rows_of(at)], sem)
-    copy.start()
-    copy.wait()
+    begin = frame_of(at) * TILE
+    copies = []
+    for first in range(0, TILE, CHUNK):
+        rows = slice(first, first + CHUNK)
+        for h in range(HEADS):
+            cols = slice(h * HD, (h + 1) * HD)
+            value = mine[rows, cols] * columns[rows, h : h + 1]
+            for m in range(n_more):
+                c = (m + 1) * HEADS + h
+                part = travelled[m][rows, cols].astype(jnp.float32)
+                value = value + part * columns[rows, c : c + 1]
+            made[rows, cols] = value.astype(made.dtype)
+        to = out.at[pl.ds(pl.multiple_of(begin + first, CHUNK), CHUNK)]
+        copies.append(pltpu.make_async_copy(made.at[rows], to, sems.at[first // CHUNK]))
+        copies[-1].start()
+    for copy in copies:
+        copy.wait()
 
 
 def combine(at, parts, n_more, into=None):
@@ -281,7 +289,7 @@
         out_specs=ANYWHERE,
         scratch_shapes=[
             pltpu.VMEM((TILE, HEADS * HD), jnp.bfloat16),
-            pltpu.SemaphoreType.DMA,
+            pltpu.SemaphoreType.DMA((TILE // CHUNK,)),
         ],
         input_output_aliases=aliases,
         compiler_params=pltpu.CompilerParams(vmem_limit_bytes=VMEM),

time: 64.5 us -> 64.4 us (level)
  no operation moved by 1% of the time
where the time goes in v8:
time: 64.4 us; the launch traced here: 64 us
  waiting for transfers between devices  29 us (45%)
  starting transfers between devices  19.1 us (30%)
  Pallas kernels  15.7 us (24%)
    ppermute x9, waiting for transfers between devices, blk_move(): return lax.ppermute(block, 'blk', pairs)  24.8 us
    ppermute x9, starting transfers between devices, blk_move(): return lax.ppermute(block, 'blk', pairs)  15.5 us
    pallas_call x4, Pallas kernels, attend(): pl.pallas_call(functools.partial(attend_kernel, at, places, travels), out...  9.42 us
    ppermute x3, waiting for transfers between devices, uly_swap(): return lax.ppermute(block, 'uly', [(0, 1), (1, 0)])  4.2 us
    ppermute x3, starting transfers between devices, uly_swap(): return lax.ppermute(block, 'uly', [(0, 1), (1, 0)])  3.62 us
    pallas_call x2, Pallas kernels, biases(): pl.pallas_call(functools.partial(bias_kernel, which, height_step, len(liv...  2.65 us
    pallas_call x2, Pallas kernels, combine(): pl.pallas_call(functools.partial(combine_kernel, at, n_more), out_shape=j...  2.39 us
  transfers between devices with their start and end apart: 12, of which 7 were waited for; matrix products, arithmetic and copies ran while one was open for 0% of the time, Pallas kernels for 23%

profile of v8, /device:TPU:0, one launch (start us, length us, event | category | flops | bytes accessed | tf_op | source)
XLA Modules:
  0.0 64.0 jit_solution(14849519452613172774)
XLA Ops:
  0.0 0.0 copy-start
  0.0 4.0 %collective-permute-start = (s32[4,4,1,27]{3,2,1,0:T(1,128)}, s32[4,4,1,27]{3,2,1,0:T(1,128)S(1)}, u32[]{:S(2)}, u32[]{:S(2)}) collective-permute-start(s32[4,4,1,27]{3,2,1,0:T(1,128)} %param.7), channel_id=1, source_target_pairs={{0,8},{1,9},{2,10},{3,11},{4,12},{5,13},{6,14},{7,15},{8,0},{9,1},... | collective-permute-start | bytes 5192 | tf_op jit(solution)/shard_map/ppermute | solution.py:305
  4.0 0.0 copy-start.1
  4.0 1.3 %pack_kv.1 = (bf16[512,1024]{1,0:T(8,128)(2,1)S(1)}, bf16[256,1024]{1,0:T(8,128)(2,1)S(1)}, bf16[256,1024]{1,0:T(8,128)(2,1)S(1)}) custom-call(bf16[256,1024]{1,0:T(8,128)(2,1)} %key.1, bf16[256,1024]{1,0:T(8,128)(2,1)} %value.1), custom_call_target="tpu_custom_call" | custom-call | bytes 2097152 | tf_op jit(solution)/shard_map/pack_kv/pallas_call | solution.py:72
  5.3 0.6 collective-permute-done
  5.9 0.0 collective-permute-start.4
  5.9 0.7 %collective-permute-start.1 = (bf16[256,1024]{1,0:T(8,128)(2,1)S(1)}, bf16[256,1024]{1,0:T(8,128)(2,1)S(1)}, u32[]{:S(2)}, u32[]{:S(2)}) collective-permute-start(bf16[256,1024]{1,0:T(8,128)(2,1)S(1)} %get-tuple-element.42), channel_id=1, source_target_pairs={{2,1},{4,3},{6,5},{10,9},{12,11},{14,13},{1,2},{3,4},{5,6},{9,10},... | collective-permute-start | bytes 1572872 | tf_op jit(solution)/shard_map/ppermute | solution.py:305
  6.6 0.0 copy-done
  6.6 3.0 %collective-permute-start.3 = (bf16[256,1024]{1,0:T(8,128)(2,1)S(1)}, bf16[256,1024]{1,0:T(8,128)(2,1)S(1)}, u32[]{:S(2)}, u32[]{:S(2)}) collective-permute-start(bf16[256,1024]{1,0:T(8,128)(2,1)S(1)} %copy-done), channel_id=1, source_target_pairs={{0,8},{1,9},{2,10},{3,11},{4,12},{5,13},{6,14},{7,15},{8,0},{9,1},... | collective-permute-start | bytes 1572872 | tf_op jit(solution)/shard_map/ppermute | solution.py:305
  9.6 0.7 %collective-permute-start.6 = (bf16[256,1024]{1,0:T(8,128)(2,1)S(1)}, bf16[256,1024]{1,0:T(8,128)(2,1)S(1)}, u32[]{:S(2)}, u32[]{:S(2)}) collective-permute-start(bf16[256,1024]{1,0:T(8,128)(2,1)S(1)} %get-tuple-element.41), channel_id=1, source_target_pairs={{2,1},{4,3},{6,5},{10,9},{12,11},{14,13},{1,2},{3,4},{5,6},{9,10},... | collective-permute-start | bytes 1572872 | tf_op jit(solution)/shard_map/ppermute | solution.py:305
  10.3 0.0 copy-done.1
  10.3 1.6 %collective-permute-start.2 = (s32[8,4,1,27]{3,2,1,0:T(1,128)S(1)}, s32[8,4,1,27]{3,2,1,0:T(1,128)S(1)}, u32[]{:S(2)}, u32[]{:S(2)}) collective-permute-start(s32[8,4,1,27]{3,2,1,0:T(1,128)S(1)} %pad_add_fusion.refs_0_), channel_id=1, source_target_pairs={{0,16},{16,0},{1,17},{17,1},{2,18},{18,2},{3,19},{19,3},{4,20},{20... | collective-permute-start | bytes 10376 | tf_op jit(solution)/shard_map/ppermute | solution.py:312
  11.9 2.2 %collective-permute-done.2.refs_1_ = s32[8,4,1,27]{3,2,1,0:T(1,128)S(1)} collective-permute-done((s32[8,4,1,27]{3,2,1,0:T(1,128)S(1)}, s32[8,4,1,27]{3,2,1,0:T(1,128)S(1)}, u32[]{:S(2)}, u32[]{:S(2)}) %collective-permute-start.2) | collective-permute-done | bytes 3488 | tf_op jit(solution)/shard_map/ppermute | solution.py:312
  14.1 1.5 %collective-permute-start.7 = (bf16[256,1024]{1,0:T(8,128)(2,1)S(1)}, bf16[256,1024]{1,0:T(8,128)(2,1)S(1)}, u32[]{:S(2)}, u32[]{:S(2)}) collective-permute-start(bf16[256,1024]{1,0:T(8,128)(2,1)S(1)} %get-tuple-element.42), channel_id=1, source_target_pairs={{0,16},{16,0},{1,17},{17,1},{2,18},{18,2},{3,19},{19,3},{4,20},{20... | collective-permute-start | bytes 1572872 | tf_op jit(solution)/shard_map/ppermute | solution.py:312
  15.6 1.3 %bias_beside.1.bias = f32[120,128]{1,0:T(8,128)S(1)} custom-call(s32[8,4,1,27]{3,2,1,0:T(1,128)S(1)} %pad_add_fusion.refs_0_, s32[8,4,1,27]{3,2,1,0:T(1,128)S(1)} %collective-permute-done.2.refs_1_), custom_call_target="tpu_custom_call" | custom-call | tf_op jit(solution)/shard_map/bias_beside/pallas_call | solution.py:115
  17.0 0.0 collective-permute-done.1.refs_2_
  17.0 3.8 %collective-permute-start.5 = (bf16[128,1024]{1,0:T(8,128)(2,1)S(1)}, bf16[128,1024]{1,0:T(8,128)(2,1)S(1)}, u32[]{:S(2)}, u32[]{:S(2)}) collective-permute-start(bf16[128,1024]{1,0:T(8,128)(2,1)S(1)} %slice.3), channel_id=1, source_target_pairs={{0,1},{1,0},{2,3},{3,2},{4,5},{5,4},{6,7},{7,6},{8,9},{9,8},{10,11... | collective-permute-start | bytes 786440 | tf_op jit(solution)/shard_map/ppermute | solution.py:305
  20.8 1.2 %collective-permute-done.5.refs_8_ = bf16[128,1024]{1,0:T(8,128)(2,1)S(1)} collective-permute-done((bf16[128,1024]{1,0:T(8,128)(2,1)S(1)}, bf16[128,1024]{1,0:T(8,128)(2,1)S(1)}, u32[]{:S(2)}, u32[]{:S(2)}) %collective-permute-start.5) | collective-permute-done | bytes 262176 | tf_op jit(solution)/shard_map/ppermute | solution.py:305
  21.9 0.5 collective-permute-start.9
  22.4 8.9 %collective-permute-done.3.query = bf16[256,1024]{1,0:T(8,128)(2,1)S(1)} collective-permute-done((bf16[256,1024]{1,0:T(8,128)(2,1)S(1)}, bf16[256,1024]{1,0:T(8,128)(2,1)S(1)}, u32[]{:S(2)}, u32[]{:S(2)}) %collective-permute-start.3) | collective-permute-done | bytes 524320 | tf_op jit(solution)/shard_map/ppermute | solution.py:305
  31.3 0.0 collective-permute-done.6.refs_3_
  31.3 0.0 collective-permute-done.4.refs_1_
  31.4 1.9 %attend_beside.2.refs_7_ = bf16[136,1024]{1,0:T(8,128)(2,1)S(1)} custom-call(f32[120,128]{1,0:T(8,128)S(1)} %bias_beside.1.bias, bf16[256,1024]{1,0:T(8,128)(2,1)S(1)} %collective-permute-done.3.query, bf16[512,1024]{1,0:T(8,128)(2,1)S(1)} %get-tuple-element.38.refs_0_, bf16[512,1024]{1,0:T(8,128)(2,1)S(1)} %collective-permute-done.4.refs_1_, ...), custom_call_target="tpu_custom_call" | custom-call | flops 402653184 | bytes 4194304 | tf_op jit(solution)/shard_map/attend_beside/pallas_call | solution.py:201
  33.3 0.0 collective-permute-done.7.refs_4_
  33.3 2.1 %collective-permute-start.8 = (bf16[256,1024]{1,0:T(8,128)(2,1)S(1)}, bf16[256,1024]{1,0:T(8,128)(2,1)S(1)}, u32[]{:S(2)}, u32[]{:S(2)}) collective-permute-start(bf16[256,1024]{1,0:T(8,128)(2,1)S(1)} %collective-permute-done.7.refs_4_), channel_id=1, source_target_pairs={{0,1},{1,0},{2,3},{3,2},{4,5},{5,4},{6,7},{7,6},{8,9},{9,8},{10,11... | collective-permute-start | bytes 1572872 | tf_op jit(solution)/shard_map/ppermute | solution.py:305
  35.4 0.0 collective-permute-start.11
  35.4 2.0 %collective-permute-done.9.refs_6_ = bf16[256,1024]{1,0:T(8,128)(2,1)S(1)} collective-permute-done((bf16[256,1024]{1,0:T(8,128)(2,1)S(1)}, bf16[256,1024]{1,0:T(8,128)(2,1)S(1)}, u32[]{:S(2)}, u32[]{:S(2)}) %collective-permute-start.9) | collective-permute-done | bytes 524320 | tf_op jit(solution)/shard_map/ppermute | solution.py:312
  37.4 0.0 collective-permute-done.8.refs_5_
  37.4 2.9 %attend_beside.3 = bf16[136,1024]{1,0:T(8,128)(2,1)S(1)} custom-call(f32[120,128]{1,0:T(8,128)S(1)} %bias_beside.1.bias, bf16[256,1024]{1,0:T(8,128)(2,1)S(1)} %collective-permute-done.3.query, bf16[512,1024]{1,0:T(8,128)(2,1)S(1)} %get-tuple-element.38.refs_0_, bf16[512,1024]{1,0:T(8,128)(2,1)S(1)} %collective-permute-done.4.refs_1_, ...), custom_call_target="tpu_custom_call" | custom-call | flops 603979776 | bytes 5767168 | tf_op jit(solution)/shard_map/attend_beside/pallas_call | solution.py:201
  40.2 1.2 %collective-permute-start.10 = (bf16[136,1024]{1,0:T(8,128)(2,1)S(1)}, bf16[136,1024]{1,0:T(8,128)(2,1)S(1)}, u32[]{:S(2)}, u32[]{:S(2)}) collective-permute-start(bf16[136,1024]{1,0:T(8,128)(2,1)S(1)} %attend_beside.3), channel_id=1, source_target_pairs={{0,8},{1,9},{2,10},{3,11},{4,12},{5,13},{6,14},{7,15},{8,0},{9,1},... | collective-permute-start | bytes 835592 | tf_op jit(solution)/shard_map/ppermute | solution.py:305
  41.4 1.3 %bias_own.1.bias = f32[120,128]{1,0:T(8,128)S(1)} custom-call(s32[8,4,1,27]{3,2,1,0:T(1,128)S(1)} %pad_add_fusion.refs_0_, s32[8,4,1,27]{3,2,1,0:T(1,128)S(1)} %collective-permute-done.2.refs_1_), custom_call_target="tpu_custom_call" | custom-call | tf_op jit(solution)/shard_map/bias_own/pallas_call | solution.py:115
  42.8 1.9 %attend_own.3 = (f32[128,1024]{1,0:T(8,128)S(1)}, f32[16,128]{1,0:T(8,128)S(1)}) custom-call(f32[120,128]{1,0:T(8,128)S(1)} %bias_own.1.bias, bf16[256,1024]{1,0:T(8,128)(2,1)S(1)} %copy-done, bf16[512,1024]{1,0:T(8,128)(2,1)S(1)} %get-tuple-element.38.refs_0_, bf16[512,1024]{1,0:T(8,128)(2,1)S(1)} %collective-permute-done.4.refs_1_, ...), custom_call_target="tpu_custom_call" | custom-call | flops 402653184 | bytes 4194304 | tf_op jit(solution)/shard_map/attend_own/pallas_call | solution.py:201
  44.6 2.8 %attend_own.2 = (f32[128,1024]{1,0:T(8,128)S(1)}, f32[16,128]{1,0:T(8,128)S(1)}) custom-call(f32[120,128]{1,0:T(8,128)S(1)} %bias_own.1.bias, bf16[256,1024]{1,0:T(8,128)(2,1)S(1)} %copy-done, bf16[512,1024]{1,0:T(8,128)(2,1)S(1)} %get-tuple-element.38.refs_0_, bf16[512,1024]{1,0:T(8,128)(2,1)S(1)} %collective-permute-done.4.refs_1_, ...), custom_call_target="tpu_custom_call" | custom-call | flops 603979776 | bytes 5767168 | tf_op jit(solution)/shard_map/attend_own/pallas_call | solution.py:201
  47.4 10.3 %collective-permute-done.11.refs_0_ = bf16[136,1024]{1,0:T(8,128)(2,1)S(1)} collective-permute-done((bf16[136,1024]{1,0:T(8,128)(2,1)S(1)}, bf16[136,1024]{1,0:T(8,128)(2,1)S(1)}, u32[]{:S(2)}, u32[]{:S(2)}) %collective-permute-start.11) | collective-permute-done | bytes 278560 | tf_op jit(solution)/shard_map/ppermute | solution.py:305
  57.7 1.2 %combine.2.refs_3_ = bf16[256,1024]{1,0:T(8,128)(2,1)} custom-call(bf16[136,1024]{1,0:T(8,128)(2,1)S(1)} %collective-permute-done.11.refs_0_, f32[128,1024]{1,0:T(8,128)S(1)} %get-tuple-element.53.refs_1_, f32[16,128]{1,0:T(8,128)S(1)} %get-tuple-element.54.refs_2_), custom_call_target="tpu_custom_call" | custom-call | tf_op jit(solution)/shard_map/combine/pallas_call | solution.py:285
  58.9 3.9 %collective-permute-done.10.refs_0_ = bf16[136,1024]{1,0:T(8,128)(2,1)S(1)} collective-permute-done((bf16[136,1024]{1,0:T(8,128)(2,1)S(1)}, bf16[136,1024]{1,0:T(8,128)(2,1)S(1)}, u32[]{:S(2)}, u32[]{:S(2)}) %collective-permute-start.10) | collective-permute-done | bytes 278560 | tf_op jit(solution)/shard_map/ppermute | solution.py:305
  62.8 1.2 %combine.3 = bf16[256,1024]{1,0:T(8,128)(2,1)} custom-call(bf16[136,1024]{1,0:T(8,128)(2,1)S(1)} %collective-permute-done.10.refs_0_, f32[128,1024]{1,0:T(8,128)S(1)} %get-tuple-element.50.refs_1_, f32[16,128]{1,0:T(8,128)S(1)} %get-tuple-element.51.refs_2_, bf16[256,1024]{1,0:T(8,128)(2,1)} %combine.2.refs_3_), custom_call_target="tpu_custom_call", output_to_operand_aliasing={{}: (3, {})} | custom-call | tf_op jit(solution)/shard_map/combine/pallas_call | solution.py:285
  (2 shorter events, 0.0 us)
Async XLA Ops:
  0.0 6.6 %copy-start = (bf16[256,1024]{1,0:T(8,128)(2,1)S(1)}, bf16[256,1024]{1,0:T(8,128)(2,1)}, u32[]{:S(2)}) copy-start(bf16[256,1024]{1,0:T(8,128)(2,1)} %query.1) | copy-start | bytes 1572868
  0.0 5.9 %collective-permute-start = (s32[4,4,1,27]{3,2,1,0:T(1,128)}, s32[4,4,1,27]{3,2,1,0:T(1,128)S(1)}, u32[]{:S(2)}, u32[]{:S(2)}) collective-permute-start(s32[4,4,1,27]{3,2,1,0:T(1,128)} %param.7), channel_id=1, source_target_pairs={{0,8},{1,9},{2,10},{3,11},{4,12},{5,13},{6,14},{7,15},{8,0},{9,1},... | collective-permute-start | bytes 5192 | tf_op jit(solution)/shard_map/ppermute | solution.py:305
  4.0 6.2 %copy-start.1 = (s32[4,4,1,27]{3,2,1,0:T(1,128)S(1)}, s32[4,4,1,27]{3,2,1,0:T(1,128)}, u32[]{:S(2)}) copy-start(s32[4,4,1,27]{3,2,1,0:T(1,128)} %param.7) | copy-start | bytes 5188
  5.9 25.5 %collective-permute-start.4 = (bf16[512,1024]{1,0:T(8,128)(2,1)S(1)}, bf16[512,1024]{1,0:T(8,128)(2,1)S(1)}, u32[]{:S(2)}, u32[]{:S(2)}) collective-permute-start(bf16[512,1024]{1,0:T(8,128)(2,1)S(1)} %get-tuple-element.38.refs_0_), channel_id=1, source_target_pairs={{0,1},{1,0},{2,3},{3,2},{4,5},{5,4},{6,7},{7,6},{8,9},{9,8},{10,11... | collective-permute-start | bytes 3145736 | tf_op jit(solution)/shard_map/ppermute | solution.py:305
  5.9 11.1 %collective-permute-start.1 = (bf16[256,1024]{1,0:T(8,128)(2,1)S(1)}, bf16[256,1024]{1,0:T(8,128)(2,1)S(1)}, u32[]{:S(2)}, u32[]{:S(2)}) collective-permute-start(bf16[256,1024]{1,0:T(8,128)(2,1)S(1)} %get-tuple-element.42), channel_id=1, source_target_pairs={{2,1},{4,3},{6,5},{10,9},{12,11},{14,13},{1,2},{3,4},{5,6},{9,10},... | collective-permute-start | bytes 1572872 | tf_op jit(solution)/shard_map/ppermute | solution.py:305
  6.6 24.8 %collective-permute-start.3 = (bf16[256,1024]{1,0:T(8,128)(2,1)S(1)}, bf16[256,1024]{1,0:T(8,128)(2,1)S(1)}, u32[]{:S(2)}, u32[]{:S(2)}) collective-permute-start(bf16[256,1024]{1,0:T(8,128)(2,1)S(1)} %copy-done), channel_id=1, source_target_pairs={{0,8},{1,9},{2,10},{3,11},{4,12},{5,13},{6,14},{7,15},{8,0},{9,1},... | collective-permute-start | bytes 1572872 | tf_op jit(solution)/shard_map/ppermute | solution.py:305
  9.6 21.8 %collective-permute-start.6 = (bf16[256,1024]{1,0:T(8,128)(2,1)S(1)}, bf16[256,1024]{1,0:T(8,128)(2,1)S(1)}, u32[]{:S(2)}, u32[]{:S(2)}) collective-permute-start(bf16[256,1024]{1,0:T(8,128)(2,1)S(1)} %get-tuple-element.41), channel_id=1, source_target_pairs={{2,1},{4,3},{6,5},{10,9},{12,11},{14,13},{1,2},{3,4},{5,6},{9,10},... | collective-permute-start | bytes 1572872 | tf_op jit(solution)/shard_map/ppermute | solution.py:305
  10.3 3.8 %collective-permute-start.2 = (s32[8,4,1,27]{3,2,1,0:T(1,128)S(1)}, s32[8,4,1,27]{3,2,1,0:T(1,128)S(1)}, u32[]{:S(2)}, u32[]{:S(2)}) collective-permute-start(s32[8,4,1,27]{3,2,1,0:T(1,128)S(1)} %pad_add_fusion.refs_0_), channel_id=1, source_target_pairs={{0,16},{16,0},{1,17},{17,1},{2,18},{18,2},{3,19},{19,3},{4,20},{20... | collective-permute-start | bytes 10376 | tf_op jit(solution)/shard_map/ppermute | solution.py:312
  14.1 19.2 %collective-permute-start.7 = (bf16[256,1024]{1,0:T(8,128)(2,1)S(1)}, bf16[256,1024]{1,0:T(8,128)(2,1)S(1)}, u32[]{:S(2)}, u32[]{:S(2)}) collective-permute-start(bf16[256,1024]{1,0:T(8,128)(2,1)S(1)} %get-tuple-element.42), channel_id=1, source_target_pairs={{0,16},{16,0},{1,17},{17,1},{2,18},{18,2},{3,19},{19,3},{4,20},{20... | collective-permute-start | bytes 1572872 | tf_op jit(solution)/shard_map/ppermute | solution.py:312
  17.0 4.9 %collective-permute-start.5 = (bf16[128,1024]{1,0:T(8,128)(2,1)S(1)}, bf16[128,1024]{1,0:T(8,128)(2,1)S(1)}, u32[]{:S(2)}, u32[]{:S(2)}) collective-permute-start(bf16[128,1024]{1,0:T(8,128)(2,1)S(1)} %slice.3), channel_id=1, source_target_pairs={{0,1},{1,0},{2,3},{3,2},{4,5},{5,4},{6,7},{7,6},{8,9},{9,8},{10,11... | collective-permute-start | bytes 786440 | tf_op jit(solution)/shard_map/ppermute | solution.py:305
  21.9 15.4 %collective-permute-start.9 = (bf16[256,1024]{1,0:T(8,128)(2,1)S(1)}, bf16[256,1024]{1,0:T(8,128)(2,1)S(1)}, u32[]{:S(2)}, u32[]{:S(2)}) collective-permute-start(bf16[256,1024]{1,0:T(8,128)(2,1)S(1)} %collective-permute-done.1.refs_2_), channel_id=1, source_target_pairs={{0,16},{16,0},{1,17},{17,1},{2,18},{18,2},{3,19},{19,3},{4,20},{20... | collective-permute-start | bytes 1572872 | tf_op jit(solution)/shard_map/ppermute | solution.py:312
  33.3 4.1 %collective-permute-start.8 = (bf16[256,1024]{1,0:T(8,128)(2,1)S(1)}, bf16[256,1024]{1,0:T(8,128)(2,1)S(1)}, u32[]{:S(2)}, u32[]{:S(2)}) collective-permute-start(bf16[256,1024]{1,0:T(8,128)(2,1)S(1)} %collective-permute-done.7.refs_4_), channel_id=1, source_target_pairs={{0,1},{1,0},{2,3},{3,2},{4,5},{5,4},{6,7},{7,6},{8,9},{9,8},{10,11... | collective-permute-start | bytes 1572872 | tf_op jit(solution)/shard_map/ppermute | solution.py:305
  35.4 22.3 %collective-permute-start.11 = (bf16[136,1024]{1,0:T(8,128)(2,1)S(1)}, bf16[136,1024]{1,0:T(8,128)(2,1)S(1)}, u32[]{:S(2)}, u32[]{:S(2)}) collective-permute-start(bf16[136,1024]{1,0:T(8,128)(2,1)S(1)} %attend_beside.2.refs_7_), channel_id=1, source_target_pairs={{0,8},{1,9},{2,10},{3,11},{4,12},{5,13},{6,14},{7,15},{8,0},{9,1},... | collective-permute-start | bytes 835592 | tf_op jit(solution)/shard_map/ppermute | solution.py:305
  40.2 22.6 %collective-permute-start.10 = (bf16[136,1024]{1,0:T(8,128)(2,1)S(1)}, bf16[136,1024]{1,0:T(8,128)(2,1)S(1)}, u32[]{:S(2)}, u32[]{:S(2)}) collective-permute-start(bf16[136,1024]{1,0:T(8,128)(2,1)S(1)} %attend_beside.3), channel_id=1, source_target_pairs={{0,8},{1,9},{2,10},{3,11},{4,12},{5,13},{6,14},{7,15},{8,0},{9,1},... | collective-permute-start | bytes 835592 | tf_op jit(solution)/shard_map/ppermute | solution.py:305
